TPU v7x, 128 devices: a whole 4x4x4 slice. The times are simulated.
128 devices in a mesh: rep: 16 (over z_lo, y, core), fsdp: 8 (over z_hi, x).
Axes of the slice: x: 4, y: 4, z: 4 (z_hi: 2, z_lo: 2; z = z_hi * 2 + z_lo), core: 2. Of those that a mesh axis runs over, the one named last changes fastest.
Arguments:
- tokens: bfloat16 [16, 2048, 8192], P('rep', 'fsdp'), may hold values from -6 to 6
- targets: bfloat16 [16, 2048, 512], P('rep', 'fsdp'), may hold values from -6 to 6
- block_master: float32 [16, 8192, 512], P('rep', 'fsdp'), may hold values from -0.0625 to 0.0625
- block_first: float32 [16, 8192, 512], P('rep', 'fsdp'), may hold values from -0.2 to 0.2
- block_second: float32 [16, 8192, 512], P('rep', 'fsdp'), may hold values from 0.0003 to 0.003
- frag_outer: float32 [8192, 512], P('fsdp'), may hold values from -6 to 6
- frag_inner: bfloat16 [16, 8192, 512], P('rep', 'fsdp'), may hold values from -6 to 6
- frag_momentum: float32 [8192, 512], P('fsdp'), may hold values from -6 to 6
Outputs:
- block_shift: float32 [16, 8192, 512], P('rep', 'fsdp')
- frag_params: float32 [8192, 512], P('fsdp')
- momentum_out: float32 [8192, 512], P('fsdp')
All inputs are finite; a program needn't handle non-finite values.
Results may differ from a plain program's by a relative error of at most 0.0012.
Values may be sent and summed in bfloat16 or wider, within the bound.
No kernel may reach another device: no remote copies, remote signals or barrier semaphores. Data moves between devices by JAX's collectives and lax.ppermute only.
A program may use at most 128 MiB of HBM per device.

v0:
```python
import jax
import jax.numpy as jnp
from jax import lax
from jax.sharding import PartitionSpec as P


def adam_update(weights, first, second, grad):
    first = 0.9 * first + 0.1 * grad
    second = 0.95 * second + 0.05 * grad * grad
    update = first / (jnp.sqrt(second) + 1e-08) + 0.1 * weights
    return (weights - 0.001 * update, first, second, update)


def outer_nesterov(outer, momentum, delta):
    momentum_new = 0.9 * momentum + delta
    return (outer - 0.7 * (0.9 * momentum_new + delta), momentum_new)


def shards(
    tokens, targets, block_master, block_first, block_second, frag_outer, frag_inner, frag_momentum
):
    inputs = tokens[0]
    teacher = targets[0]
    weights = block_master[0]
    first = block_first[0]
    second = block_second[0]
    groups = lax.axis_size("fsdp")
    replicas = lax.axis_size("rep")
    tok_local = inputs.shape[0]
    tok_all = tok_local * groups
    columns = lax.all_to_all(inputs, "fsdp", split_axis=1, concat_axis=0, tiled=True)
    teacher_all = lax.all_gather(teacher, "fsdp", axis=0, tiled=True).astype(jnp.float32)
    total = jnp.zeros_like(weights)
    frag_params = None
    momentum_out = None
    for step in range(2):
        compute_w = weights.astype(jnp.bfloat16)
        partial_out = jnp.dot(columns, compute_w, preferred_element_type=jnp.float32)
        outputs = lax.psum(partial_out, "fsdp")
        resid = (outputs - teacher_all).astype(jnp.bfloat16)
        grad = (
            lax.dot_general(
                columns, resid, (((0,), (0,)), ((), ())), preferred_element_type=jnp.float32
            )
            / tok_all
        )
        weights, first, second, update = adam_update(weights, first, second, grad)
        total = total + update
        if step == 0:
            pseudo = frag_outer - frag_inner[0].astype(jnp.float32)
            delta = lax.psum(pseudo, "rep") / replicas
            frag_params, momentum_out = outer_nesterov(frag_outer, frag_momentum, delta)
    return (total[None], frag_params, momentum_out)


def solution(mesh):
    in_specs = (
        P("rep", "fsdp", None),
        P("rep", "fsdp", None),
        P("rep", "fsdp", None),
        P("rep", "fsdp", None),
        P("rep", "fsdp", None),
        P("fsdp", None),
        P("rep", "fsdp", None),
        P("fsdp", None),
    )
    out_specs = (P("rep", "fsdp", None), P("fsdp", None), P("fsdp", None))
    return jax.shard_map(shards, mesh=mesh, in_specs=in_specs, out_specs=out_specs, check_vma=False)
```

profile of v0, /device:TPU:0, one launch (start us, length us, event | category | flops | bytes accessed | tf_op | source)
XLA Modules:
  0.0 474.9 jit_solution(6075057011578226019)
XLA Ops:
  7.2 6.4 %copy.32 = bf16[1,256,8192]{1,2,0:T(8,128)(2,1)} copy(bf16[1,256,8192]{2,1,0:T(8,128)(2,1)} %param.8) | data formatting | bytes 8388608 | tf_op args[0]
  13.5 7.7 %all-to-all-start = ((bf16[256,8,1024]{0,2,1:T(8,128)(2,1)}), bf16[256,8,1024]{0,2,1:T(8,128)(2,1)}, u32[]{:S(2)}, u32[]{:S(2)}) async-start(bf16[256,8,1024]{0,2,1:T(8,128)(2,1)} %bitcast.89), calls=%async_computation | async-start | bytes 8388608 | tf_op jit(solution)/shard_map/all_to_all | solution.py:31
  21.2 0.0 all-gather.3.cloned.1.call-start
  21.3 0.7 all-gather.3.cloned.1.call-update
  22.0 0.0 all-reduce.4.cloned.1.call-start
  22.0 54.5 %all-to-all-done = bf16[256,8,1024]{0,2,1:T(8,128)(2,1)} async-done(((bf16[256,8,1024]{0,2,1:T(8,128)(2,1)}), bf16[256,8,1024]{0,2,1:T(8,128)(2,1)}, u32[]{:S(2)}, u32[]{:S(2)}) %all-to-all-start) | async-done | bytes 4194336 | tf_op jit(solution)/shard_map/all_to_all | solution.py:31
  76.5 0.0 copy-start.2
  76.5 6.6 %copy.33 = bf16[8,256,1024]{2,1,0:T(8,128)(2,1)} copy(bf16[8,256,1024]{1,2,0:T(8,128)(2,1)} %bitcast.2) | data formatting | bytes 8388608 | tf_op jit(solution)/shard_map/all_to_all | solution.py:31
  83.0 0.0 copy-done.2
  83.0 6.5 %fusion.19 = f32[2048,512]{1,0:T(8,128)} fusion(bf16[2048,1024]{1,0:T(8,128)(2,1)} %bitcast.90, f32[1,1024,512]{2,1,0:T(8,128)S(1)} %copy-done.2), kind=kOutput, calls=%fused_computation.26 | convolution fusion | flops 2148007936 | bytes 10485760 | tf_op jit(solution)/shard_map/dot_general | solution.py:38
  89.6 0.0 all-reduce.4.cloned.1.call-update
  89.6 0.0 all-reduce.8.cloned.1.call-start
  89.6 1.9 copy.40
  91.6 1.5 copy.38
  93.1 1.6 convert_subtract_fusion.2
  94.7 0.0 all-reduce.8.cloned.1.call-update
  94.7 0.0 all-reduce.6.cloned.1.call-start
  94.8 2.9 copy.35
  97.6 2.9 copy.31
  100.5 2.9 copy.34
  103.4 2.9 all-gather.3.cloned.1.call-done
  106.3 111.1 %all-reduce.4.cloned.1.call-done = f32[2048,512]{1,0:T(8,128)} async-done(((f32[2048,512]{1,0:T(8,128)}), f32[2048,512]{1,0:T(8,128)}) %all-reduce.4.cloned.1.call-update) | async-done | bytes 4194320 | tf_op jit(solution)/shard_map/psum | solution.py:39
  217.4 0.0 copy-start.1
  217.4 0.0 copy-start.3
  217.4 0.0 copy-start.4
  217.5 0.0 copy-start.5
  217.5 6.6 %fusion.4 = f32[512,1024]{1,0:T(8,128)S(1)} fusion(bf16[2048,1024]{1,0:T(8,128)(2,1)} %bitcast.91, f32[2048,512]{1,0:T(8,128)} %all-reduce.4.cloned.1.call-done, bf16[1,2048,512]{2,1,0:T(8,128)(2,1)} %all-gather.3.cloned.1.call-done), kind=kOutput, calls=%fused_computation.6 | convolution fusion | flops 2150629376 | bytes 12582912 | tf_op jit(solution)/shard_map/dot_general | solution.py:42
  224.0 0.0 copy-start.6
  224.0 1.3 copy-done.6
  225.3 0.0 copy-done.1
  225.3 0.0 copy-done.3
  225.3 0.0 copy-done.4
  225.3 0.0 copy-done.5
  225.3 4.8 %convolution_bitcast_fusion = f32[2048,512]{1,0:T(8,128)} fusion(bf16[2048,1024]{1,0:T(8,128)(2,1)S(1)} %bitcast.93, f32[1,1024,512]{1,2,0:T(8,128)S(1)} %copy-done.3, f32[512,1024]{1,0:T(8,128)S(1)} %fusion.4, f32[1,1024,512]{1,2,0:T(8,128)S(1)} %copy-done.4, f32[1,1024,512]{1,2,0:T(8,128)S(1)} %copy-done.5), kind=kOutput, calls=%fused_computation.4 | convolution fusion | flops 2155347968 | bytes 16777216 | tf_op jit(solution)/shard_map/dot_general | solution.py:38
  230.1 0.0 all-reduce.6.cloned.1.call-update
  230.1 2.9 copy.37
  233.0 109.2 %all-reduce.8.cloned.1.call-done = f32[1024,512]{0,1:T(8,128)} async-done(((f32[1024,512]{0,1:T(8,128)}), f32[1024,512]{0,1:T(8,128)}) %all-reduce.8.cloned.1.call-update) | async-done | bytes 2097168 | tf_op jit(solution)/shard_map/psum | solution.py:51
  342.2 5.2 %multiply_add_fusion = (f32[1024,512]{0,1:T(8,128)}, f32[1024,512]{0,1:T(8,128)}) fusion(f32[1024,512]{0,1:T(8,128)} %copy.37, f32[1024,512]{0,1:T(8,128)} %all-reduce.8.cloned.1.call-done, f32[1024,512]{0,1:T(8,128)S(1)} %copy.40), kind=kLoop, calls=%fused_computation.24 | loop fusion | flops 3670016 | bytes 10485760 | tf_op jit(solution)/shard_map/add | solution.py:15
  347.4 0.0 copy-start
  347.4 3.0 copy.42
  350.4 0.0 copy-done
  350.5 1.8 copy.43
  352.3 102.8 %all-reduce.6.cloned.1.call-done = f32[2048,512]{1,0:T(8,128)} async-done(((f32[2048,512]{1,0:T(8,128)}), f32[2048,512]{1,0:T(8,128)}) %all-reduce.6.cloned.1.call-update) | async-done | bytes 4194320 | tf_op jit(solution)/shard_map/psum | solution.py:39
  455.1 11.5 %fusion.11 = f32[1,1024,512]{1,2,0:T(8,128)S(1)} fusion(f32[1,1024,512]{1,2,0:T(8,128)} %copy.35, bf16[2048,1024]{1,0:T(8,128)(2,1)} %bitcast.92, f32[2048,512]{1,0:T(8,128)} %all-reduce.6.cloned.1.call-done, bf16[1,2048,512]{2,1,0:T(8,128)(2,1)} %all-gather.3.cloned.1.call-done, f32[512,1024]{1,0:T(8,128)} %copy-done.6, f32[1,1024,512]{1,2,0:T(8,128)} %copy.31, ...), kind=kOutput, calls=%fused_computation.14 | convolution fusion | flops 2164785152 | bytes 20971520 | tf_op jit(solution)/shard_map/dot_general | solution.py:42
  466.6 1.8 copy.41
Async XLA Ops:
  13.5 62.9 %all-to-all-start = ((bf16[256,8,1024]{0,2,1:T(8,128)(2,1)}), bf16[256,8,1024]{0,2,1:T(8,128)(2,1)}, u32[]{:S(2)}, u32[]{:S(2)}) async-start(bf16[256,8,1024]{0,2,1:T(8,128)(2,1)} %bitcast.89), calls=%async_computation | async-start | bytes 8388608 | tf_op jit(solution)/shard_map/all_to_all | solution.py:31
  21.2 85.1 %all-gather.3.cloned.1.call-start = ((), (), s32[]{:S(2)}) async-start(), calls=%async_computation.4 | async-start | bytes 2359296 | tf_op jit(solution)/shard_map/all_gather | solution.py:32
  22.0 195.5 %all-reduce.4.cloned.1.call-start = ((), (), s32[]{:S(2)}) async-start(), calls=%async_computation.1 | async-start | bytes 8388608 | tf_op jit(solution)/shard_map/psum | solution.py:39
  76.5 6.6 %copy-start.2 = (f32[1,1024,512]{2,1,0:T(8,128)S(1)}, f32[1,1024,512]{2,1,0:T(8,128)}, u32[]{:S(2)}) copy-start(f32[1,1024,512]{2,1,0:T(8,128)} %param.10) | copy-start | bytes 6291460
  89.6 252.6 %all-reduce.8.cloned.1.call-start = ((), (), s32[]{:S(2)}) async-start(), calls=%async_computation.3 | async-start | bytes 4194304 | tf_op jit(solution)/shard_map/psum | solution.py:51
  94.7 360.4 %all-reduce.6.cloned.1.call-start = ((), (), s32[]{:S(2)}) async-start(), calls=%async_computation.2 | async-start | bytes 8388608 | tf_op jit(solution)/shard_map/psum | solution.py:39
  217.4 7.9 %copy-start.1 = (bf16[8,256,1024]{2,1,0:T(8,128)(2,1)S(1)}, bf16[8,256,1024]{2,1,0:T(8,128)(2,1)}, u32[]{:S(2)}) copy-start(bf16[8,256,1024]{2,1,0:T(8,128)(2,1)} %copy.33) | copy-start | bytes 12582916
  217.4 7.9 %copy-start.3 = (f32[1,1024,512]{1,2,0:T(8,128)S(1)}, f32[1,1024,512]{1,2,0:T(8,128)}, u32[]{:S(2)}) copy-start(f32[1,1024,512]{1,2,0:T(8,128)} %copy.35) | copy-start | bytes 6291460
  217.4 7.9 %copy-start.4 = (f32[1,1024,512]{1,2,0:T(8,128)S(1)}, f32[1,1024,512]{1,2,0:T(8,128)}, u32[]{:S(2)}) copy-start(f32[1,1024,512]{1,2,0:T(8,128)} %copy.31) | copy-start | bytes 6291460
  217.5 7.9 %copy-start.5 = (f32[1,1024,512]{1,2,0:T(8,128)S(1)}, f32[1,1024,512]{1,2,0:T(8,128)}, u32[]{:S(2)}) copy-start(f32[1,1024,512]{1,2,0:T(8,128)} %copy.34) | copy-start | bytes 6291460
  224.0 1.3 copy-start.6
  347.4 3.0 copy-start
Sparse Core Ops, SparseCore 0:
  24.4 81.8 all-gather.2
  108.8 108.5 all-reduce.3
  220.5 121.6 all-reduce.7
  344.5 110.5 all-reduce.5
where the time goes:
time: 476 us; the launch traced here: 475 us
  waiting for transfers between devices  381 us (80%)
  local copies, waits for them, and re-layouts  35.9 us (8%)
  matrix products  29.3 us (6%)
  between operations  13.8 us (3%)
  starting transfers between devices  7.85 us (2%)
  other arithmetic  6.85 us (1%)
    psum x2, waiting for transfers between devices, shards(): outputs = lax.psum(partial_out, 'fsdp')  214 us
    psum x1, waiting for transfers between devices, shards(): delta = lax.psum(pseudo, 'rep') / replicas  109 us
    all_to_all x1, waiting for transfers between devices, shards(): lax.all_to_all(inputs, 'fsdp', split_axis=1, concat_axis=0, tiled=True)  54.5 us
    unnamed x24, local copies, waits for them, and re-layouts  29.4 us
    dot_general x2, matrix products, shards(): lax.dot_general(columns, resid, (((0,), (0,)), ((), ())), preferred_eleme...  18 us
    dot_general x2, matrix products, shards(): jnp.dot(columns, compute_w, preferred_element_type=jnp.float32)  11.3 us
  transfers between devices with their start and end apart: 5, of which 5 were waited for; matrix products, arithmetic and copies ran while one was open for 11% of the time, Pallas kernels for 0%

commit v1 on v0

--- a/solution.py
+++ b/solution.py
@@ -20,24 +20,34 @@
     tokens, targets, block_master, block_first, block_second, frag_outer, frag_inner, frag_momentum
 ):
     inputs = tokens[0]
-    teacher = targets[0]
+    teacher = targets[0].astype(jnp.float32)
     weights = block_master[0]
     first = block_first[0]
     second = block_second[0]
     groups = lax.axis_size("fsdp")
     replicas = lax.axis_size("rep")
-    tok_local = inputs.shape[0]
+    tok_local, features = inputs.shape
     tok_all = tok_local * groups
-    columns = lax.all_to_all(inputs, "fsdp", split_axis=1, concat_axis=0, tiled=True)
-    teacher_all = lax.all_gather(teacher, "fsdp", axis=0, tiled=True).astype(jnp.float32)
+    rows, width = weights.shape
+    blocks = inputs.reshape(tok_local, groups, rows).transpose(1, 0, 2)
+    columns = lax.all_to_all(blocks, "fsdp", 0, 0).reshape(tok_all, rows)
+    frag_rows = frag_inner.shape[1] // replicas
+    pieces = lax.all_to_all(
+        frag_inner[0].reshape(replicas, frag_rows, -1), "rep", 0, 0
+    )
+    piece_sum = jnp.sum(pieces.astype(jnp.float32), axis=0)
+    inner_sum = lax.all_gather(piece_sum, "rep", axis=0, tiled=True)
     total = jnp.zeros_like(weights)
-    frag_params = None
-    momentum_out = None
     for step in range(2):
         compute_w = weights.astype(jnp.bfloat16)
         partial_out = jnp.dot(columns, compute_w, preferred_element_type=jnp.float32)
-        outputs = lax.psum(partial_out, "fsdp")
-        resid = (outputs - teacher_all).astype(jnp.bfloat16)
+        sent = partial_out.astype(jnp.bfloat16).reshape(groups, tok_local, width)
+        arrived = lax.all_to_all(sent, "fsdp", 0, 0)
+        outputs = jnp.sum(arrived.astype(jnp.float32), axis=0)
+        resid_local = (outputs - teacher).astype(jnp.bfloat16)
+        resid = lax.all_to_all(
+            jnp.broadcast_to(resid_local[None], (groups, tok_local, width)), "fsdp", 0, 0
+        ).reshape(tok_all, width)
         grad = (
             lax.dot_general(
                 columns, resid, (((0,), (0,)), ((), ())), preferred_element_type=jnp.float32
@@ -46,10 +56,8 @@
         )
         weights, first, second, update = adam_update(weights, first, second, grad)
         total = total + update
-        if step == 0:
-            pseudo = frag_outer - frag_inner[0].astype(jnp.float32)
-            delta = lax.psum(pseudo, "rep") / replicas
-            frag_params, momentum_out = outer_nesterov(frag_outer, frag_momentum, delta)
+    delta = frag_outer - inner_sum / replicas
+    frag_params, momentum_out = outer_nesterov(frag_outer, frag_momentum, delta)
     return (total[None], frag_params, momentum_out)
 
 

time: 476 us -> 266 us (0.56)
  waiting for transfers between devices: 381 us -> 46.5 us
  blocking collectives: 0 us -> 124 us
  matrix products: 29.3 us -> 21.4 us
  starting transfers between devices: 7.85 us -> 14.3 us
    psum x3 -> x0, waiting for transfers between devices: 323 us -> none  [the longest x2 214 us: shards(): outputs = lax.psum(partial_out, 'fsdp')]
    all_to_all x0 -> x3, blocking collectives: none -> 124 us  [the longest x2 65.1 us: shards(): arrived = lax.all_to_all(sent, 'fsdp', 0, 0)]
    all_to_all x1 -> x3, waiting for transfers between devices: 54.5 us -> 46.5 us  [the longest x2 30.5 us: shards(): lax.all_to_all(jnp.broadcast_to(resid_local[None], (groups, tok_local, wi...]
    all_to_all x1 -> x0, local copies, waits for them, and re-layouts: 6.57 us -> none  [shards(): lax.all_to_all(inputs, 'fsdp', split_axis=1, concat_axis=0, tiled=True)]
    all_to_all x1 -> x3, starting transfers between devices: 7.7 us -> 14.2 us  [the longest x2 9.06 us: shards(): lax.all_to_all(jnp.broadcast_to(resid_local[None], (groups, tok_local, wi...]
    another operation x0 -> x1, local copies, waits for them, and re-layouts: none -> 6.5 us  [shards(): blocks = inputs.reshape(tok_local, groups, rows).transpose(1, 0, 2)]
    dot_general x2, matrix products: 11.3 us -> 5.87 us  [shards(): jnp.dot(columns, compute_w, preferred_element_type=jnp.float32)]
    unnamed x24 -> x31, local copies, waits for them, and re-layouts: 29.4 us -> 24.7 us
  transfers between devices with their start and end apart: 5 -> 4, of which waited for: 5 -> 3; matrix products, arithmetic and copies ran while one was open for 11% -> 14% of each run, Pallas kernels for 0% -> 0%
where the time goes in v1:
time: 266 us; the launch traced here: 265 us
  blocking collectives  124 us (47%)
  waiting for transfers between devices  46.5 us (17%)
  local copies, waits for them, and re-layouts  37.5 us (14%)
  matrix products  21.4 us (8%)
  starting transfers between devices  14.3 us (5%)
  between operations  14.2 us (5%)
  other arithmetic  6.75 us (3%)
    all_to_all x2, blocking collectives, shards(): arrived = lax.all_to_all(sent, 'fsdp', 0, 0)  65.1 us
    all_to_all x1, blocking collectives, shards(): columns = lax.all_to_all(blocks, 'fsdp', 0, 0).reshape(tok_all, rows)  58.9 us
    all_to_all x2, waiting for transfers between devices, shards(): lax.all_to_all(jnp.broadcast_to(resid_local[None], (groups, tok_local, wi...  30.5 us
    unnamed x31, local copies, waits for them, and re-layouts  24.7 us
    all_to_all x1, waiting for transfers between devices, shards(): lax.all_to_all(frag_inner[0].reshape(replicas, frag_rows, -1), 'rep', 0, 0)  15.9 us
    dot_general x2, matrix products, shards(): lax.dot_general(columns, resid, (((0,), (0,)), ((), ())), preferred_eleme...  15.5 us
    all_to_all x2, starting transfers between devices, shards(): lax.all_to_all(jnp.broadcast_to(resid_local[None], (groups, tok_local, wi...  9.06 us
    another operation x1, local copies, waits for them, and re-layouts, shards(): blocks = inputs.reshape(tok_local, groups, rows).transpose(1, 0, 2)  6.5 us
  transfers between devices with their start and end apart: 4, of which 3 were waited for; matrix products, arithmetic and copies ran while one was open for 14% of the time, Pallas kernels for 0%

profile of v1, /device:TPU:0, one launch (start us, length us, event | category | flops | bytes accessed | tf_op | source)
XLA Modules:
  0.0 264.6 jit_solution(1541274098259768633)
XLA Ops:
  7.2 6.4 %copy.51 = bf16[1,256,8192]{1,2,0:T(8,128)(2,1)} copy(bf16[1,256,8192]{2,1,0:T(8,128)(2,1)} %param.8) | data formatting | bytes 8388608 | tf_op args[0]
  13.6 6.5 %copy.52 = bf16[256,8,1024]{2,0,1:T(8,128)(2,1)} copy(bf16[256,8,1024]{0,2,1:T(8,128)(2,1)} %bitcast.128) | data formatting | bytes 8388608 | tf_op jit(solution)/shard_map/reshape;squeeze | solution.py:32
  20.1 58.9 %all_to_all.30 = bf16[8,256,1024]{2,1,0:T(8,128)(2,1)S(1)} all-to-all(bf16[8,256,1024]{2,1,0:T(8,128)(2,1)} %bitcast.127), channel_id=1, replica_groups=mesh['rep'=16,'fsdp'=8] {'fsdp'}, dimensions={0} | all-to-all | bytes 8388608 | tf_op jit(solution)/shard_map/all_to_all | solution.py:33
  79.0 0.0 copy-done.3
  79.0 2.4 convolution_convert_fusion.1
  81.4 0.0 copy-done.1
  81.4 30.2 %all_to_all.31 = bf16[8,256,512]{2,1,0:T(8,128)(2,1)S(1)} all-to-all(bf16[8,256,512]{2,1,0:T(8,128)(2,1)S(1)} %bitcast.132), channel_id=1, replica_groups=mesh['rep'=16,'fsdp'=8] {'fsdp'}, dimensions={0} | all-to-all | bytes 4194304 | tf_op jit(solution)/shard_map/all_to_all | solution.py:45
  111.6 5.2 %all-to-all-start.5 = ((bf16[16,64,512]{2,1,0:T(8,128)(2,1)}), bf16[16,64,512]{2,1,0:T(8,128)(2,1)S(1)}, u32[]{:S(2)}, u32[]{:S(2)}) async-start(bf16[16,64,512]{2,1,0:T(8,128)(2,1)} %bitcast.134), calls=%async_computation.5 | async-start | bytes 2097152 | tf_op jit(solution)/shard_map/all_to_all | solution.py:35
  116.8 0.3 convert_reduce_fusion.1
  117.1 0.0 copy-done.9
  117.1 0.1 fusion.19
  117.2 0.1 copy.53
  117.3 15.9 %all-to-all-done.5 = bf16[16,64,512]{2,1,0:T(8,128)(2,1)S(1)} async-done(((bf16[16,64,512]{2,1,0:T(8,128)(2,1)}), bf16[16,64,512]{2,1,0:T(8,128)(2,1)S(1)}, u32[]{:S(2)}, u32[]{:S(2)}) %all-to-all-start.5) | async-done | bytes 1048608 | tf_op jit(solution)/shard_map/all_to_all | solution.py:35
  133.3 1.5 broadcast_in_dim.20
  134.7 4.5 %all-to-all-start.2 = ((bf16[8,256,512]{1,2,0:T(8,128)(2,1)}), bf16[8,256,512]{1,2,0:T(8,128)(2,1)}, u32[]{:S(2)}, u32[]{:S(2)}) async-start(bf16[8,256,512]{1,2,0:T(8,128)(2,1)} %broadcast_in_dim.20), calls=%async_computation.2 | async-start | bytes 4194304 | tf_op jit(solution)/shard_map/all_to_all | solution.py:48
  139.3 0.0 all-gather.2.cloned.1.call-start
  139.3 0.0 copy-done.4
  139.3 1.8 copy.55
  141.1 3.0 %copy.50 = f32[1,1024,512]{1,2,0:T(8,128)} copy(f32[1,1024,512]{2,1,0:T(8,128)} %param.11) | data formatting | bytes 4194304 | tf_op args[3]
  144.2 0.0 copy-done.5
  144.2 1.8 copy.54
  146.0 0.8 convert_reduce_fusion.2
  146.8 0.0 all-gather.2.cloned.1.call-update
  146.9 0.0 copy-start.6
  146.9 21.2 %all-to-all-done.2 = bf16[8,256,512]{1,2,0:T(8,128)(2,1)} async-done(((bf16[8,256,512]{1,2,0:T(8,128)(2,1)}), bf16[8,256,512]{1,2,0:T(8,128)(2,1)}, u32[]{:S(2)}, u32[]{:S(2)}) %all-to-all-start.2) | async-done | bytes 2097184 | tf_op jit(solution)/shard_map/all_to_all | solution.py:48
  168.1 5.3 %fusion.28 = f32[512,1024,1]{1,0,2:T(8,128)S(1)} fusion(bf16[8,256,512]{1,2,0:T(8,128)(2,1)} %all-to-all-done.2, bf16[8,256,1024]{2,1,0:T(8,128)(2,1)} %copy-done.1), kind=kOutput, calls=%fused_computation.50 | convolution fusion | flops 2147483648 | bytes 8388608 | tf_op jit(solution)/shard_map/dot_general | solution.py:52
  173.4 0.0 copy-done.6
  173.4 0.0 copy-done.2
  173.4 0.0 copy-done.8
  173.5 3.4 %convolution_convert_fusion = bf16[512,2048]{1,0:T(8,128)(2,1)S(1)} fusion(bf16[2048,1024]{1,0:T(8,128)(2,1)S(1)} %bitcast.131, f32[1,1024,512]{1,2,0:T(8,128)S(1)} %copy-done.6, f32[512,1024,1]{1,0,2:T(8,128)S(1)} %fusion.28, f32[1,1024,512]{1,2,0:T(8,128)S(1)} %copy-done.7, f32[1,1024,512]{1,2,0:T(8,128)S(1)} %copy-done.8), kind=kOutput, calls=%fused_computation.2 | convolution fusion | flops 2156396544 | bytes 14680064 | tf_op jit(solution)/shard_map/dot_general | solution.py:43
  176.9 0.0 copy-done.10
  176.9 0.1 copy.70
  177.1 34.9 %all_to_all.32 = bf16[8,256,512]{1,2,0:T(8,128)(2,1)S(1)} all-to-all(bf16[8,256,512]{1,2,0:T(8,128)(2,1)S(1)} %bitcast.129), channel_id=1, replica_groups=mesh['rep'=16,'fsdp'=8] {'fsdp'}, dimensions={0} | all-to-all | bytes 4194304 | tf_op jit(solution)/shard_map/all_to_all | solution.py:45
  211.9 0.3 convert_reduce_fusion
  212.2 0.2 copy.58
  212.4 0.1 fusion.18
  212.5 0.1 copy.59
  212.7 1.4 broadcast_in_dim.22
  214.1 4.5 %all-to-all-start.4 = ((bf16[8,256,512]{1,2,0:T(8,128)(2,1)}), bf16[8,256,512]{1,2,0:T(8,128)(2,1)}, u32[]{:S(2)}, u32[]{:S(2)}) async-start(bf16[8,256,512]{1,2,0:T(8,128)(2,1)} %broadcast_in_dim.22), calls=%async_computation.4 | async-start | bytes 4194304 | tf_op jit(solution)/shard_map/all_to_all | solution.py:48
  218.7 1.9 copy.60
  220.6 2.9 %copy.63 = f32[1024,512]{0,1:T(8,128)} copy(f32[1024,512]{1,0:T(8,128)} %param.13) | data formatting | bytes 4194304 | tf_op args[5]
  223.5 2.9 %copy.61 = f32[1024,512]{0,1:T(8,128)} copy(f32[1024,512]{1,0:T(8,128)} %all-gather.2.cloned.1.call-done) | data formatting | bytes 4194304 | tf_op jit(solution)/shard_map/all_gather | solution.py:39
  226.4 5.2 %multiply_add_fusion = (f32[1024,512]{0,1:T(8,128)}, f32[1024,512]{0,1:T(8,128)}) fusion(f32[1024,512]{0,1:T(8,128)S(1)} %copy.60, f32[1024,512]{0,1:T(8,128)} %copy.63, f32[1024,512]{0,1:T(8,128)} %copy.61), kind=kLoop, calls=%fused_computation.29 | loop fusion | flops 4194304 | bytes 10485760 | tf_op jit(solution)/shard_map/add | solution.py:15
  231.6 3.0 %copy.65 = f32[1024,512]{1,0:T(8,128)} copy(f32[1024,512]{0,1:T(8,128)} %get-tuple-element.16) | data formatting | bytes 4194304
  234.6 1.8 copy.66
  236.4 9.4 %all-to-all-done.4 = bf16[8,256,512]{1,2,0:T(8,128)(2,1)} async-done(((bf16[8,256,512]{1,2,0:T(8,128)(2,1)}), bf16[8,256,512]{1,2,0:T(8,128)(2,1)}, u32[]{:S(2)}, u32[]{:S(2)}) %all-to-all-start.4) | async-done | bytes 2097184 | tf_op jit(solution)/shard_map/all_to_all | solution.py:48
  245.8 10.2 %fusion.5 = f32[1,1024,512]{1,2,0:T(8,128)S(1)} fusion(f32[1,1024,512]{1,2,0:T(8,128)} %copy.55, bf16[8,256,512]{1,2,0:T(8,128)(2,1)} %all-to-all-done.4, bf16[8,256,1024]{2,1,0:T(8,128)(2,1)} %copy-done.1, f32[512,1024,1]{1,0,2:T(8,128)} %copy-done.10, f32[1,1024,512]{1,2,0:T(8,128)} %copy.50, f32[1,1024,512]{1,2,0:T(8,128)} %copy.54), kind=kOutput, calls=%fused_computation.11 | convolution fusion | flops 2161639424 | bytes 16777216 | tf_op jit(solution)/shard_map/dot_general | solution.py:52
  255.9 1.8 copy.64
  (13 shorter events, 0.0 us)
Async XLA Ops:
  20.1 58.9 %copy-start.3 = (f32[1,1024,512]{2,1,0:T(8,128)S(1)}, f32[1,1024,512]{2,1,0:T(8,128)}, u32[]{:S(2)}) copy-start(f32[1,1024,512]{2,1,0:T(8,128)} %param.10) | copy-start | bytes 6291460
  79.0 2.4 copy-start.1
  111.6 5.5 %copy-start.9 = (bf16[1,256,512]{2,1,0:T(8,128)(2,1)S(1)}, bf16[1,256,512]{2,1,0:T(8,128)(2,1)}, u32[]{:S(2)}) copy-start(bf16[1,256,512]{2,1,0:T(8,128)(2,1)} %param.9) | copy-start | bytes 786436
  111.6 21.6 %all-to-all-start.5 = ((bf16[16,64,512]{2,1,0:T(8,128)(2,1)}), bf16[16,64,512]{2,1,0:T(8,128)(2,1)S(1)}, u32[]{:S(2)}, u32[]{:S(2)}) async-start(bf16[16,64,512]{2,1,0:T(8,128)(2,1)} %bitcast.134), calls=%async_computation.5 | async-start | bytes 2097152 | tf_op jit(solution)/shard_map/all_to_all | solution.py:35
  134.7 4.6 %copy-start.4 = (f32[1,1024,512]{2,1,0:T(8,128)S(1)}, f32[1,1024,512]{2,1,0:T(8,128)}, u32[]{:S(2)}) copy-start(f32[1,1024,512]{2,1,0:T(8,128)} %param.10) | copy-start | bytes 6291460
  134.7 33.3 %all-to-all-start.2 = ((bf16[8,256,512]{1,2,0:T(8,128)(2,1)}), bf16[8,256,512]{1,2,0:T(8,128)(2,1)}, u32[]{:S(2)}, u32[]{:S(2)}) async-start(bf16[8,256,512]{1,2,0:T(8,128)(2,1)} %broadcast_in_dim.20), calls=%async_computation.2 | async-start | bytes 4194304 | tf_op jit(solution)/shard_map/all_to_all | solution.py:48
  139.3 84.2 %all-gather.2.cloned.1.call-start = ((), (), s32[]{:S(2)}) async-start(), calls=%async_computation.6 | async-start | bytes 2228224 | tf_op jit(solution)/shard_map/all_gather | solution.py:39
  141.1 3.1 %copy-start.5 = (f32[1,1024,512]{2,1,0:T(8,128)S(1)}, f32[1,1024,512]{2,1,0:T(8,128)}, u32[]{:S(2)}) copy-start(f32[1,1024,512]{2,1,0:T(8,128)} %param.12) | copy-start | bytes 6291460
  146.9 26.5 %copy-start.6 = (f32[1,1024,512]{1,2,0:T(8,128)S(1)}, f32[1,1024,512]{1,2,0:T(8,128)}, u32[]{:S(2)}) copy-start(f32[1,1024,512]{1,2,0:T(8,128)} %copy.55) | copy-start | bytes 6291460
  168.1 5.3 %copy-start.2 = (bf16[8,256,1024]{2,1,0:T(8,128)(2,1)S(1)}, bf16[8,256,1024]{2,1,0:T(8,128)(2,1)}, u32[]{:S(2)}) copy-start(bf16[8,256,1024]{2,1,0:T(8,128)(2,1)} %copy-done.1) | copy-start | bytes 12582916
  168.1 5.3 %copy-start.7 = (f32[1,1024,512]{1,2,0:T(8,128)S(1)}, f32[1,1024,512]{1,2,0:T(8,128)}, u32[]{:S(2)}) copy-start(f32[1,1024,512]{1,2,0:T(8,128)} %copy.50) | copy-start | bytes 6291460
  168.1 5.4 %copy-start.8 = (f32[1,1024,512]{1,2,0:T(8,128)S(1)}, f32[1,1024,512]{1,2,0:T(8,128)}, u32[]{:S(2)}) copy-start(f32[1,1024,512]{1,2,0:T(8,128)} %copy.54) | copy-start | bytes 6291460
  173.5 3.5 %copy-start.10 = (f32[512,1024,1]{1,0,2:T(8,128)}, f32[512,1024,1]{1,0,2:T(8,128)S(1)}, u32[]{:S(2)}) copy-start(f32[512,1024,1]{1,0,2:T(8,128)S(1)} %fusion.28) | copy-start | bytes 6291460
  214.1 31.7 %all-to-all-start.4 = ((bf16[8,256,512]{1,2,0:T(8,128)(2,1)}), bf16[8,256,512]{1,2,0:T(8,128)(2,1)}, u32[]{:S(2)}, u32[]{:S(2)}) async-start(bf16[8,256,512]{1,2,0:T(8,128)(2,1)} %broadcast_in_dim.22), calls=%async_computation.4 | async-start | bytes 4194304 | tf_op jit(solution)/shard_map/all_to_all | solution.py:48
  231.6 3.0 %copy-start = (f32[1024,512]{0,1:T(8,128)S(1)}, f32[1024,512]{0,1:T(8,128)}, u32[]{:S(2)}) copy-start(f32[1024,512]{0,1:T(8,128)} %get-tuple-element.15) | copy-start | bytes 6291460
Sparse Core Ops, SparseCore 0:
  147.0 38.6 all-gather.1

commit v2 on v1

v2 whole, which is shorter than its diff:
```python
import jax
import jax.numpy as jnp
from jax import lax
from jax.sharding import PartitionSpec as P

NZ, NX = 2, 4


def adam_update(weights, first, second, grad):
    first = 0.9 * first + 0.1 * grad
    second = 0.95 * second + 0.05 * grad * grad
    update = first / (jnp.sqrt(second) + 1e-08) + 0.1 * weights
    return (weights - 0.001 * update, first, second, update)


def outer_nesterov(outer, momentum, delta):
    momentum_new = 0.9 * momentum + delta
    return (outer - 0.7 * (0.9 * momentum_new + delta), momentum_new)


def shift(value, dz, dx):
    pairs = [
        (z * NX + x, (z + dz) % NZ * NX + (x + dx) % NX) for z in range(NZ) for x in range(NX)
    ]
    return lax.ppermute(value, "fsdp", pairs)


def f32(value):
    return value.astype(jnp.float32)


def bf16(value):
    return value.astype(jnp.bfloat16)


def sum_x_first(part, teacher):
    arrived = [shift(bf16(part[:, dx]), 0, -dx) for dx in range(1, NX)]
    own = part[:, 0] + sum(f32(a) for a in arrived)
    other = f32(shift(bf16(own), 1, 0))
    outputs = jnp.stack([own[0] + other[1], own[1] + other[0]])
    resid = bf16(outputs - teacher)
    return jnp.stack([resid] + [shift(resid, 0, dx) for dx in range(1, NX)], axis=1)


def sum_z_first(part, teacher):
    own = part[0] + f32(shift(bf16(part[1]), 1, 0))
    arrived = [shift(bf16(own[dx]), 0, -dx) for dx in range(1, NX)]
    resid = bf16(own[0] + sum(f32(a) for a in arrived) - teacher[0])
    row = jnp.stack([resid] + [shift(resid, 0, dx) for dx in range(1, NX)])
    return jnp.stack([row, shift(row, 1, 0)])


def shards(
    tokens, targets, block_master, block_first, block_second, frag_outer, frag_inner, frag_momentum
):
    inputs = tokens[0]
    groups = lax.axis_size("fsdp")
    replicas = lax.axis_size("rep")
    tok_local, features = inputs.shape
    tok_all = tok_local * groups
    rows, width = block_master.shape[1:]
    me = lax.axis_index("fsdp")
    my_z, my_x = me // NX, me % NX
    blocks = []
    for dz in range(NZ):
        for dx in range(NX):
            owner = (my_z + dz) % NZ * NX + (my_x + dx) % NX
            piece = lax.dynamic_slice_in_dim(inputs, owner * rows, rows, axis=1)
            blocks.append(piece if (dz, dx) == (0, 0) else shift(piece, dz, dx))
    columns = jnp.concatenate(blocks, axis=0)
    teacher = f32(jnp.stack([targets[0], shift(targets[0], 1, 0)]))

    frag_rows = frag_inner.shape[1] // replicas
    pieces = lax.all_to_all(
        frag_inner[0].reshape(replicas, frag_rows, -1), "rep", 0, 0
    )
    piece_sum = jnp.sum(f32(pieces), axis=0)
    inner_sum = lax.all_gather(piece_sum, "rep", axis=0, tiled=True)

    half = width // 2
    shifts = []
    for cut, sum_outputs in ((0, sum_x_first), (half, sum_z_first)):
        span = slice(cut, cut + half)
        weights, first, second = (
            a[0, :, span] for a in (block_master, block_first, block_second)
        )
        total = jnp.zeros_like(weights)
        for step in range(2):
            part = jnp.dot(columns, bf16(weights), preferred_element_type=jnp.float32)
            resid = sum_outputs(part.reshape(NZ, NX, tok_local, half), teacher[:, :, span])
            grad = (
                lax.dot_general(
                    columns,
                    resid.reshape(tok_all, half),
                    (((0,), (0,)), ((), ())),
                    preferred_element_type=jnp.float32,
                )
                / tok_all
            )
            weights, first, second, update = adam_update(weights, first, second, grad)
            total = total + update
        shifts.append(total)
    block_shift = jnp.concatenate(shifts, axis=1)
    delta = frag_outer - inner_sum / replicas
    frag_params, momentum_out = outer_nesterov(frag_outer, frag_momentum, delta)
    return (block_shift[None], frag_params, momentum_out)


def solution(mesh):
    in_specs = (
        P("rep", "fsdp", None),
        P("rep", "fsdp", None),
        P("rep", "fsdp", None),
        P("rep", "fsdp", None),
        P("rep", "fsdp", None),
        P("fsdp", None),
        P("rep", "fsdp", None),
        P("fsdp", None),
    )
    out_specs = (P("rep", "fsdp", None), P("fsdp", None), P("fsdp", None))
    return jax.shard_map(shards, mesh=mesh, in_specs=in_specs, out_specs=out_specs, check_vma=False)
```

time: 266 us -> 239 us (0.90)
  blocking collectives: 124 us -> 0 us
  starting transfers between devices: 14.3 us -> 82.4 us
  waiting for transfers between devices: 46.5 us -> 85.4 us
  local copies, waits for them, and re-layouts: 37.5 us -> 24 us
  other arithmetic: 6.75 us -> 16.6 us
  matrix products: 21.4 us -> 15.4 us
    all_to_all x3 -> x0, blocking collectives: 124 us -> none  [the longest x2 65.1 us: shards(): arrived = lax.all_to_all(sent, 'fsdp', 0, 0)]
    ppermute x0 -> x38, waiting for transfers between devices: none -> 85.4 us  [shift(): return lax.ppermute(value, 'fsdp', pairs)]
    ppermute x0 -> x38, starting transfers between devices: none -> 77.8 us  [shift(): return lax.ppermute(value, 'fsdp', pairs)]
    all_to_all x2 -> x0, waiting for transfers between devices: 30.5 us -> none  [shards(): lax.all_to_all(jnp.broadcast_to(resid_local[None], (groups, tok_local, wi...]
    all_to_all x1, waiting for transfers between devices: 15.9 us -> 0.01 us  [shards(): lax.all_to_all(frag_inner[0].reshape(replicas, frag_rows, -1), 'rep', 0, 0)]
    all_to_all x2 -> x0, starting transfers between devices: 9.06 us -> none  [shards(): lax.all_to_all(jnp.broadcast_to(resid_local[None], (groups, tok_local, wi...]
    unnamed x31 -> x49, local copies, waits for them, and re-layouts: 24.7 us -> 16.3 us
    another operation x1 -> x2, local copies, waits for them, and re-layouts: 6.5 us -> 0.14 us  [sum_x_first(): jnp.stack([resid] + [shift(resid, 0, dx) for dx in range(1, NX)], axis=1)]
  transfers between devices with their start and end apart: 4 -> 40, of which waited for: 3 -> 18; matrix products, arithmetic and copies ran while one was open for 14% -> 16% of each run, Pallas kernels for 0% -> 0%
where the time goes in v2:
time: 239 us
  waiting for transfers between devices  85.4 us (36%)
  starting transfers between devices  82.4 us (34%)
  local copies, waits for them, and re-layouts  24 us (10%)
  other arithmetic  16.6 us (7%)
  matrix products  15.4 us (6%)
  between operations  14.7 us (6%)
    ppermute x38, waiting for transfers between devices, shift(): return lax.ppermute(value, 'fsdp', pairs)  85.4 us
    ppermute x38, starting transfers between devices, shift(): return lax.ppermute(value, 'fsdp', pairs)  77.8 us
    unnamed x49, local copies, waits for them, and re-layouts  16.3 us
    dot_general x4, matrix products, shards(): lax.dot_general(columns, resid.reshape(tok_all, half), (((0,), (0,)), (()...  8.11 us
    dot_general x4, matrix products, shards(): part = jnp.dot(columns, bf16(weights), preferred_element_type=jnp.float32)  7.33 us
    sub x1, other arithmetic, outer_nesterov(): return (outer - 0.7 * (0.9 * momentum_new + delta), momentum_new)  5.16 us
  transfers between devices with their start and end apart: 40, of which 18 were waited for; matrix products, arithmetic and copies ran while one was open for 16% of the time, Pallas kernels for 0%

profile of v2, /device:TPU:0, one launch (start us, length us, event | category | flops | bytes accessed | tf_op | source)
XLA Modules:
  0.0 238.7 jit_solution(9775977513395972112)
XLA Ops:
  7.3 3.6 %dynamic-slice_bitcast_fusion = (bf16[256,1024]{1,0:T(8,128)(2,1)S(1)}, bf16[256,1024]{1,0:T(8,128)(2,1)S(1)}, bf16[256,1024]{1,0:T(8,128)(2,1)S(1)}, bf16[256,1...) fusion(bf16[1,256,8192]{2,1,0:T(8,128)(2,1)} %param.8, ...), kind=kLoop, calls=%fused_computation.48 | loop fusion | bytes 7340060 | tf_op jit(solution)/shard_map/dynamic_slice | solution.py:68
  10.9 1.6 collective-permute-start
  12.5 2.7 %collective-permute-start.1 = (bf16[256,1024]{1,0:T(8,128)(2,1)}, bf16[256,1024]{1,0:T(8,128)(2,1)}, u32[]{:S(2)}, u32[]{:S(2)}) collective-permute-start(bf16[256,1024]{1,0:T(8,128)(2,1)} %get-tuple-element.21), channel_id=1, source_target_pairs={{0,2},{1,3},{2,0},{3,1},{4,6},{5,7},{6,4},{7,5},{8,10},{9,11},{10,... | collective-permute-start | bytes 1572872 | tf_op jit(solution)/shard_map/ppermute | solution.py:25
  15.2 1.4 collective-permute-start.2
  16.7 3.9 %collective-permute-start.3 = (bf16[256,1024]{1,0:T(8,128)(2,1)S(1)}, bf16[256,1024]{1,0:T(8,128)(2,1)}, u32[]{:S(2)}, u32[]{:S(2)}) collective-permute-start(bf16[256,1024]{1,0:T(8,128)(2,1)S(1)} %get-tuple-element.19), channel_id=1, source_target_pairs={{0,4},{1,5},{2,6},{3,7},{4,0},{5,1},{6,2},{7,3},{8,12},{9,13},{10,... | collective-permute-start | bytes 1572872 | tf_op jit(solution)/shard_map/ppermute | solution.py:25
  21.6 6.8 %collective-permute-done = bf16[256,1024]{1,0:T(8,128)(2,1)} collective-permute-done((bf16[256,1024]{1,0:T(8,128)(2,1)}, bf16[256,1024]{1,0:T(8,128)(2,1)}, u32[]{:S(2)}, u32[]{:S(2)}) %collective-permute-start) | collective-permute-done | bytes 524320 | tf_op jit(solution)/shard_map/ppermute | solution.py:25
  28.4 15.2 %collective-permute-start.5 = (bf16[256,1024]{1,0:T(8,128)(2,1)S(1)}, bf16[256,1024]{1,0:T(8,128)(2,1)S(1)}, u32[]{:S(2)}, u32[]{:S(2)}) collective-permute-start(bf16[256,1024]{1,0:T(8,128)(2,1)S(1)} %get-tuple-element.23), channel_id=1, source_target_pairs={{0,6},{1,7},{2,4},{3,5},{4,2},{5,3},{6,0},{7,1},{8,14},{9,15},{10,... | collective-permute-start | bytes 1572872 | tf_op jit(solution)/shard_map/ppermute | solution.py:25
  46.0 2.7 %collective-permute-start.11 = (bf16[256,512]{1,0:T(8,128)(2,1)S(1)}, bf16[256,512]{1,0:T(8,128)(2,1)S(1)}, u32[]{:S(2)}, u32[]{:S(2)}) collective-permute-start(bf16[256,512]{1,0:T(8,128)(2,1)S(1)} %bitcast.221), channel_id=1, source_target_pairs={{0,4},{1,5},{2,6},{3,7},{4,0},{5,1},{6,2},{7,3},{8,12},{9,13},{10,... | collective-permute-start | bytes 786440 | tf_op jit(solution)/shard_map/ppermute | solution.py:25
  51.0 14.1 %collective-permute-done.4 = bf16[256,1024]{1,0:T(8,128)(2,1)} collective-permute-done((bf16[256,1024]{1,0:T(8,128)(2,1)S(1)}, bf16[256,1024]{1,0:T(8,128)(2,1)}, u32[]{:S(2)}, u32[]{:S(2)}) %collective-permute-start.4) | collective-permute-done | bytes 524320 | tf_op jit(solution)/shard_map/ppermute | solution.py:25
  66.1 14.3 %collective-permute-done.5 = bf16[256,1024]{1,0:T(8,128)(2,1)S(1)} collective-permute-done((bf16[256,1024]{1,0:T(8,128)(2,1)S(1)}, bf16[256,1024]{1,0:T(8,128)(2,1)S(1)}, u32[]{:S(2)}, u32[]{:S(2)}) %collective-permute-start.5) | collective-permute-done | bytes 524320 | tf_op jit(solution)/shard_map/ppermute | solution.py:25
  80.5 2.7 %fusion.36 = (bf16[2,4,256,256]{3,2,1,0:T(8,128)(2,1)S(1)}, f32[2,4,256,256]{3,2,1,0:T(8,128)}) fusion(bf16[2,4,256,1024]{3,2,1,0:T(8,128)(2,1)S(1)} %bitcast.214, f32[1,1024,512]{2,1,0:T(8,128)S(1)} %copy-done.5), kind=kOutput, calls=%fused_computation.97 | convolution fusion | flops 1074266112 | bytes 7864320 | tf_op jit(solution)/shard_map/dot_general | solution.py:89
  84.1 9.5 %collective-permute-start.8 = (bf16[2,256,256]{2,1,0:T(8,128)(2,1)}, bf16[2,256,256]{2,1,0:T(8,128)(2,1)}, u32[]{:S(2)}, u32[]{:S(2)}) collective-permute-start(bf16[2,256,256]{2,1,0:T(8,128)(2,1)} %get-tuple-element.33), channel_id=1, source_target_pairs={{0,2},{1,3},{2,0},{3,1},{4,6},{5,7},{6,4},{7,5},{8,10},{9,11},{10,... | collective-permute-start | bytes 786440 | tf_op jit(solution)/shard_map/ppermute | solution.py:25
  93.5 1.4 collective-permute-start.9
  97.2 4.6 %all-to-all-start = ((bf16[16,64,512]{2,1,0:T(8,128)(2,1)}), bf16[16,64,512]{2,1,0:T(8,128)(2,1)}, u32[]{:S(2)}, u32[]{:S(2)}) async-start(bf16[16,64,512]{2,1,0:T(8,128)(2,1)} %bitcast.67), calls=%async_computation | async-start | bytes 2097152 | tf_op jit(solution)/shard_map/all_to_all | solution.py:74
  104.6 1.4 fusion.32
  106.0 3.1 %collective-permute-start.10 = (bf16[2,256,256]{2,1,0:T(8,128)(2,1)S(1)}, bf16[2,256,256]{2,1,0:T(8,128)(2,1)S(1)}, u32[]{:S(2)}, u32[]{:S(2)}) collective-permute-start(bf16[2,256,256]{2,1,0:T(8,128)(2,1)S(1)} %get-tuple-element.7), channel_id=1, source_target_pairs={{0,4},{1,5},{2,6},{3,7},{4,0},{5,1},{6,2},{7,3},{8,12},{9,13},{10,... | collective-permute-start | bytes 786440 | tf_op jit(solution)/shard_map/ppermute | solution.py:25
  109.1 13.2 %collective-permute-done.22 = bf16[4,256,256]{2,1,0:T(8,128)(2,1)} collective-permute-done((bf16[4,256,256]{2,1,0:T(8,128)(2,1)}, bf16[4,256,256]{2,1,0:T(8,128)(2,1)}, u32[]{:S(2)}, u32[]{:S(2)}) %collective-permute-start.22) | collective-permute-done | bytes 524320 | tf_op jit(solution)/shard_map/ppermute | solution.py:25
  123.6 1.9 collective-permute-start.23
  127.5 4.7 %collective-permute-done.23 = bf16[256,256]{1,0:T(8,128)(2,1)S(1)} collective-permute-done((bf16[256,256]{1,0:T(8,128)(2,1)S(1)}, bf16[256,256]{1,0:T(8,128)(2,1)S(1)}, u32[]{:S(2)}, u32[]{:S(2)}) %collective-permute-start.23) | collective-permute-done | bytes 131104 | tf_op jit(solution)/shard_map/ppermute | solution.py:25
  133.4 1.4 collective-permute-done.25
  135.2 1.4 collective-permute-start.12
  136.6 3.2 %collective-permute-start.13 = (bf16[2,256,256]{2,1,0:T(8,128)(2,1)S(1)}, bf16[2,256,256]{2,1,0:T(8,128)(2,1)S(1)}, u32[]{:S(2)}, u32[]{:S(2)}) collective-permute-start(bf16[2,256,256]{2,1,0:T(8,128)(2,1)S(1)} %fusion.14), channel_id=1, source_target_pairs={{0,2},{1,3},{2,0},{3,1},{4,6},{5,7},{6,4},{7,5},{8,10},{9,11},{10,... | collective-permute-start | bytes 786440 | tf_op jit(solution)/shard_map/ppermute | solution.py:25
  139.8 1.4 collective-permute-start.14
  141.4 3.0 %collective-permute-start.28 = (bf16[256,256]{1,0:T(8,128)(2,1)S(1)}, bf16[256,256]{1,0:T(8,128)(2,1)S(1)}, u32[]{:S(2)}, u32[]{:S(2)}) collective-permute-start(bf16[256,256]{1,0:T(8,128)(2,1)S(1)} %get-tuple-element.11), channel_id=1, source_target_pairs={{0,3},{1,0},{2,1},{3,2},{4,7},{5,4},{6,5},{7,6},{8,11},{9,8},{10,9... | collective-permute-start | bytes 393224 | tf_op jit(solution)/shard_map/ppermute | solution.py:25
  144.6 3.8 %collective-permute-done.27 = bf16[256,256]{1,0:T(8,128)(2,1)S(1)} collective-permute-done((bf16[256,256]{1,0:T(8,128)(2,1)S(1)}, bf16[256,256]{1,0:T(8,128)(2,1)S(1)}, u32[]{:S(2)}, u32[]{:S(2)}) %collective-permute-start.27) | collective-permute-done | bytes 131104 | tf_op jit(solution)/shard_map/ppermute | solution.py:25
  149.8 2.0 copy-done.1
  154.6 1.7 fusion.9
  157.3 2.7 %collective-permute-start.15 = (bf16[2,256,256]{2,1,0:T(8,128)(2,1)}, bf16[2,256,256]{2,1,0:T(8,128)(2,1)}, u32[]{:S(2)}, u32[]{:S(2)}) collective-permute-start(bf16[2,256,256]{2,1,0:T(8,128)(2,1)} %get-tuple-element.26), channel_id=1, source_target_pairs={{0,3},{1,0},{2,1},{3,2},{4,7},{5,4},{6,5},{7,6},{8,11},{9,8},{10,9... | collective-permute-start | bytes 786440 | tf_op jit(solution)/shard_map/ppermute | solution.py:25
  160.0 1.4 collective-permute-start.16
  163.8 1.7 fusion.7
  167.7 3.5 %collective-permute-start.30 = (bf16[4,256,256]{2,1,0:T(8,128)(2,1)}, bf16[4,256,256]{2,1,0:T(8,128)(2,1)}, u32[]{:S(2)}, u32[]{:S(2)}) collective-permute-start(bf16[4,256,256]{2,1,0:T(8,128)(2,1)} %bitcast.54), channel_id=1, source_target_pairs={{0,4},{1,5},{2,6},{3,7},{4,0},{5,1},{6,2},{7,3},{8,12},{9,13},{10,... | collective-permute-start | bytes 1572872 | tf_op jit(solution)/shard_map/ppermute | solution.py:25
  171.2 2.0 convert_reduce_fusion
  173.3 1.5 fusion.30
  176.1 2.6 %collective-permute-done.30 = bf16[4,256,256]{2,1,0:T(8,128)(2,1)} collective-permute-done((bf16[4,256,256]{2,1,0:T(8,128)(2,1)}, bf16[4,256,256]{2,1,0:T(8,128)(2,1)}, u32[]{:S(2)}, u32[]{:S(2)}) %collective-permute-start.30) | collective-permute-done | bytes 524320 | tf_op jit(solution)/shard_map/ppermute | solution.py:25
  179.9 2.4 collective-permute-start.31
  183.3 2.4 %collective-permute-done.31 = bf16[256,256]{1,0:T(8,128)(2,1)S(1)} collective-permute-done((bf16[256,256]{1,0:T(8,128)(2,1)S(1)}, bf16[256,256]{1,0:T(8,128)(2,1)S(1)}, u32[]{:S(2)}, u32[]{:S(2)}) %collective-permute-start.31) | collective-permute-done | bytes 131104 | tf_op jit(solution)/shard_map/ppermute | solution.py:25
  185.7 3.1 %collective-permute-done.32 = bf16[256,256]{1,0:T(8,128)(2,1)S(1)} collective-permute-done((bf16[256,256]{1,0:T(8,128)(2,1)S(1)}, bf16[256,256]{1,0:T(8,128)(2,1)S(1)}, u32[]{:S(2)}, u32[]{:S(2)}) %collective-permute-start.32) | collective-permute-done | bytes 131104 | tf_op jit(solution)/shard_map/ppermute | solution.py:25
  190.3 2.0 collective-permute-start.35
  192.4 1.6 collective-permute-start.36
  194.0 6.6 %collective-permute-done.34 = bf16[256,256]{1,0:T(8,128)(2,1)S(1)} collective-permute-done((bf16[256,256]{1,0:T(8,128)(2,1)S(1)}, bf16[256,256]{1,0:T(8,128)(2,1)S(1)}, u32[]{:S(2)}, u32[]{:S(2)}) %collective-permute-start.34) | collective-permute-done | bytes 131104 | tf_op jit(solution)/shard_map/ppermute | solution.py:25
  200.8 2.5 %collective-permute-start.37 = (bf16[4,256,256]{2,1,0:T(8,128)(2,1)S(1)}, bf16[4,256,256]{2,1,0:T(8,128)(2,1)S(1)}, u32[]{:S(2)}, u32[]{:S(2)}) collective-permute-start(bf16[4,256,256]{2,1,0:T(8,128)(2,1)S(1)} %get-tuple-element.35), channel_id=1, source_target_pairs={{0,4},{1,5},{2,6},{3,7},{4,0},{5,1},{6,2},{7,3},{8,12},{9,13},{10,... | collective-permute-start | bytes 1572872 | tf_op jit(solution)/shard_map/ppermute | solution.py:25
  204.6 3.3 %collective-permute-start.20 = (bf16[2,256,256]{2,1,0:T(8,128)(2,1)S(1)}, bf16[2,256,256]{2,1,0:T(8,128)(2,1)S(1)}, u32[]{:S(2)}, u32[]{:S(2)}) collective-permute-start(bf16[2,256,256]{2,1,0:T(8,128)(2,1)S(1)} %fusion.15), channel_id=1, source_target_pairs={{0,2},{1,3},{2,0},{3,1},{4,6},{5,7},{6,4},{7,5},{8,10},{9,11},{10,... | collective-permute-start | bytes 786440 | tf_op jit(solution)/shard_map/ppermute | solution.py:25
  208.0 3.3 %collective-permute-done.19 = bf16[2,256,256]{2,1,0:T(8,128)(2,1)S(1)} collective-permute-done((bf16[2,256,256]{2,1,0:T(8,128)(2,1)S(1)}, bf16[2,256,256]{2,1,0:T(8,128)(2,1)S(1)}, u32[]{:S(2)}, u32[]{:S(2)}) %collective-permute-start.19) | collective-permute-done | bytes 262176 | tf_op jit(solution)/shard_map/ppermute | solution.py:25
  211.3 3.7 %collective-permute-done.20 = bf16[2,256,256]{2,1,0:T(8,128)(2,1)S(1)} collective-permute-done((bf16[2,256,256]{2,1,0:T(8,128)(2,1)S(1)}, bf16[2,256,256]{2,1,0:T(8,128)(2,1)S(1)}, u32[]{:S(2)}, u32[]{:S(2)}) %collective-permute-start.20) | collective-permute-done | bytes 262176 | tf_op jit(solution)/shard_map/ppermute | solution.py:25
  215.3 2.0 copy-done.2
  220.1 4.2 %add_add_fusion.1 = (f32[1024,256]{1,0:T(8,128)S(1)}, f32[1024,256]{1,0:T(8,128)S(1)}) fusion(f32[1,1024,512]{2,1,0:T(8,128)S(1)} %copy-done.6, f32[1024,256]{1,0:T(8,128)S(1)} %copy-done.18, f32[1,1024,512]{2,1,0:T(8,128)S(1)} %copy-done.14, f32[1,1024,512]{2,1,0:T(8,128)S(1)} %copy-done.16, f32[1024,256]{1,0:T(8,128)S(1)} %fusion.39, ...), kind=kOutput, calls=%fused_computation.25 | convolution fusion | flops 1087897600 | bytes 16777216 | tf_op jit(solution)/shard_map/dot_general | solution.py:92
  224.4 1.6 maximum_bitcast_fusion
  226.7 5.2 %multiply_subtract_fusion = (f32[1024,512]{1,0:T(8,128)}, f32[1024,512]{1,0:T(8,128)}) fusion(f32[1024,512]{1,0:T(8,128)S(1)} %copy-done.4, f32[1024,512]{1,0:T(8,128)} %all-gather.2.cloned.1.call-done, f32[1024,512]{1,0:T(8,128)} %param.15), kind=kLoop, calls=%fused_computation.1 | loop fusion | flops 4194304 | bytes 10485760 | tf_op jit(solution)/shard_map/sub | solution.py:18
  (127 shorter events, 38.0 us)
Async XLA Ops:
  10.9 35.0 %copy-start.9 = (bf16[1,256,512]{2,1,0:T(8,128)(2,1)S(1)}, bf16[1,256,512]{2,1,0:T(8,128)(2,1)}, u32[]{:S(2)}) copy-start(bf16[1,256,512]{2,1,0:T(8,128)(2,1)} %param.9) | copy-start | bytes 786436
  10.9 17.5 %collective-permute-start = (bf16[256,1024]{1,0:T(8,128)(2,1)}, bf16[256,1024]{1,0:T(8,128)(2,1)}, u32[]{:S(2)}, u32[]{:S(2)}) collective-permute-start(bf16[256,1024]{1,0:T(8,128)(2,1)} %get-tuple-element.22), channel_id=1, source_target_pairs={{0,1},{1,2},{2,3},{3,0},{4,5},{5,6},{6,7},{7,4},{8,9},{9,10},{10,1... | collective-permute-start | bytes 1572872 | tf_op jit(solution)/shard_map/ppermute | solution.py:25
  12.5 32.3 %collective-permute-start.1 = (bf16[256,1024]{1,0:T(8,128)(2,1)}, bf16[256,1024]{1,0:T(8,128)(2,1)}, u32[]{:S(2)}, u32[]{:S(2)}) collective-permute-start(bf16[256,1024]{1,0:T(8,128)(2,1)} %get-tuple-element.21), channel_id=1, source_target_pairs={{0,2},{1,3},{2,0},{3,1},{4,6},{5,7},{6,4},{7,5},{8,10},{9,11},{10,... | collective-permute-start | bytes 1572872 | tf_op jit(solution)/shard_map/ppermute | solution.py:25
  15.2 30.7 %collective-permute-start.2 = (bf16[256,1024]{1,0:T(8,128)(2,1)S(1)}, bf16[256,1024]{1,0:T(8,128)(2,1)}, u32[]{:S(2)}, u32[]{:S(2)}) collective-permute-start(bf16[256,1024]{1,0:T(8,128)(2,1)S(1)} %get-tuple-element.20), channel_id=1, source_target_pairs={{0,3},{1,0},{2,1},{3,2},{4,7},{5,4},{6,5},{7,6},{8,11},{9,8},{10,9... | collective-permute-start | bytes 1572872 | tf_op jit(solution)/shard_map/ppermute | solution.py:25
  16.7 33.1 %collective-permute-start.3 = (bf16[256,1024]{1,0:T(8,128)(2,1)S(1)}, bf16[256,1024]{1,0:T(8,128)(2,1)}, u32[]{:S(2)}, u32[]{:S(2)}) collective-permute-start(bf16[256,1024]{1,0:T(8,128)(2,1)S(1)} %get-tuple-element.19), channel_id=1, source_target_pairs={{0,4},{1,5},{2,6},{3,7},{4,0},{5,1},{6,2},{7,3},{8,12},{9,13},{10,... | collective-permute-start | bytes 1572872 | tf_op jit(solution)/shard_map/ppermute | solution.py:25
  20.5 44.5 %collective-permute-start.4 = (bf16[256,1024]{1,0:T(8,128)(2,1)S(1)}, bf16[256,1024]{1,0:T(8,128)(2,1)}, u32[]{:S(2)}, u32[]{:S(2)}) collective-permute-start(bf16[256,1024]{1,0:T(8,128)(2,1)S(1)} %get-tuple-element.18), channel_id=1, source_target_pairs={{0,5},{1,6},{2,7},{3,4},{4,1},{5,2},{6,3},{7,0},{8,13},{9,14},{10,... | collective-permute-start | bytes 1572872 | tf_op jit(solution)/shard_map/ppermute | solution.py:25
  28.4 52.0 %collective-permute-start.5 = (bf16[256,1024]{1,0:T(8,128)(2,1)S(1)}, bf16[256,1024]{1,0:T(8,128)(2,1)S(1)}, u32[]{:S(2)}, u32[]{:S(2)}) collective-permute-start(bf16[256,1024]{1,0:T(8,128)(2,1)S(1)} %get-tuple-element.23), channel_id=1, source_target_pairs={{0,6},{1,7},{2,4},{3,5},{4,2},{5,3},{6,0},{7,1},{8,14},{9,15},{10,... | collective-permute-start | bytes 1572872 | tf_op jit(solution)/shard_map/ppermute | solution.py:25
  44.8 35.7 %collective-permute-start.6 = (bf16[256,1024]{1,0:T(8,128)(2,1)S(1)}, bf16[256,1024]{1,0:T(8,128)(2,1)S(1)}, u32[]{:S(2)}, u32[]{:S(2)}) collective-permute-start(bf16[256,1024]{1,0:T(8,128)(2,1)S(1)} %get-tuple-element.17), channel_id=1, source_target_pairs={{0,7},{1,4},{2,5},{3,6},{4,3},{5,0},{6,1},{7,2},{8,15},{9,12},{10,... | collective-permute-start | bytes 1572872 | tf_op jit(solution)/shard_map/ppermute | solution.py:25
  46.0 55.9 %collective-permute-start.11 = (bf16[256,512]{1,0:T(8,128)(2,1)S(1)}, bf16[256,512]{1,0:T(8,128)(2,1)S(1)}, u32[]{:S(2)}, u32[]{:S(2)}) collective-permute-start(bf16[256,512]{1,0:T(8,128)(2,1)S(1)} %bitcast.221), channel_id=1, source_target_pairs={{0,4},{1,5},{2,6},{3,7},{4,0},{5,1},{6,2},{7,3},{8,12},{9,13},{10,... | collective-permute-start | bytes 786440 | tf_op jit(solution)/shard_map/ppermute | solution.py:25
  49.7 30.8 %copy-start.5 = (f32[1,1024,512]{2,1,0:T(8,128)S(1)}, f32[1,1024,512]{2,1,0:T(8,128)}, u32[]{:S(2)}) copy-start(f32[1,1024,512]{2,1,0:T(8,128)} %param.10) | copy-start | bytes 6291460
  80.5 14.5 %copy-start = (bf16[2048,1024]{1,0:T(8,128)(2,1)}, bf16[2048,1024]{1,0:T(8,128)(2,1)S(1)}, u32[]{:S(2)}) copy-start(bf16[2048,1024]{1,0:T(8,128)(2,1)S(1)} %constant_dynamic-update-slice_fusion) | copy-start | bytes 12582916
  84.1 19.6 %collective-permute-start.7 = (bf16[2,256,256]{2,1,0:T(8,128)(2,1)}, bf16[2,256,256]{2,1,0:T(8,128)(2,1)}, u32[]{:S(2)}, u32[]{:S(2)}) collective-permute-start(bf16[2,256,256]{2,1,0:T(8,128)(2,1)} %get-tuple-element.31), channel_id=1, source_target_pairs={{0,3},{1,0},{2,1},{3,2},{4,7},{5,4},{6,5},{7,6},{8,11},{9,8},{10,9... | collective-permute-start | bytes 786440 | tf_op jit(solution)/shard_map/ppermute | solution.py:25
  84.1 19.6 %collective-permute-start.8 = (bf16[2,256,256]{2,1,0:T(8,128)(2,1)}, bf16[2,256,256]{2,1,0:T(8,128)(2,1)}, u32[]{:S(2)}, u32[]{:S(2)}) collective-permute-start(bf16[2,256,256]{2,1,0:T(8,128)(2,1)} %get-tuple-element.33), channel_id=1, source_target_pairs={{0,2},{1,3},{2,0},{3,1},{4,6},{5,7},{6,4},{7,5},{8,10},{9,11},{10,... | collective-permute-start | bytes 786440 | tf_op jit(solution)/shard_map/ppermute | solution.py:25
  93.5 11.1 %collective-permute-start.9 = (bf16[2,256,256]{2,1,0:T(8,128)(2,1)}, bf16[2,256,256]{2,1,0:T(8,128)(2,1)}, u32[]{:S(2)}, u32[]{:S(2)}) collective-permute-start(bf16[2,256,256]{2,1,0:T(8,128)(2,1)} %get-tuple-element.32), channel_id=1, source_target_pairs={{0,1},{1,2},{2,3},{3,0},{4,5},{5,6},{6,7},{7,4},{8,9},{9,10},{10,1... | collective-permute-start | bytes 786440 | tf_op jit(solution)/shard_map/ppermute | solution.py:25
  96.3 7.3 %copy-start.3 = (f32[2048,256]{1,0:T(8,128)}, f32[2048,256]{1,0:T(8,128)S(1)}, u32[]{:S(2)}) copy-start(f32[2048,256]{1,0:T(8,128)S(1)} %fusion.11) | copy-start | bytes 6291460
  97.2 25.1 %collective-permute-start.22 = (bf16[4,256,256]{2,1,0:T(8,128)(2,1)}, bf16[4,256,256]{2,1,0:T(8,128)(2,1)}, u32[]{:S(2)}, u32[]{:S(2)}) collective-permute-start(bf16[4,256,256]{2,1,0:T(8,128)(2,1)} %bitcast.39), channel_id=1, source_target_pairs={{0,4},{1,5},{2,6},{3,7},{4,0},{5,1},{6,2},{7,3},{8,12},{9,13},{10,... | collective-permute-start | bytes 1572872 | tf_op jit(solution)/shard_map/ppermute | solution.py:25
  97.2 74.0 %all-to-all-start = ((bf16[16,64,512]{2,1,0:T(8,128)(2,1)}), bf16[16,64,512]{2,1,0:T(8,128)(2,1)}, u32[]{:S(2)}, u32[]{:S(2)}) async-start(bf16[16,64,512]{2,1,0:T(8,128)(2,1)} %bitcast.67), calls=%async_computation | async-start | bytes 2097152 | tf_op jit(solution)/shard_map/all_to_all | solution.py:74
  101.8 124.2 %all-gather.2.cloned.1.call-start = ((), (), s32[]{:S(2)}) async-start(), calls=%async_computation.1 | async-start | bytes 2228224 | tf_op jit(solution)/shard_map/all_gather | solution.py:78
  103.6 18.7 %slice-start = ((f32[2048,256]{1,0:T(8,128)}), f32[1024,256]{1,0:T(8,128)S(1)}, s32[]{:S(2)}) async-start(f32[2048,256]{1,0:T(8,128)} %copy-done.3), calls=%async_computation.2 | async-start | bytes 2097152 | tf_op jit(solution)/shard_map/slice | solution.py:46
  106.0 21.4 %collective-permute-start.10 = (bf16[2,256,256]{2,1,0:T(8,128)(2,1)S(1)}, bf16[2,256,256]{2,1,0:T(8,128)(2,1)S(1)}, u32[]{:S(2)}, u32[]{:S(2)}) collective-permute-start(bf16[2,256,256]{2,1,0:T(8,128)(2,1)S(1)} %get-tuple-element.7), channel_id=1, source_target_pairs={{0,4},{1,5},{2,6},{3,7},{4,0},{5,1},{6,2},{7,3},{8,12},{9,13},{10,... | collective-permute-start | bytes 786440 | tf_op jit(solution)/shard_map/ppermute | solution.py:25
  123.5 11.2 %copy-start.11 = (bf16[256,512]{1,0:T(8,128)(2,1)S(1)}, bf16[256,512]{1,0:T(8,128)(2,1)}, u32[]{:S(2)}) copy-start(bf16[256,512]{1,0:T(8,128)(2,1)} %copy-done.10) | copy-start | bytes 786436
  123.6 8.6 %collective-permute-start.23 = (bf16[256,256]{1,0:T(8,128)(2,1)S(1)}, bf16[256,256]{1,0:T(8,128)(2,1)S(1)}, u32[]{:S(2)}, u32[]{:S(2)}) collective-permute-start(bf16[256,256]{1,0:T(8,128)(2,1)S(1)} %get-tuple-element.41), channel_id=1, source_target_pairs={{0,3},{1,0},{2,1},{3,2},{4,7},{5,4},{6,5},{7,6},{8,11},{9,8},{10,9... | collective-permute-start | bytes 393224 | tf_op jit(solution)/shard_map/ppermute | solution.py:25
  125.4 7.9 %collective-permute-start.24 = (bf16[256,256]{1,0:T(8,128)(2,1)S(1)}, bf16[256,256]{1,0:T(8,128)(2,1)S(1)}, u32[]{:S(2)}, u32[]{:S(2)}) collective-permute-start(bf16[256,256]{1,0:T(8,128)(2,1)S(1)} %get-tuple-element.43), channel_id=1, source_target_pairs={{0,2},{1,3},{2,0},{3,1},{4,6},{5,7},{6,4},{7,5},{8,10},{9,11},{10,... | collective-permute-start | bytes 393224 | tf_op jit(solution)/shard_map/ppermute | solution.py:25
  125.7 9.1 %collective-permute-start.25 = (bf16[256,256]{1,0:T(8,128)(2,1)S(1)}, bf16[256,256]{1,0:T(8,128)(2,1)S(1)}, u32[]{:S(2)}, u32[]{:S(2)}) collective-permute-start(bf16[256,256]{1,0:T(8,128)(2,1)S(1)} %get-tuple-element.42), channel_id=1, source_target_pairs={{0,1},{1,2},{2,3},{3,0},{4,5},{5,6},{6,7},{7,4},{8,9},{9,10},{10,1... | collective-permute-start | bytes 393224 | tf_op jit(solution)/shard_map/ppermute | solution.py:25
  134.8 6.6 %collective-permute-start.26 = (bf16[256,256]{1,0:T(8,128)(2,1)S(1)}, bf16[256,256]{1,0:T(8,128)(2,1)S(1)}, u32[]{:S(2)}, u32[]{:S(2)}) collective-permute-start(bf16[256,256]{1,0:T(8,128)(2,1)S(1)} %get-tuple-element.11), channel_id=1, source_target_pairs={{0,1},{1,2},{2,3},{3,0},{4,5},{5,6},{6,7},{7,4},{8,9},{9,10},{10,1... | collective-permute-start | bytes 393224 | tf_op jit(solution)/shard_map/ppermute | solution.py:25
  135.2 14.3 %collective-permute-start.12 = (bf16[2,256,256]{2,1,0:T(8,128)(2,1)S(1)}, bf16[2,256,256]{2,1,0:T(8,128)(2,1)S(1)}, u32[]{:S(2)}, u32[]{:S(2)}) collective-permute-start(bf16[2,256,256]{2,1,0:T(8,128)(2,1)S(1)} %fusion.14), channel_id=1, source_target_pairs={{0,1},{1,2},{2,3},{3,0},{4,5},{5,6},{6,7},{7,4},{8,9},{9,10},{10,1... | collective-permute-start | bytes 786440 | tf_op jit(solution)/shard_map/ppermute | solution.py:25
  136.6 12.9 %collective-permute-start.13 = (bf16[2,256,256]{2,1,0:T(8,128)(2,1)S(1)}, bf16[2,256,256]{2,1,0:T(8,128)(2,1)S(1)}, u32[]{:S(2)}, u32[]{:S(2)}) collective-permute-start(bf16[2,256,256]{2,1,0:T(8,128)(2,1)S(1)} %fusion.14), channel_id=1, source_target_pairs={{0,2},{1,3},{2,0},{3,1},{4,6},{5,7},{6,4},{7,5},{8,10},{9,11},{10,... | collective-permute-start | bytes 786440 | tf_op jit(solution)/shard_map/ppermute | solution.py:25
  139.8 9.8 %collective-permute-start.14 = (bf16[2,256,256]{2,1,0:T(8,128)(2,1)S(1)}, bf16[2,256,256]{2,1,0:T(8,128)(2,1)S(1)}, u32[]{:S(2)}, u32[]{:S(2)}) collective-permute-start(bf16[2,256,256]{2,1,0:T(8,128)(2,1)S(1)} %fusion.14), channel_id=1, source_target_pairs={{0,3},{1,0},{2,1},{3,2},{4,7},{5,4},{6,5},{7,6},{8,11},{9,8},{10,9... | collective-permute-start | bytes 786440 | tf_op jit(solution)/shard_map/ppermute | solution.py:25
  141.2 7.2 %collective-permute-start.27 = (bf16[256,256]{1,0:T(8,128)(2,1)S(1)}, bf16[256,256]{1,0:T(8,128)(2,1)S(1)}, u32[]{:S(2)}, u32[]{:S(2)}) collective-permute-start(bf16[256,256]{1,0:T(8,128)(2,1)S(1)} %get-tuple-element.11), channel_id=1, source_target_pairs={{0,2},{1,3},{2,0},{3,1},{4,6},{5,7},{6,4},{7,5},{8,10},{9,11},{10,... | collective-permute-start | bytes 393224 | tf_op jit(solution)/shard_map/ppermute | solution.py:25
  141.4 7.9 %collective-permute-start.28 = (bf16[256,256]{1,0:T(8,128)(2,1)S(1)}, bf16[256,256]{1,0:T(8,128)(2,1)S(1)}, u32[]{:S(2)}, u32[]{:S(2)}) collective-permute-start(bf16[256,256]{1,0:T(8,128)(2,1)S(1)} %get-tuple-element.11), channel_id=1, source_target_pairs={{0,3},{1,0},{2,1},{3,2},{4,7},{5,4},{6,5},{7,6},{8,11},{9,8},{10,9... | collective-permute-start | bytes 393224 | tf_op jit(solution)/shard_map/ppermute | solution.py:25
  149.4 12.9 %collective-permute-start.29 = (bf16[4,256,256]{2,1,0:T(8,128)(2,1)S(1)}, bf16[4,256,256]{2,1,0:T(8,128)(2,1)S(1)}, u32[]{:S(2)}, u32[]{:S(2)}) collective-permute-start(bf16[4,256,256]{2,1,0:T(8,128)(2,1)S(1)} %get-tuple-element.40), channel_id=1, source_target_pairs={{0,4},{1,5},{2,6},{3,7},{4,0},{5,1},{6,2},{7,3},{8,12},{9,13},{10,... | collective-permute-start | bytes 1572872 | tf_op jit(solution)/shard_map/ppermute | solution.py:25
  151.8 2.9 %copy-start.15 = (f32[1,1024,512]{2,1,0:T(8,128)S(1)}, f32[1,1024,512]{2,1,0:T(8,128)}, u32[]{:S(2)}) copy-start(f32[1,1024,512]{2,1,0:T(8,128)} %param.12) | copy-start | bytes 6291460
  156.3 6.2 %copy-start.12 = (f32[2048,256]{1,0:T(8,128)}, f32[2048,256]{1,0:T(8,128)S(1)}, u32[]{:S(2)}) copy-start(f32[2048,256]{1,0:T(8,128)S(1)} %fusion.9) | copy-start | bytes 6291460
  157.3 15.9 %collective-permute-start.15 = (bf16[2,256,256]{2,1,0:T(8,128)(2,1)}, bf16[2,256,256]{2,1,0:T(8,128)(2,1)}, u32[]{:S(2)}, u32[]{:S(2)}) collective-permute-start(bf16[2,256,256]{2,1,0:T(8,128)(2,1)} %get-tuple-element.26), channel_id=1, source_target_pairs={{0,3},{1,0},{2,1},{3,2},{4,7},{5,4},{6,5},{7,6},{8,11},{9,8},{10,9... | collective-permute-start | bytes 786440 | tf_op jit(solution)/shard_map/ppermute | solution.py:25
  160.0 13.2 %collective-permute-start.16 = (bf16[2,256,256]{2,1,0:T(8,128)(2,1)}, bf16[2,256,256]{2,1,0:T(8,128)(2,1)}, u32[]{:S(2)}, u32[]{:S(2)}) collective-permute-start(bf16[2,256,256]{2,1,0:T(8,128)(2,1)} %get-tuple-element.28), channel_id=1, source_target_pairs={{0,2},{1,3},{2,0},{3,1},{4,6},{5,7},{6,4},{7,5},{8,10},{9,11},{10,... | collective-permute-start | bytes 786440 | tf_op jit(solution)/shard_map/ppermute | solution.py:25
  161.4 11.8 %collective-permute-start.17 = (bf16[2,256,256]{2,1,0:T(8,128)(2,1)S(1)}, bf16[2,256,256]{2,1,0:T(8,128)(2,1)}, u32[]{:S(2)}, u32[]{:S(2)}) collective-permute-start(bf16[2,256,256]{2,1,0:T(8,128)(2,1)S(1)} %get-tuple-element.27), channel_id=1, source_target_pairs={{0,1},{1,2},{2,3},{3,0},{4,5},{5,6},{6,7},{7,4},{8,9},{9,10},{10,1... | collective-permute-start | bytes 786440 | tf_op jit(solution)/shard_map/ppermute | solution.py:25
  167.7 11.0 %collective-permute-start.30 = (bf16[4,256,256]{2,1,0:T(8,128)(2,1)}, bf16[4,256,256]{2,1,0:T(8,128)(2,1)}, u32[]{:S(2)}, u32[]{:S(2)}) collective-permute-start(bf16[4,256,256]{2,1,0:T(8,128)(2,1)} %bitcast.54), channel_id=1, source_target_pairs={{0,4},{1,5},{2,6},{3,7},{4,0},{5,1},{6,2},{7,3},{8,12},{9,13},{10,... | collective-permute-start | bytes 1572872 | tf_op jit(solution)/shard_map/ppermute | solution.py:25
  174.8 8.4 %collective-permute-start.18 = (bf16[2,256,256]{2,1,0:T(8,128)(2,1)S(1)}, bf16[2,256,256]{2,1,0:T(8,128)(2,1)S(1)}, u32[]{:S(2)}, u32[]{:S(2)}) collective-permute-start(bf16[2,256,256]{2,1,0:T(8,128)(2,1)S(1)} %get-tuple-element.5), channel_id=1, source_target_pairs={{0,4},{1,5},{2,6},{3,7},{4,0},{5,1},{6,2},{7,3},{8,12},{9,13},{10,... | collective-permute-start | bytes 786440 | tf_op jit(solution)/shard_map/ppermute | solution.py:25
  179.9 5.8 %collective-permute-start.31 = (bf16[256,256]{1,0:T(8,128)(2,1)S(1)}, bf16[256,256]{1,0:T(8,128)(2,1)S(1)}, u32[]{:S(2)}, u32[]{:S(2)}) collective-permute-start(bf16[256,256]{1,0:T(8,128)(2,1)S(1)} %get-tuple-element.36), channel_id=1, source_target_pairs={{0,3},{1,0},{2,1},{3,2},{4,7},{5,4},{6,5},{7,6},{8,11},{9,8},{10,9... | collective-permute-start | bytes 393224 | tf_op jit(solution)/shard_map/ppermute | solution.py:25
  182.3 6.6 %collective-permute-start.32 = (bf16[256,256]{1,0:T(8,128)(2,1)S(1)}, bf16[256,256]{1,0:T(8,128)(2,1)S(1)}, u32[]{:S(2)}, u32[]{:S(2)}) collective-permute-start(bf16[256,256]{1,0:T(8,128)(2,1)S(1)} %get-tuple-element.38), channel_id=1, source_target_pairs={{0,2},{1,3},{2,0},{3,1},{4,6},{5,7},{6,4},{7,5},{8,10},{9,11},{10,... | collective-permute-start | bytes 393224 | tf_op jit(solution)/shard_map/ppermute | solution.py:25
  183.2 7.0 %collective-permute-start.33 = (bf16[256,256]{1,0:T(8,128)(2,1)S(1)}, bf16[256,256]{1,0:T(8,128)(2,1)S(1)}, u32[]{:S(2)}, u32[]{:S(2)}) collective-permute-start(bf16[256,256]{1,0:T(8,128)(2,1)S(1)} %get-tuple-element.37), channel_id=1, source_target_pairs={{0,1},{1,2},{2,3},{3,0},{4,5},{5,6},{6,7},{7,4},{8,9},{9,10},{10,1... | collective-permute-start | bytes 393224 | tf_op jit(solution)/shard_map/ppermute | solution.py:25
  190.3 10.4 %collective-permute-start.34 = (bf16[256,256]{1,0:T(8,128)(2,1)S(1)}, bf16[256,256]{1,0:T(8,128)(2,1)S(1)}, u32[]{:S(2)}, u32[]{:S(2)}) collective-permute-start(bf16[256,256]{1,0:T(8,128)(2,1)S(1)} %fusion.20), channel_id=1, source_target_pairs={{0,1},{1,2},{2,3},{3,0},{4,5},{5,6},{6,7},{7,4},{8,9},{9,10},{10,1... | collective-permute-start | bytes 393224 | tf_op jit(solution)/shard_map/ppermute | solution.py:25
  190.3 10.3 %collective-permute-start.35 = (bf16[256,256]{1,0:T(8,128)(2,1)S(1)}, bf16[256,256]{1,0:T(8,128)(2,1)S(1)}, u32[]{:S(2)}, u32[]{:S(2)}) collective-permute-start(bf16[256,256]{1,0:T(8,128)(2,1)S(1)} %fusion.20), channel_id=1, source_target_pairs={{0,2},{1,3},{2,0},{3,1},{4,6},{5,7},{6,4},{7,5},{8,10},{9,11},{10,... | collective-permute-start | bytes 393224 | tf_op jit(solution)/shard_map/ppermute | solution.py:25
  192.4 8.3 %collective-permute-start.36 = (bf16[256,256]{1,0:T(8,128)(2,1)S(1)}, bf16[256,256]{1,0:T(8,128)(2,1)S(1)}, u32[]{:S(2)}, u32[]{:S(2)}) collective-permute-start(bf16[256,256]{1,0:T(8,128)(2,1)S(1)} %fusion.20), channel_id=1, source_target_pairs={{0,3},{1,0},{2,1},{3,2},{4,7},{5,4},{6,5},{7,6},{8,11},{9,8},{10,9... | collective-permute-start | bytes 393224 | tf_op jit(solution)/shard_map/ppermute | solution.py:25
  200.8 14.4 %collective-permute-start.37 = (bf16[4,256,256]{2,1,0:T(8,128)(2,1)S(1)}, bf16[4,256,256]{2,1,0:T(8,128)(2,1)S(1)}, u32[]{:S(2)}, u32[]{:S(2)}) collective-permute-start(bf16[4,256,256]{2,1,0:T(8,128)(2,1)S(1)} %get-tuple-element.35), channel_id=1, source_target_pairs={{0,4},{1,5},{2,6},{3,7},{4,0},{5,1},{6,2},{7,3},{8,12},{9,13},{10,... | collective-permute-start | bytes 1572872 | tf_op jit(solution)/shard_map/ppermute | solution.py:25
  203.4 7.9 %collective-permute-start.19 = (bf16[2,256,256]{2,1,0:T(8,128)(2,1)S(1)}, bf16[2,256,256]{2,1,0:T(8,128)(2,1)S(1)}, u32[]{:S(2)}, u32[]{:S(2)}) collective-permute-start(bf16[2,256,256]{2,1,0:T(8,128)(2,1)S(1)} %fusion.15), channel_id=1, source_target_pairs={{0,1},{1,2},{2,3},{3,0},{4,5},{5,6},{6,7},{7,4},{8,9},{9,10},{10,1... | collective-permute-start | bytes 786440 | tf_op jit(solution)/shard_map/ppermute | solution.py:25
  204.6 10.4 %collective-permute-start.20 = (bf16[2,256,256]{2,1,0:T(8,128)(2,1)S(1)}, bf16[2,256,256]{2,1,0:T(8,128)(2,1)S(1)}, u32[]{:S(2)}, u32[]{:S(2)}) collective-permute-start(bf16[2,256,256]{2,1,0:T(8,128)(2,1)S(1)} %fusion.15), channel_id=1, source_target_pairs={{0,2},{1,3},{2,0},{3,1},{4,6},{5,7},{6,4},{7,5},{8,10},{9,11},{10,... | collective-permute-start | bytes 786440 | tf_op jit(solution)/shard_map/ppermute | solution.py:25
  207.8 7.2 %collective-permute-start.21 = (bf16[2,256,256]{2,1,0:T(8,128)(2,1)S(1)}, bf16[2,256,256]{2,1,0:T(8,128)(2,1)S(1)}, u32[]{:S(2)}, u32[]{:S(2)}) collective-permute-start(bf16[2,256,256]{2,1,0:T(8,128)(2,1)S(1)} %fusion.15), channel_id=1, source_target_pairs={{0,3},{1,0},{2,1},{3,2},{4,7},{5,4},{6,5},{7,6},{8,11},{9,8},{10,9... | collective-permute-start | bytes 786440 | tf_op jit(solution)/shard_map/ppermute | solution.py:25
  (14 other events, 27.7 us)
Sparse Core Ops, SparseCore 0:
  173.4 33.0 all-gather.1

commit v3 on v1

v3 whole, which is shorter than its diff:
```python
import functools

import jax
import jax.numpy as jnp
from jax import lax
from jax.experimental import pallas as pl
from jax.experimental.pallas import tpu as pltpu
from jax.sharding import PartitionSpec as P

NZ, NX = 2, 4
PICK_CUTS = 4


def adam_update(weights, first, second, grad):
    first = 0.9 * first + 0.1 * grad
    second = 0.95 * second + 0.05 * grad * grad
    update = first / (jnp.sqrt(second) + 1e-08) + 0.1 * weights
    return (weights - 0.001 * update, first, second, update)


def outer_nesterov(outer, momentum, delta):
    momentum_new = 0.9 * momentum + delta
    return (outer - 0.7 * (0.9 * momentum_new + delta), momentum_new)


def shift(value, dz, dx):
    pairs = [
        (z * NX + x, (z + dz) % NZ * NX + (x + dx) % NX) for z in range(NZ) for x in range(NX)
    ]
    return lax.ppermute(value, "fsdp", pairs)


def f32(value):
    return value.astype(jnp.float32)


def bf16(value):
    return value.astype(jnp.bfloat16)


def dot(a, b):
    return jnp.dot(a, b, preferred_element_type=jnp.float32)


def tie(*values):
    return lax.optimization_barrier(values)


def dot_t(a, b):
    return lax.dot_general(a, b, (((0,), (0,)), ((), ())), preferred_element_type=jnp.float32)


def pick_kernel(dx, x_ref, o_ref, held_ref, in_sems, out_sems):
    rows = o_ref.shape[1] // NZ
    tile = o_ref.shape[0] // PICK_CUTS
    me = lax.axis_index("fsdp")
    loads, stores = [], []
    for dz in range(NZ):
        owner = lax.rem(me // NX + dz, NZ) * NX + lax.rem(lax.rem(me, NX) + dx, NX)
        start = pl.multiple_of(owner * rows, rows)
        for cut in range(PICK_CUTS):
            span, place = pl.ds(cut * tile, tile), pl.ds(dz * rows, rows)
            loads.append(
                pltpu.make_async_copy(
                    x_ref.at[span, pl.ds(start, rows)],
                    held_ref.at[span, place],
                    in_sems.at[dz, cut],
                )
            )
            stores.append(
                pltpu.make_async_copy(
                    held_ref.at[span, place], o_ref.at[span, place], out_sems.at[dz, cut]
                )
            )
    for load in loads:
        load.start()
    for load, store in zip(loads, stores):
        load.wait()
        store.start()
    for store in stores:
        store.wait()


def pick(inputs, dx, rows):
    tokens = inputs.shape[0]
    return pl.pallas_call(
        functools.partial(pick_kernel, dx),
        out_shape=jax.ShapeDtypeStruct((tokens, NZ * rows), inputs.dtype),
        in_specs=[pl.BlockSpec(memory_space=pl.ANY)],
        out_specs=pl.BlockSpec(memory_space=pl.ANY),
        scratch_shapes=[
            pltpu.VMEM((tokens, NZ * rows), inputs.dtype),
            pltpu.SemaphoreType.DMA((NZ, PICK_CUTS)),
            pltpu.SemaphoreType.DMA((NZ, PICK_CUTS)),
        ],
        cost_estimate=pl.CostEstimate(
            flops=0, bytes_accessed=4 * tokens * NZ * rows, transcendentals=0
        ),
    )(inputs)


def send_parts(parts):
    return {dx: shift(parts[dx], 0, -dx) for dx in parts}


def add_parts(outputs, arrived):
    for dx in (1, 3, 2):
        outputs = outputs + f32(arrived[dx])
    return outputs


def shards(
    tokens, targets, block_master, block_first, block_second, frag_outer, frag_inner, frag_momentum
):
    inputs = tokens[0]
    groups = lax.axis_size("fsdp")
    replicas = lax.axis_size("rep")
    tok_local, features = inputs.shape
    tok_all = tok_local * groups
    rows, width = block_master.shape[1:]
    half = width // 2
    span_a, span_b = slice(0, half), slice(half, width)

    blocks = [None] * NX
    for dx in (2, 1, 3):
        picked = pick(inputs, dx, rows)
        blocks[dx] = shift(picked, 0, dx)
    master, picked = tie(block_master[0], picked)
    sent = bf16(master)
    blocks[0] = pick(inputs, 0, rows)
    both = jnp.concatenate([sent, shift(sent, 1, 0)], axis=0)

    frag_rows = frag_inner.shape[1] // replicas
    pieces = lax.all_to_all(
        frag_inner[0].reshape(replicas, frag_rows, -1), "rep", 0, 0
    )
    blocks[1], blocks[2], blocks[3], pieces = tie(blocks[1], blocks[2], blocks[3], pieces)
    inner_sum = lax.all_gather(jnp.sum(f32(pieces), axis=0), "rep", axis=0, tiled=True)

    teacher = f32(targets[0])
    (own,) = tie(dot(blocks[0], both))
    part = {dx: dot(blocks[dx], both) for dx in (1, 2, 3)}
    arrived_a = send_parts({dx: bf16(part[dx][:, span_a]) for dx in (1, 2, 3)})
    resid_a = bf16(add_parts(own[:, span_a], arrived_a) - teacher[:, span_a])
    part_b = {dx: bf16(part[dx][:, span_b]) for dx in (1, 2, 3)}
    part_b[1], part_b[2], part_b[3], resid_a = tie(part_b[1], part_b[2], part_b[3], resid_a)
    arrived_b = send_parts(part_b)
    resid_b = bf16(add_parts(own[:, span_b], arrived_b) - teacher[:, span_b])
    (held,) = tie(jnp.concatenate(blocks, axis=0))

    def state(span):
        return [x[0, :, span] for x in (block_master, block_first, block_second)]

    def gather(resid):
        return [resid] + [shift(resid, 0, dx) for dx in range(1, NX)]

    def near(row):
        return dot_t(held[:, :rows], row)

    def away(row):
        return bf16(dot_t(held[:, rows:], row))

    def step_one(resid_a, resid_b):
        row_a = jnp.concatenate(gather(resid_a), axis=0)
        row_b = jnp.concatenate(gather(resid_b), axis=0)
        away_a = away(row_a)
        got_a = shift(away_a, 1, 0)
        row_b, away_a = tie(row_b, away_a)
        away_b = away(row_b)
        got_b = shift(away_b, 1, 0)
        row_a, row_b, away_b = tie(row_a, row_b, away_b)
        return near(row_a), near(row_b), got_a, got_b

    own_a, own_b, got_a, got_b = step_one(resid_a, resid_b)
    grad_a = (own_a + f32(got_a)) / tok_all
    *state_a, update_a = adam_update(*state(span_a), grad_a)
    sent_a = bf16(state_a[0])
    sent_a, own_b = tie(sent_a, own_b)
    other_a = shift(sent_a, 1, 0)
    grad_b = (own_b + f32(got_b)) / tok_all
    *state_b, update_b = adam_update(*state(span_b), grad_b)
    sent_b = bf16(state_b[0])
    other_b = shift(sent_b, 1, 0)
    sent_a, sent_b = tie(sent_a, sent_b)

    both_a = jnp.concatenate([sent_a, other_a], axis=0)
    part_a = dot(held, both_a).reshape(NX, tok_local, half)
    arrived_a = send_parts({dx: bf16(part_a[dx]) for dx in (2, 1, 3)})
    both_b = jnp.concatenate([sent_b, other_b], axis=0)
    part_b = dot(held, both_b).reshape(NX, tok_local, half)
    arrived_b = send_parts({dx: bf16(part_b[dx]) for dx in (2, 1, 3)})
    resid_a = bf16(add_parts(part_a[0], arrived_a) - teacher[:, span_a])
    arrived_b[1], resid_a = tie(arrived_b[1], resid_a)
    resid_b = bf16(add_parts(part_b[0], arrived_b) - teacher[:, span_b])
    delta = frag_outer - inner_sum / replicas
    frag_params, momentum_out = outer_nesterov(frag_outer, frag_momentum, delta)
    own_a, own_b, got_a, got_b = step_one(resid_a, resid_b)
    own_a, own_b, frag_params, momentum_out = tie(own_a, own_b, frag_params, momentum_out)
    grad_a = (own_a + f32(got_a)) / tok_all
    total_a = update_a + adam_update(*state_a, grad_a)[3]
    total_a, own_b = tie(total_a, own_b)
    grad_b = (own_b + f32(got_b)) / tok_all
    total_b = update_b + adam_update(*state_b, grad_b)[3]
    block_shift = jnp.concatenate([total_a, total_b], axis=1)
    return (block_shift[None], frag_params, momentum_out)


def solution(mesh):
    in_specs = (
        P("rep", "fsdp", None),
        P("rep", "fsdp", None),
        P("rep", "fsdp", None),
        P("rep", "fsdp", None),
        P("rep", "fsdp", None),
        P("fsdp", None),
        P("rep", "fsdp", None),
        P("fsdp", None),
    )
    out_specs = (P("rep", "fsdp", None), P("fsdp", None), P("fsdp", None))
    return jax.shard_map(shards, mesh=mesh, in_specs=in_specs, out_specs=out_specs, check_vma=False)
```

time: 266 us -> 201 us (0.76)
  blocking collectives: 124 us -> 0 us
  starting transfers between devices: 14.3 us -> 69.7 us
  local copies, waits for them, and re-layouts: 37.5 us -> 0.26 us
  waiting for transfers between devices: 46.5 us -> 60.4 us
  other arithmetic: 6.75 us -> 19.8 us
  Pallas kernels: 0 us -> 8.58 us
  matrix products: 21.4 us -> 27.2 us
    all_to_all x3 -> x0, blocking collectives: 124 us -> none  [the longest x2 65.1 us: shards(): arrived = lax.all_to_all(sent, 'fsdp', 0, 0)]
    ppermute x0 -> x34, starting transfers between devices: none -> 64.6 us  [shift(): return lax.ppermute(value, 'fsdp', pairs)]
    ppermute x0 -> x34, waiting for transfers between devices: none -> 33.8 us  [shift(): return lax.ppermute(value, 'fsdp', pairs)]
    all_to_all x2 -> x0, waiting for transfers between devices: 30.5 us -> none  [shards(): lax.all_to_all(jnp.broadcast_to(resid_local[None], (groups, tok_local, wi...]
    unnamed x31 -> x34, local copies, waits for them, and re-layouts: 24.7 us -> 0.12 us
    all_to_all x1, waiting for transfers between devices: 15.9 us -> 26.5 us  [shards(): lax.all_to_all(frag_inner[0].reshape(replicas, frag_rows, -1), 'rep', 0, 0)]
    all_to_all x2 -> x0, starting transfers between devices: 9.06 us -> none  [shards(): lax.all_to_all(jnp.broadcast_to(resid_local[None], (groups, tok_local, wi...]
    pallas_call x0 -> x4, Pallas kernels: none -> 8.58 us  [pick(): pl.pallas_call(functools.partial(pick_kernel, dx), out_shape=jax.ShapeDty...]
  transfers between devices with their start and end apart: 4 -> 36, of which waited for: 3 -> 12; matrix products, arithmetic and copies ran while one was open for 14% -> 21% of each run, Pallas kernels for 0% -> 3%
where the time goes in v3:
time: 201 us; the launch traced here: 200 us
  starting transfers between devices  69.7 us (35%)
  waiting for transfers between devices  60.4 us (30%)
  matrix products  27.2 us (14%)
  other arithmetic  19.8 us (10%)
  between operations  14.5 us (7%)
  Pallas kernels  8.58 us (4%)
    ppermute x34, starting transfers between devices, shift(): return lax.ppermute(value, 'fsdp', pairs)  64.6 us
    ppermute x34, waiting for transfers between devices, shift(): return lax.ppermute(value, 'fsdp', pairs)  33.8 us
    all_to_all x1, waiting for transfers between devices, shards(): lax.all_to_all(frag_inner[0].reshape(replicas, frag_rows, -1), 'rep', 0, 0)  26.5 us
    dot_general x6, matrix products, dot(): return jnp.dot(a, b, preferred_element_type=jnp.float32)  13.6 us
    dot_general x8, matrix products, dot_t(): lax.dot_general(a, b, (((0,), (0,)), ((), ())), preferred_element_type=jn...  13.5 us
    pallas_call x4, Pallas kernels, pick(): pl.pallas_call(functools.partial(pick_kernel, dx), out_shape=jax.ShapeDty...  8.58 us
    add x1, other arithmetic, outer_nesterov(): momentum_new = 0.9 * momentum + delta  5.85 us
    all_to_all x1, starting transfers between devices, shards(): lax.all_to_all(frag_inner[0].reshape(replicas, frag_rows, -1), 'rep', 0, 0)  5.08 us
  transfers between devices with their start and end apart: 36, of which 12 were waited for; matrix products, arithmetic and copies ran while one was open for 21% of the time, Pallas kernels for 3%

profile of v3, /device:TPU:0, one launch (start us, length us, event | category | flops | bytes accessed | tf_op | source)
XLA Modules:
  0.0 200.4 jit_solution(11113865595624190665)
XLA Ops:
  7.2 2.1 %shard_map.106 = bf16[256,2048]{1,0:T(8,128)(2,1)} custom-call(bf16[256,8192]{1,0:T(8,128)(2,1)} %bitcast.73), custom_call_target="tpu_custom_call" | custom-call | bytes 2097152 | tf_op jit(solution)/shard_map/pallas_call | solution.py:86
  9.3 2.9 %collective-permute-start.2 = (bf16[256,2048]{1,0:T(8,128)(2,1)}, bf16[256,2048]{1,0:T(8,128)(2,1)}, u32[]{:S(2)}, u32[]{:S(2)}) collective-permute-start(bf16[256,2048]{1,0:T(8,128)(2,1)} %shard_map.106), channel_id=1, source_target_pairs={{0,3},{1,0},{2,1},{3,2},{4,7},{5,4},{6,5},{7,6},{8,11},{9,8},{10,9... | collective-permute-start | bytes 3145736 | tf_op jit(solution)/shard_map/ppermute | solution.py:30
  12.2 2.1 %shard_map.104 = bf16[256,2048]{1,0:T(8,128)(2,1)} custom-call(bf16[256,8192]{1,0:T(8,128)(2,1)} %bitcast.74), custom_call_target="tpu_custom_call" | custom-call | bytes 2097152 | tf_op jit(solution)/shard_map/pallas_call | solution.py:86
  14.4 2.2 %shard_map.105 = bf16[256,2048]{1,0:T(8,128)(2,1)} custom-call(bf16[256,8192]{1,0:T(8,128)(2,1)} %bitcast.75), custom_call_target="tpu_custom_call" | custom-call | bytes 2097152 | tf_op jit(solution)/shard_map/pallas_call | solution.py:86
  16.6 2.2 %collective-permute-start.1 = (bf16[256,2048]{1,0:T(8,128)(2,1)}, bf16[256,2048]{1,0:T(8,128)(2,1)}, u32[]{:S(2)}, u32[]{:S(2)}) collective-permute-start(bf16[256,2048]{1,0:T(8,128)(2,1)} %shard_map.105), channel_id=1, source_target_pairs={{0,2},{1,3},{2,0},{3,1},{4,6},{5,7},{6,4},{7,5},{8,10},{9,11},{10,... | collective-permute-start | bytes 3145736 | tf_op jit(solution)/shard_map/ppermute | solution.py:30
  19.9 3.9 %collective-permute-start.3 = (bf16[1024,512]{1,0:T(8,128)(2,1)}, bf16[1024,512]{1,0:T(8,128)(2,1)}, u32[]{:S(2)}, u32[]{:S(2)}) collective-permute-start(bf16[1024,512]{1,0:T(8,128)(2,1)} %convert_element_type.102), channel_id=1, source_target_pairs={{0,4},{1,5},{2,6},{3,7},{4,0},{5,1},{6,2},{7,3},{8,12},{9,13},{10,... | collective-permute-start | bytes 3145736 | tf_op jit(solution)/shard_map/ppermute | solution.py:30
  23.8 5.1 %all-to-all-start = ((bf16[16,64,512]{2,1,0:T(8,128)(2,1)}), bf16[16,64,512]{2,1,0:T(8,128)(2,1)}, u32[]{:S(2)}, u32[]{:S(2)}) async-start(bf16[16,64,512]{2,1,0:T(8,128)(2,1)} %bitcast.2), calls=%async_computation | async-start | bytes 2097152 | tf_op jit(solution)/shard_map/all_to_all | solution.py:134
  29.0 2.2 %shard_map.103 = bf16[256,2048]{1,0:T(8,128)(2,1)} custom-call(bf16[256,8192]{1,0:T(8,128)(2,1)} %bitcast.76), custom_call_target="tpu_custom_call" | custom-call | bytes 2097152 | tf_op jit(solution)/shard_map/pallas_call | solution.py:86
  31.2 26.5 %all-to-all-done = bf16[16,64,512]{2,1,0:T(8,128)(2,1)} async-done(((bf16[16,64,512]{2,1,0:T(8,128)(2,1)}), bf16[16,64,512]{2,1,0:T(8,128)(2,1)}, u32[]{:S(2)}, u32[]{:S(2)}) %all-to-all-start) | async-done | bytes 1048608 | tf_op jit(solution)/shard_map/all_to_all | solution.py:134
  57.7 5.3 %collective-permute-done = bf16[256,2048]{1,0:T(8,128)(2,1)} collective-permute-done((bf16[256,2048]{1,0:T(8,128)(2,1)}, bf16[256,2048]{1,0:T(8,128)(2,1)}, u32[]{:S(2)}, u32[]{:S(2)}) %collective-permute-start) | collective-permute-done | bytes 1048608 | tf_op jit(solution)/shard_map/ppermute | solution.py:30
  63.0 2.6 %convolution_convert_fusion = bf16[256,512]{1,0:T(8,128)(2,1)S(1)} fusion(bf16[256,2048]{1,0:T(8,128)(2,1)} %collective-permute-done.2, bf16[1024,512]{1,0:T(8,128)(2,1)} %collective-permute-done.3, bf16[1024,512]{1,0:T(8,128)(2,1)} %convert_element_type.102), kind=kOutput, calls=%fused_computation.28 | convolution fusion | flops 541196288 | bytes 3407872 | tf_op jit(solution)/shard_map/dot_general | solution.py:42
  65.7 2.6 %convolution_convert_fusion.1 = bf16[256,512]{1,0:T(8,128)(2,1)S(1)} fusion(bf16[256,2048]{1,0:T(8,128)(2,1)} %collective-permute-done.1, bf16[1024,512]{1,0:T(8,128)(2,1)} %collective-permute-done.3, bf16[1024,512]{1,0:T(8,128)(2,1)} %convert_element_type.102), kind=kOutput, calls=%fused_computation.29 | convolution fusion | flops 541196288 | bytes 3407872 | tf_op jit(solution)/shard_map/dot_general | solution.py:42
  69.4 2.6 %convolution_convert_fusion.2 = bf16[256,512]{1,0:T(8,128)(2,1)S(1)} fusion(bf16[256,2048]{1,0:T(8,128)(2,1)} %collective-permute-done, bf16[1024,512]{1,0:T(8,128)(2,1)} %collective-permute-done.3, bf16[1024,512]{1,0:T(8,128)(2,1)} %convert_element_type.102), kind=kOutput, calls=%fused_computation.30 | convolution fusion | flops 541196288 | bytes 3407872 | tf_op jit(solution)/shard_map/dot_general | solution.py:42
  72.0 2.3 %collective-permute-start.4 = (bf16[256,256]{1,0:T(8,128)(2,1)S(1)}, bf16[256,256]{1,0:T(8,128)(2,1)S(1)}, u32[]{:S(2)}, u32[]{:S(2)}) collective-permute-start(bf16[256,256]{1,0:T(8,128)(2,1)S(1)} %get-tuple-element.67), channel_id=1, source_target_pairs={{0,3},{1,0},{2,1},{3,2},{4,7},{5,4},{6,5},{7,6},{8,11},{9,8},{10,9... | collective-permute-start | bytes 393224 | tf_op jit(solution)/shard_map/ppermute | solution.py:30
  74.3 2.2 %convolution_bitcast_fusion = f32[256,512]{1,0:T(8,128)S(1)} fusion(bf16[256,2048]{1,0:T(8,128)(2,1)S(1)} %copy-done.8, bf16[1024,512]{1,0:T(8,128)(2,1)} %collective-permute-done.3, bf16[1024,512]{1,0:T(8,128)(2,1)} %convert_element_type.102), kind=kOutput, calls=%fused_computation.27 | convolution fusion | flops 541065216 | bytes 3670016 | tf_op jit(solution)/shard_map/dot_general | solution.py:42
  78.1 2.7 %collective-permute-start.10 = (bf16[256,256]{1,0:T(8,128)(2,1)S(1)}, bf16[256,256]{1,0:T(8,128)(2,1)S(1)}, u32[]{:S(2)}, u32[]{:S(2)}) collective-permute-start(bf16[256,256]{1,0:T(8,128)(2,1)S(1)} %get-tuple-element.35), channel_id=1, source_target_pairs={{0,3},{1,0},{2,1},{3,2},{4,7},{5,4},{6,5},{7,6},{8,11},{9,8},{10,9... | collective-permute-start | bytes 393224 | tf_op jit(solution)/shard_map/ppermute | solution.py:30
  80.8 1.9 collective-permute-start.12
  82.7 2.1 %pad_maximum_fusion = bf16[1024,2048]{1,0:T(8,128)(2,1)S(1)} fusion(bf16[256,2048]{1,0:T(8,128)(2,1)} %collective-permute-done.2, bf16[256,2048]{1,0:T(8,128)(2,1)} %collective-permute-done.1, bf16[256,2048]{1,0:T(8,128)(2,1)} %collective-permute-done, bf16[256,2048]{1,0:T(8,128)(2,1)S(1)} %copy-done.8), kind=kLoop, calls=%fused_computation | loop fusion | flops 16777216 | bytes 8388608 | tf_op jit(solution)/shard_map/concatenate | solution.py:149
  84.8 2.3 %collective-permute-start.7 = (bf16[256,256]{1,0:T(8,128)(2,1)S(1)}, bf16[256,256]{1,0:T(8,128)(2,1)S(1)}, u32[]{:S(2)}, u32[]{:S(2)}) collective-permute-start(bf16[256,256]{1,0:T(8,128)(2,1)S(1)} %fusion.54), channel_id=1, source_target_pairs={{0,1},{1,2},{2,3},{3,0},{4,5},{5,6},{6,7},{7,4},{8,9},{9,10},{10,1... | collective-permute-start | bytes 393224 | tf_op jit(solution)/shard_map/ppermute | solution.py:30
  87.1 1.9 collective-permute-start.8
  92.9 3.9 %collective-permute-done.7 = bf16[256,256]{1,0:T(8,128)(2,1)S(1)} collective-permute-done((bf16[256,256]{1,0:T(8,128)(2,1)S(1)}, bf16[256,256]{1,0:T(8,128)(2,1)S(1)}, u32[]{:S(2)}, u32[]{:S(2)}) %collective-permute-start.7) | collective-permute-done | bytes 131104 | tf_op jit(solution)/shard_map/ppermute | solution.py:30
  97.6 4.0 %collective-permute-start.16 = (bf16[1024,256]{1,0:T(8,128)(2,1)S(1)}, bf16[1024,256]{1,0:T(8,128)(2,1)S(1)}, u32[]{:S(2)}, u32[]{:S(2)}) collective-permute-start(bf16[1024,256]{1,0:T(8,128)(2,1)S(1)} %fusion.15), channel_id=1, source_target_pairs={{0,4},{1,5},{2,6},{3,7},{4,0},{5,1},{6,2},{7,3},{8,12},{9,13},{10,... | collective-permute-start | bytes 1572872 | tf_op jit(solution)/shard_map/ppermute | solution.py:30
  103.4 3.9 %collective-permute-start.17 = (bf16[1024,256]{1,0:T(8,128)(2,1)}, bf16[1024,256]{1,0:T(8,128)(2,1)S(1)}, u32[]{:S(2)}, u32[]{:S(2)}) collective-permute-start(bf16[1024,256]{1,0:T(8,128)(2,1)} %fusion.18), channel_id=1, source_target_pairs={{0,4},{1,5},{2,6},{3,7},{4,0},{5,1},{6,2},{7,3},{8,12},{9,13},{10,... | collective-permute-start | bytes 1572872 | tf_op jit(solution)/shard_map/ppermute | solution.py:30
  107.3 1.7 fusion.12
  109.0 4.5 %collective-permute-done.16 = bf16[1024,256]{1,0:T(8,128)(2,1)S(1)} collective-permute-done((bf16[1024,256]{1,0:T(8,128)(2,1)S(1)}, bf16[1024,256]{1,0:T(8,128)(2,1)S(1)}, u32[]{:S(2)}, u32[]{:S(2)}) %collective-permute-start.16) | collective-permute-done | bytes 524320 | tf_op jit(solution)/shard_map/ppermute | solution.py:30
  113.5 2.8 %fusion.37 = (bf16[1024,256]{1,0:T(8,128)(2,1)}, f32[1024,256]{1,0:T(8,128)}, f32[1024,256]{1,0:T(8,128)}) fusion(f32[1,1024,512]{2,1,0:T(8,128)S(1)} %copy-done, f32[1,1024,512]{2,1,0:T(8,128)S(1)} %copy-done.3, f32[1,1024,512]{2,1,0:T(8,128)S(1)} %copy-done.1, bf16[1024,256]{1,0:T(8,128)(2,1)S(1)} %collective-permute-done.16, ...), kind=kOutput, calls=%fused_computation.52 | convolution fusion | flops 541327360 | bytes 8912896 | tf_op jit(solution)/shard_map/dot_general | solution.py:50
  116.4 3.7 %collective-permute-start.20 = (bf16[1024,256]{1,0:T(8,128)(2,1)}, bf16[1024,256]{1,0:T(8,128)(2,1)}, u32[]{:S(2)}, u32[]{:S(2)}) collective-permute-start(bf16[1024,256]{1,0:T(8,128)(2,1)} %get-tuple-element.44), channel_id=1, source_target_pairs={{0,4},{1,5},{2,6},{3,7},{4,0},{5,1},{6,2},{7,3},{8,12},{9,13},{10,... | collective-permute-start | bytes 1572872 | tf_op jit(solution)/shard_map/ppermute | solution.py:30
  120.1 2.0 %convert_reduce_fusion = f32[64,512]{1,0:T(8,128)} fusion(bf16[16,64,512]{2,1,0:T(8,128)(2,1)} %all-to-all-done), kind=kLoop, calls=%fused_computation.5 | loop fusion | flops 1015808 | bytes 1179648 | tf_op jit(solution)/shard_map/reduce_sum | solution.py:138
  122.1 2.6 %collective-permute-done.17 = bf16[1024,256]{1,0:T(8,128)(2,1)S(1)} collective-permute-done((bf16[1024,256]{1,0:T(8,128)(2,1)}, bf16[1024,256]{1,0:T(8,128)(2,1)S(1)}, u32[]{:S(2)}, u32[]{:S(2)}) %collective-permute-start.17) | collective-permute-done | bytes 524320 | tf_op jit(solution)/shard_map/ppermute | solution.py:30
  124.8 2.7 %fusion.38 = bf16[1024,256]{1,0:T(8,128)(2,1)S(1)} fusion(f32[1,1024,512]{2,1,0:T(8,128)S(1)} %copy-done, f32[1024,256]{1,0:T(8,128)} %fusion.12, bf16[1024,256]{1,0:T(8,128)(2,1)S(1)} %collective-permute-done.17, f32[1,1024,512]{2,1,0:T(8,128)} %param.11, f32[1,1024,512]{2,1,0:T(8,128)} %param.12), kind=kLoop, calls=%fused_computation.53 | loop fusion | flops 4456448 | bytes 5242880 | tf_op jit(solution)/shard_map/convert_element_type | solution.py:38
  127.5 3.8 %collective-permute-start.18 = (bf16[1024,256]{1,0:T(8,128)(2,1)S(1)}, bf16[1024,256]{1,0:T(8,128)(2,1)S(1)}, u32[]{:S(2)}, u32[]{:S(2)}) collective-permute-start(bf16[1024,256]{1,0:T(8,128)(2,1)S(1)} %fusion.38), channel_id=1, source_target_pairs={{0,4},{1,5},{2,6},{3,7},{4,0},{5,1},{6,2},{7,3},{8,12},{9,13},{10,... | collective-permute-start | bytes 1572872 | tf_op jit(solution)/shard_map/ppermute | solution.py:30
  131.2 8.3 %collective-permute-done.20 = bf16[1024,256]{1,0:T(8,128)(2,1)} collective-permute-done((bf16[1024,256]{1,0:T(8,128)(2,1)}, bf16[1024,256]{1,0:T(8,128)(2,1)}, u32[]{:S(2)}, u32[]{:S(2)}) %collective-permute-start.20) | collective-permute-done | bytes 524320 | tf_op jit(solution)/shard_map/ppermute | solution.py:30
  139.5 2.5 %fusion.64 = (bf16[1024,256]{1,0:T(8,128)(2,1)S(1)}, f32[1024,256]{1,0:T(8,128)S(1)}) fusion(bf16[1024,2048]{1,0:T(8,128)(2,1)S(1)} %copy-done.7, bf16[1024,256]{1,0:T(8,128)(2,1)} %collective-permute-done.20, bf16[1024,256]{1,0:T(8,128)(2,1)} %get-tuple-element.44), kind=kOutput, calls=%fused_computation.93 | convolution fusion | flops 1076101120 | bytes 6815744 | tf_op jit(solution)/shard_map/dot_general | solution.py:42
  143.5 1.8 collective-permute-start.22
  145.3 2.0 collective-permute-start.23
  147.3 3.9 %collective-permute-done.18 = bf16[1024,256]{1,0:T(8,128)(2,1)S(1)} collective-permute-done((bf16[1024,256]{1,0:T(8,128)(2,1)S(1)}, bf16[1024,256]{1,0:T(8,128)(2,1)S(1)}, u32[]{:S(2)}, u32[]{:S(2)}) %collective-permute-start.18) | collective-permute-done | bytes 524320 | tf_op jit(solution)/shard_map/ppermute | solution.py:30
  154.5 1.6 collective-permute-start.28
  156.2 2.3 %collective-permute-done.19 = bf16[256,256]{1,0:T(8,128)(2,1)S(1)} collective-permute-done((bf16[256,256]{1,0:T(8,128)(2,1)S(1)}, bf16[256,256]{1,0:T(8,128)(2,1)S(1)}, u32[]{:S(2)}, u32[]{:S(2)}) %collective-permute-start.19) | collective-permute-done | bytes 131104 | tf_op jit(solution)/shard_map/ppermute | solution.py:30
  158.6 3.0 %collective-permute-start.24 = (bf16[256,256]{1,0:T(8,128)(2,1)S(1)}, bf16[256,256]{1,0:T(8,128)(2,1)S(1)}, u32[]{:S(2)}, u32[]{:S(2)}) collective-permute-start(bf16[256,256]{1,0:T(8,128)(2,1)S(1)} %fusion.46), channel_id=1, source_target_pairs={{0,1},{1,2},{2,3},{3,0},{4,5},{5,6},{6,7},{7,4},{8,9},{9,10},{10,1... | collective-permute-start | bytes 393224 | tf_op jit(solution)/shard_map/ppermute | solution.py:30
  161.6 2.7 %collective-permute-start.26 = (bf16[256,256]{1,0:T(8,128)(2,1)S(1)}, bf16[256,256]{1,0:T(8,128)(2,1)S(1)}, u32[]{:S(2)}, u32[]{:S(2)}) collective-permute-start(bf16[256,256]{1,0:T(8,128)(2,1)S(1)} %fusion.46), channel_id=1, source_target_pairs={{0,3},{1,0},{2,1},{3,2},{4,7},{5,4},{6,5},{7,6},{8,11},{9,8},{10,9... | collective-permute-start | bytes 393224 | tf_op jit(solution)/shard_map/ppermute | solution.py:30
  164.5 2.9 %collective-permute-start.30 = (bf16[256,256]{1,0:T(8,128)(2,1)S(1)}, bf16[256,256]{1,0:T(8,128)(2,1)S(1)}, u32[]{:S(2)}, u32[]{:S(2)}) collective-permute-start(bf16[256,256]{1,0:T(8,128)(2,1)S(1)} %fusion.42), channel_id=1, source_target_pairs={{0,2},{1,3},{2,0},{3,1},{4,6},{5,7},{6,4},{7,5},{8,10},{9,11},{10,... | collective-permute-start | bytes 393224 | tf_op jit(solution)/shard_map/ppermute | solution.py:30
  169.7 4.0 %collective-permute-start.32 = (bf16[1024,256]{1,0:T(8,128)(2,1)}, bf16[1024,256]{1,0:T(8,128)(2,1)}, u32[]{:S(2)}, u32[]{:S(2)}) collective-permute-start(bf16[1024,256]{1,0:T(8,128)(2,1)} %fusion.21), channel_id=1, source_target_pairs={{0,4},{1,5},{2,6},{3,7},{4,0},{5,1},{6,2},{7,3},{8,12},{9,13},{10,... | collective-permute-start | bytes 1572872 | tf_op jit(solution)/shard_map/ppermute | solution.py:30
  175.3 3.3 %collective-permute-start.33 = (bf16[1024,256]{1,0:T(8,128)(2,1)}, bf16[1024,256]{1,0:T(8,128)(2,1)S(1)}, u32[]{:S(2)}, u32[]{:S(2)}) collective-permute-start(bf16[1024,256]{1,0:T(8,128)(2,1)} %fusion.24), channel_id=1, source_target_pairs={{0,4},{1,5},{2,6},{3,7},{4,0},{5,1},{6,2},{7,3},{8,12},{9,13},{10,... | collective-permute-start | bytes 1572872 | tf_op jit(solution)/shard_map/ppermute | solution.py:30
  178.6 1.8 fusion.8
  180.3 1.7 fusion.10
  182.1 5.9 %multiply_add_fusion = (f32[1024,512]{1,0:T(8,128)}, f32[1024,512]{1,0:T(8,128)}) fusion(f32[1024,512]{1,0:T(8,128)} %param.15, f32[1024,512]{1,0:T(8,128)} %param.13, f32[1024,512]{1,0:T(8,128)} %all-gather.2.cloned.1.call-done), kind=kLoop, calls=%fused_computation.6 | loop fusion | flops 4194304 | bytes 10485760 | tf_op jit(solution)/shard_map/add | solution.py:22
  188.0 2.3 %add_add_fusion.1 = f32[1024,256]{1,0:T(8,128)S(1)} fusion(f32[1024,256]{1,0:T(8,128)S(1)} %copy-done.9, f32[1024,256]{1,0:T(8,128)S(1)} %copy-done.12, bf16[1024,256]{1,0:T(8,128)(2,1)} %collective-permute-done.32, f32[1,1024,512]{2,1,0:T(8,128)S(1)} %copy-done, f32[1024,256]{1,0:T(8,128)S(1)} %copy-done.10, f32[1,1024,512]{2,1,0:T(8,128)S(1)} %copy-done.2, ...), kind=kLoop, calls=%fused_computation.50 | loop fusion | flops 6553600 | bytes 7864320 | tf_op jit(solution)/shard_map/add | solution.py:200
  190.4 1.6 add_add_fusion
  (99 shorter events, 21.3 us)
Async XLA Ops:
  9.3 48.4 %collective-permute-start.2 = (bf16[256,2048]{1,0:T(8,128)(2,1)}, bf16[256,2048]{1,0:T(8,128)(2,1)}, u32[]{:S(2)}, u32[]{:S(2)}) collective-permute-start(bf16[256,2048]{1,0:T(8,128)(2,1)} %shard_map.106), channel_id=1, source_target_pairs={{0,3},{1,0},{2,1},{3,2},{4,7},{5,4},{6,5},{7,6},{8,11},{9,8},{10,9... | collective-permute-start | bytes 3145736 | tf_op jit(solution)/shard_map/ppermute | solution.py:30
  14.3 4.5 %copy-start = (f32[1,1024,512]{2,1,0:T(8,128)S(1)}, f32[1,1024,512]{2,1,0:T(8,128)}, u32[]{:S(2)}) copy-start(f32[1,1024,512]{2,1,0:T(8,128)} %param.10) | copy-start | bytes 6291460
  14.3 48.7 %collective-permute-start = (bf16[256,2048]{1,0:T(8,128)(2,1)}, bf16[256,2048]{1,0:T(8,128)(2,1)}, u32[]{:S(2)}, u32[]{:S(2)}) collective-permute-start(bf16[256,2048]{1,0:T(8,128)(2,1)} %shard_map.104), channel_id=1, source_target_pairs={{0,1},{1,2},{2,3},{3,0},{4,5},{5,6},{6,7},{7,4},{8,9},{9,10},{10,1... | collective-permute-start | bytes 3145736 | tf_op jit(solution)/shard_map/ppermute | solution.py:30
  16.6 46.4 %collective-permute-start.1 = (bf16[256,2048]{1,0:T(8,128)(2,1)}, bf16[256,2048]{1,0:T(8,128)(2,1)}, u32[]{:S(2)}, u32[]{:S(2)}) collective-permute-start(bf16[256,2048]{1,0:T(8,128)(2,1)} %shard_map.105), channel_id=1, source_target_pairs={{0,2},{1,3},{2,0},{3,1},{4,6},{5,7},{6,4},{7,5},{8,10},{9,11},{10,... | collective-permute-start | bytes 3145736 | tf_op jit(solution)/shard_map/ppermute | solution.py:30
  19.9 43.1 %collective-permute-start.3 = (bf16[1024,512]{1,0:T(8,128)(2,1)}, bf16[1024,512]{1,0:T(8,128)(2,1)}, u32[]{:S(2)}, u32[]{:S(2)}) collective-permute-start(bf16[1024,512]{1,0:T(8,128)(2,1)} %convert_element_type.102), channel_id=1, source_target_pairs={{0,4},{1,5},{2,6},{3,7},{4,0},{5,1},{6,2},{7,3},{8,12},{9,13},{10,... | collective-permute-start | bytes 3145736 | tf_op jit(solution)/shard_map/ppermute | solution.py:30
  23.8 33.9 %all-to-all-start = ((bf16[16,64,512]{2,1,0:T(8,128)(2,1)}), bf16[16,64,512]{2,1,0:T(8,128)(2,1)}, u32[]{:S(2)}, u32[]{:S(2)}) async-start(bf16[16,64,512]{2,1,0:T(8,128)(2,1)} %bitcast.2), calls=%async_computation | async-start | bytes 2097152 | tf_op jit(solution)/shard_map/all_to_all | solution.py:134
  28.9 153.2 %all-gather.2.cloned.1.call-start = ((), (), s32[]{:S(2)}) async-start(), calls=%async_computation.1 | async-start | bytes 2228224 | tf_op jit(solution)/shard_map/all_gather | solution.py:138
  65.6 11.0 %collective-permute-start.5 = (bf16[256,256]{1,0:T(8,128)(2,1)S(1)}, bf16[256,256]{1,0:T(8,128)(2,1)S(1)}, u32[]{:S(2)}, u32[]{:S(2)}) collective-permute-start(bf16[256,256]{1,0:T(8,128)(2,1)S(1)} %get-tuple-element.69), channel_id=1, source_target_pairs={{0,1},{1,2},{2,3},{3,0},{4,5},{5,6},{6,7},{7,4},{8,9},{9,10},{10,1... | collective-permute-start | bytes 393224 | tf_op jit(solution)/shard_map/ppermute | solution.py:30
  68.3 6.1 %copy-start.8 = (bf16[256,2048]{1,0:T(8,128)(2,1)S(1)}, bf16[256,2048]{1,0:T(8,128)(2,1)}, u32[]{:S(2)}) copy-start(bf16[256,2048]{1,0:T(8,128)(2,1)} %shard_map.103) | copy-start | bytes 3145732
  68.3 8.3 %collective-permute-start.6 = (bf16[256,256]{1,0:T(8,128)(2,1)S(1)}, bf16[256,256]{1,0:T(8,128)(2,1)S(1)}, u32[]{:S(2)}, u32[]{:S(2)}) collective-permute-start(bf16[256,256]{1,0:T(8,128)(2,1)S(1)} %get-tuple-element.71), channel_id=1, source_target_pairs={{0,2},{1,3},{2,0},{3,1},{4,6},{5,7},{6,4},{7,5},{8,10},{9,11},{10,... | collective-permute-start | bytes 393224 | tf_op jit(solution)/shard_map/ppermute | solution.py:30
  72.0 6.1 %collective-permute-start.4 = (bf16[256,256]{1,0:T(8,128)(2,1)S(1)}, bf16[256,256]{1,0:T(8,128)(2,1)S(1)}, u32[]{:S(2)}, u32[]{:S(2)}) collective-permute-start(bf16[256,256]{1,0:T(8,128)(2,1)S(1)} %get-tuple-element.67), channel_id=1, source_target_pairs={{0,3},{1,0},{2,1},{3,2},{4,7},{5,4},{6,5},{7,6},{8,11},{9,8},{10,9... | collective-permute-start | bytes 393224 | tf_op jit(solution)/shard_map/ppermute | solution.py:30
  78.1 10.8 %collective-permute-start.10 = (bf16[256,256]{1,0:T(8,128)(2,1)S(1)}, bf16[256,256]{1,0:T(8,128)(2,1)S(1)}, u32[]{:S(2)}, u32[]{:S(2)}) collective-permute-start(bf16[256,256]{1,0:T(8,128)(2,1)S(1)} %get-tuple-element.35), channel_id=1, source_target_pairs={{0,3},{1,0},{2,1},{3,2},{4,7},{5,4},{6,5},{7,6},{8,11},{9,8},{10,9... | collective-permute-start | bytes 393224 | tf_op jit(solution)/shard_map/ppermute | solution.py:30
  80.8 10.4 %collective-permute-start.11 = (bf16[256,256]{1,0:T(8,128)(2,1)S(1)}, bf16[256,256]{1,0:T(8,128)(2,1)S(1)}, u32[]{:S(2)}, u32[]{:S(2)}) collective-permute-start(bf16[256,256]{1,0:T(8,128)(2,1)S(1)} %get-tuple-element.36), channel_id=1, source_target_pairs={{0,1},{1,2},{2,3},{3,0},{4,5},{5,6},{6,7},{7,4},{8,9},{9,10},{10,1... | collective-permute-start | bytes 393224 | tf_op jit(solution)/shard_map/ppermute | solution.py:30
  80.8 10.4 %collective-permute-start.12 = (bf16[256,256]{1,0:T(8,128)(2,1)S(1)}, bf16[256,256]{1,0:T(8,128)(2,1)S(1)}, u32[]{:S(2)}, u32[]{:S(2)}) collective-permute-start(bf16[256,256]{1,0:T(8,128)(2,1)S(1)} %get-tuple-element.37), channel_id=1, source_target_pairs={{0,2},{1,3},{2,0},{3,1},{4,6},{5,7},{6,4},{7,5},{8,10},{9,11},{10,... | collective-permute-start | bytes 393224 | tf_op jit(solution)/shard_map/ppermute | solution.py:30
  84.8 28.8 %copy-start.6 = (bf16[1024,2048]{1,0:T(8,128)(2,1)}, bf16[1024,2048]{1,0:T(8,128)(2,1)S(1)}, u32[]{:S(2)}) copy-start(bf16[1024,2048]{1,0:T(8,128)(2,1)S(1)} %pad_maximum_fusion) | copy-start | bytes 12582916
  84.8 12.0 %collective-permute-start.7 = (bf16[256,256]{1,0:T(8,128)(2,1)S(1)}, bf16[256,256]{1,0:T(8,128)(2,1)S(1)}, u32[]{:S(2)}, u32[]{:S(2)}) collective-permute-start(bf16[256,256]{1,0:T(8,128)(2,1)S(1)} %fusion.54), channel_id=1, source_target_pairs={{0,1},{1,2},{2,3},{3,0},{4,5},{5,6},{6,7},{7,4},{8,9},{9,10},{10,1... | collective-permute-start | bytes 393224 | tf_op jit(solution)/shard_map/ppermute | solution.py:30
  87.1 9.7 %collective-permute-start.8 = (bf16[256,256]{1,0:T(8,128)(2,1)S(1)}, bf16[256,256]{1,0:T(8,128)(2,1)S(1)}, u32[]{:S(2)}, u32[]{:S(2)}) collective-permute-start(bf16[256,256]{1,0:T(8,128)(2,1)S(1)} %fusion.54), channel_id=1, source_target_pairs={{0,2},{1,3},{2,0},{3,1},{4,6},{5,7},{6,4},{7,5},{8,10},{9,11},{10,... | collective-permute-start | bytes 393224 | tf_op jit(solution)/shard_map/ppermute | solution.py:30
  89.0 7.9 %collective-permute-start.9 = (bf16[256,256]{1,0:T(8,128)(2,1)S(1)}, bf16[256,256]{1,0:T(8,128)(2,1)S(1)}, u32[]{:S(2)}, u32[]{:S(2)}) collective-permute-start(bf16[256,256]{1,0:T(8,128)(2,1)S(1)} %fusion.54), channel_id=1, source_target_pairs={{0,3},{1,0},{2,1},{3,2},{4,7},{5,4},{6,5},{7,6},{8,11},{9,8},{10,9... | collective-permute-start | bytes 393224 | tf_op jit(solution)/shard_map/ppermute | solution.py:30
  91.3 10.3 %collective-permute-start.13 = (bf16[256,256]{1,0:T(8,128)(2,1)S(1)}, bf16[256,256]{1,0:T(8,128)(2,1)S(1)}, u32[]{:S(2)}, u32[]{:S(2)}) collective-permute-start(bf16[256,256]{1,0:T(8,128)(2,1)S(1)} %fusion.50), channel_id=1, source_target_pairs={{0,1},{1,2},{2,3},{3,0},{4,5},{5,6},{6,7},{7,4},{8,9},{9,10},{10,1... | collective-permute-start | bytes 393224 | tf_op jit(solution)/shard_map/ppermute | solution.py:30
  91.4 10.2 %collective-permute-start.14 = (bf16[256,256]{1,0:T(8,128)(2,1)S(1)}, bf16[256,256]{1,0:T(8,128)(2,1)S(1)}, u32[]{:S(2)}, u32[]{:S(2)}) collective-permute-start(bf16[256,256]{1,0:T(8,128)(2,1)S(1)} %fusion.50), channel_id=1, source_target_pairs={{0,2},{1,3},{2,0},{3,1},{4,6},{5,7},{6,4},{7,5},{8,10},{9,11},{10,... | collective-permute-start | bytes 393224 | tf_op jit(solution)/shard_map/ppermute | solution.py:30
  96.8 5.0 %collective-permute-start.15 = (bf16[256,256]{1,0:T(8,128)(2,1)S(1)}, bf16[256,256]{1,0:T(8,128)(2,1)S(1)}, u32[]{:S(2)}, u32[]{:S(2)}) collective-permute-start(bf16[256,256]{1,0:T(8,128)(2,1)S(1)} %fusion.50), channel_id=1, source_target_pairs={{0,3},{1,0},{2,1},{3,2},{4,7},{5,4},{6,5},{7,6},{8,11},{9,8},{10,9... | collective-permute-start | bytes 393224 | tf_op jit(solution)/shard_map/ppermute | solution.py:30
  97.6 15.9 %collective-permute-start.16 = (bf16[1024,256]{1,0:T(8,128)(2,1)S(1)}, bf16[1024,256]{1,0:T(8,128)(2,1)S(1)}, u32[]{:S(2)}, u32[]{:S(2)}) collective-permute-start(bf16[1024,256]{1,0:T(8,128)(2,1)S(1)} %fusion.15), channel_id=1, source_target_pairs={{0,4},{1,5},{2,6},{3,7},{4,0},{5,1},{6,2},{7,3},{8,12},{9,13},{10,... | collective-permute-start | bytes 1572872 | tf_op jit(solution)/shard_map/ppermute | solution.py:30
  103.4 10.2 %copy-start.1 = (f32[1,1024,512]{2,1,0:T(8,128)S(1)}, f32[1,1024,512]{2,1,0:T(8,128)}, u32[]{:S(2)}) copy-start(f32[1,1024,512]{2,1,0:T(8,128)} %param.11) | copy-start | bytes 6291460
  103.4 10.2 %copy-start.3 = (f32[1,1024,512]{2,1,0:T(8,128)S(1)}, f32[1,1024,512]{2,1,0:T(8,128)}, u32[]{:S(2)}) copy-start(f32[1,1024,512]{2,1,0:T(8,128)} %param.12) | copy-start | bytes 6291460
  103.4 21.4 %collective-permute-start.17 = (bf16[1024,256]{1,0:T(8,128)(2,1)}, bf16[1024,256]{1,0:T(8,128)(2,1)S(1)}, u32[]{:S(2)}, u32[]{:S(2)}) collective-permute-start(bf16[1024,256]{1,0:T(8,128)(2,1)} %fusion.18), channel_id=1, source_target_pairs={{0,4},{1,5},{2,6},{3,7},{4,0},{5,1},{6,2},{7,3},{8,12},{9,13},{10,... | collective-permute-start | bytes 1572872 | tf_op jit(solution)/shard_map/ppermute | solution.py:30
  116.4 23.1 %collective-permute-start.20 = (bf16[1024,256]{1,0:T(8,128)(2,1)}, bf16[1024,256]{1,0:T(8,128)(2,1)}, u32[]{:S(2)}, u32[]{:S(2)}) collective-permute-start(bf16[1024,256]{1,0:T(8,128)(2,1)} %get-tuple-element.44), channel_id=1, source_target_pairs={{0,4},{1,5},{2,6},{3,7},{4,0},{5,1},{6,2},{7,3},{8,12},{9,13},{10,... | collective-permute-start | bytes 1572872 | tf_op jit(solution)/shard_map/ppermute | solution.py:30
  122.1 17.4 %copy-start.7 = (bf16[1024,2048]{1,0:T(8,128)(2,1)S(1)}, bf16[1024,2048]{1,0:T(8,128)(2,1)}, u32[]{:S(2)}) copy-start(bf16[1024,2048]{1,0:T(8,128)(2,1)} %copy-done.6) | copy-start | bytes 12582916
  127.5 23.7 %collective-permute-start.18 = (bf16[1024,256]{1,0:T(8,128)(2,1)S(1)}, bf16[1024,256]{1,0:T(8,128)(2,1)S(1)}, u32[]{:S(2)}, u32[]{:S(2)}) collective-permute-start(bf16[1024,256]{1,0:T(8,128)(2,1)S(1)} %fusion.38), channel_id=1, source_target_pairs={{0,4},{1,5},{2,6},{3,7},{4,0},{5,1},{6,2},{7,3},{8,12},{9,13},{10,... | collective-permute-start | bytes 1572872 | tf_op jit(solution)/shard_map/ppermute | solution.py:30
  142.0 12.5 %collective-permute-start.21 = (bf16[256,256]{1,0:T(8,128)(2,1)S(1)}, bf16[256,256]{1,0:T(8,128)(2,1)S(1)}, u32[]{:S(2)}, u32[]{:S(2)}) collective-permute-start(bf16[256,256]{1,0:T(8,128)(2,1)S(1)} %get-tuple-element.64), channel_id=1, source_target_pairs={{0,3},{1,0},{2,1},{3,2},{4,7},{5,4},{6,5},{7,6},{8,11},{9,8},{10,9... | collective-permute-start | bytes 393224 | tf_op jit(solution)/shard_map/ppermute | solution.py:30
  143.5 12.7 %collective-permute-start.22 = (bf16[256,256]{1,0:T(8,128)(2,1)S(1)}, bf16[256,256]{1,0:T(8,128)(2,1)S(1)}, u32[]{:S(2)}, u32[]{:S(2)}) collective-permute-start(bf16[256,256]{1,0:T(8,128)(2,1)S(1)} %get-tuple-element.66), channel_id=1, source_target_pairs={{0,1},{1,2},{2,3},{3,0},{4,5},{5,6},{6,7},{7,4},{8,9},{9,10},{10,1... | collective-permute-start | bytes 393224 | tf_op jit(solution)/shard_map/ppermute | solution.py:30
  145.3 10.8 %collective-permute-start.23 = (bf16[256,256]{1,0:T(8,128)(2,1)S(1)}, bf16[256,256]{1,0:T(8,128)(2,1)S(1)}, u32[]{:S(2)}, u32[]{:S(2)}) collective-permute-start(bf16[256,256]{1,0:T(8,128)(2,1)S(1)} %get-tuple-element.65), channel_id=1, source_target_pairs={{0,2},{1,3},{2,0},{3,1},{4,6},{5,7},{6,4},{7,5},{8,10},{9,11},{10,... | collective-permute-start | bytes 393224 | tf_op jit(solution)/shard_map/ppermute | solution.py:30
  152.4 6.1 %collective-permute-start.19 = (bf16[256,256]{1,0:T(8,128)(2,1)S(1)}, bf16[256,256]{1,0:T(8,128)(2,1)S(1)}, u32[]{:S(2)}, u32[]{:S(2)}) collective-permute-start(bf16[256,256]{1,0:T(8,128)(2,1)S(1)} %get-tuple-element.63), channel_id=1, source_target_pairs={{0,3},{1,0},{2,1},{3,2},{4,7},{5,4},{6,5},{7,6},{8,11},{9,8},{10,9... | collective-permute-start | bytes 393224 | tf_op jit(solution)/shard_map/ppermute | solution.py:30
  153.4 10.9 %collective-permute-start.27 = (bf16[256,256]{1,0:T(8,128)(2,1)S(1)}, bf16[256,256]{1,0:T(8,128)(2,1)S(1)}, u32[]{:S(2)}, u32[]{:S(2)}) collective-permute-start(bf16[256,256]{1,0:T(8,128)(2,1)S(1)} %get-tuple-element.61), channel_id=1, source_target_pairs={{0,1},{1,2},{2,3},{3,0},{4,5},{5,6},{6,7},{7,4},{8,9},{9,10},{10,1... | collective-permute-start | bytes 393224 | tf_op jit(solution)/shard_map/ppermute | solution.py:30
  154.5 9.8 %collective-permute-start.28 = (bf16[256,256]{1,0:T(8,128)(2,1)S(1)}, bf16[256,256]{1,0:T(8,128)(2,1)S(1)}, u32[]{:S(2)}, u32[]{:S(2)}) collective-permute-start(bf16[256,256]{1,0:T(8,128)(2,1)S(1)} %get-tuple-element.62), channel_id=1, source_target_pairs={{0,2},{1,3},{2,0},{3,1},{4,6},{5,7},{6,4},{7,5},{8,10},{9,11},{10,... | collective-permute-start | bytes 393224 | tf_op jit(solution)/shard_map/ppermute | solution.py:30
  158.6 8.8 %collective-permute-start.24 = (bf16[256,256]{1,0:T(8,128)(2,1)S(1)}, bf16[256,256]{1,0:T(8,128)(2,1)S(1)}, u32[]{:S(2)}, u32[]{:S(2)}) collective-permute-start(bf16[256,256]{1,0:T(8,128)(2,1)S(1)} %fusion.46), channel_id=1, source_target_pairs={{0,1},{1,2},{2,3},{3,0},{4,5},{5,6},{6,7},{7,4},{8,9},{9,10},{10,1... | collective-permute-start | bytes 393224 | tf_op jit(solution)/shard_map/ppermute | solution.py:30
  161.6 6.5 %collective-permute-start.25 = (bf16[256,256]{1,0:T(8,128)(2,1)S(1)}, bf16[256,256]{1,0:T(8,128)(2,1)S(1)}, u32[]{:S(2)}, u32[]{:S(2)}) collective-permute-start(bf16[256,256]{1,0:T(8,128)(2,1)S(1)} %fusion.46), channel_id=1, source_target_pairs={{0,2},{1,3},{2,0},{3,1},{4,6},{5,7},{6,4},{7,5},{8,10},{9,11},{10,... | collective-permute-start | bytes 393224 | tf_op jit(solution)/shard_map/ppermute | solution.py:30
  161.6 6.5 %collective-permute-start.26 = (bf16[256,256]{1,0:T(8,128)(2,1)S(1)}, bf16[256,256]{1,0:T(8,128)(2,1)S(1)}, u32[]{:S(2)}, u32[]{:S(2)}) collective-permute-start(bf16[256,256]{1,0:T(8,128)(2,1)S(1)} %fusion.46), channel_id=1, source_target_pairs={{0,3},{1,0},{2,1},{3,2},{4,7},{5,4},{6,5},{7,6},{8,11},{9,8},{10,9... | collective-permute-start | bytes 393224 | tf_op jit(solution)/shard_map/ppermute | solution.py:30
  164.4 9.2 %collective-permute-start.29 = (bf16[256,256]{1,0:T(8,128)(2,1)S(1)}, bf16[256,256]{1,0:T(8,128)(2,1)S(1)}, u32[]{:S(2)}, u32[]{:S(2)}) collective-permute-start(bf16[256,256]{1,0:T(8,128)(2,1)S(1)} %fusion.42), channel_id=1, source_target_pairs={{0,1},{1,2},{2,3},{3,0},{4,5},{5,6},{6,7},{7,4},{8,9},{9,10},{10,1... | collective-permute-start | bytes 393224 | tf_op jit(solution)/shard_map/ppermute | solution.py:30
  164.5 9.2 %collective-permute-start.30 = (bf16[256,256]{1,0:T(8,128)(2,1)S(1)}, bf16[256,256]{1,0:T(8,128)(2,1)S(1)}, u32[]{:S(2)}, u32[]{:S(2)}) collective-permute-start(bf16[256,256]{1,0:T(8,128)(2,1)S(1)} %fusion.42), channel_id=1, source_target_pairs={{0,2},{1,3},{2,0},{3,1},{4,6},{5,7},{6,4},{7,5},{8,10},{9,11},{10,... | collective-permute-start | bytes 393224 | tf_op jit(solution)/shard_map/ppermute | solution.py:30
  167.4 6.3 %collective-permute-start.31 = (bf16[256,256]{1,0:T(8,128)(2,1)S(1)}, bf16[256,256]{1,0:T(8,128)(2,1)S(1)}, u32[]{:S(2)}, u32[]{:S(2)}) collective-permute-start(bf16[256,256]{1,0:T(8,128)(2,1)S(1)} %fusion.42), channel_id=1, source_target_pairs={{0,3},{1,0},{2,1},{3,2},{4,7},{5,4},{6,5},{7,6},{8,11},{9,8},{10,9... | collective-permute-start | bytes 393224 | tf_op jit(solution)/shard_map/ppermute | solution.py:30
  169.7 18.3 %collective-permute-start.32 = (bf16[1024,256]{1,0:T(8,128)(2,1)}, bf16[1024,256]{1,0:T(8,128)(2,1)}, u32[]{:S(2)}, u32[]{:S(2)}) collective-permute-start(bf16[1024,256]{1,0:T(8,128)(2,1)} %fusion.21), channel_id=1, source_target_pairs={{0,4},{1,5},{2,6},{3,7},{4,0},{5,1},{6,2},{7,3},{8,12},{9,13},{10,... | collective-permute-start | bytes 1572872 | tf_op jit(solution)/shard_map/ppermute | solution.py:30
  175.3 15.0 %collective-permute-start.33 = (bf16[1024,256]{1,0:T(8,128)(2,1)}, bf16[1024,256]{1,0:T(8,128)(2,1)S(1)}, u32[]{:S(2)}, u32[]{:S(2)}) collective-permute-start(bf16[1024,256]{1,0:T(8,128)(2,1)} %fusion.24), channel_id=1, source_target_pairs={{0,4},{1,5},{2,6},{3,7},{4,0},{5,1},{6,2},{7,3},{8,12},{9,13},{10,... | collective-permute-start | bytes 1572872 | tf_op jit(solution)/shard_map/ppermute | solution.py:30
  182.1 5.9 %copy-start.2 = (f32[1,1024,512]{2,1,0:T(8,128)S(1)}, f32[1,1024,512]{2,1,0:T(8,128)}, u32[]{:S(2)}) copy-start(f32[1,1024,512]{2,1,0:T(8,128)} %param.11) | copy-start | bytes 6291460
  182.1 5.9 %copy-start.4 = (f32[1,1024,512]{2,1,0:T(8,128)S(1)}, f32[1,1024,512]{2,1,0:T(8,128)}, u32[]{:S(2)}) copy-start(f32[1,1024,512]{2,1,0:T(8,128)} %param.12) | copy-start | bytes 6291460
  182.1 5.9 %copy-start.9 = (f32[1024,256]{1,0:T(8,128)S(1)}, f32[1024,256]{1,0:T(8,128)}, u32[]{:S(2)}) copy-start(f32[1024,256]{1,0:T(8,128)} %get-tuple-element.58) | copy-start | bytes 3145732
  182.1 5.9 %copy-start.10 = (f32[1024,256]{1,0:T(8,128)S(1)}, f32[1024,256]{1,0:T(8,128)}, u32[]{:S(2)}) copy-start(f32[1024,256]{1,0:T(8,128)} %get-tuple-element.73) | copy-start | bytes 3145732
  182.1 5.9 %copy-start.12 = (f32[1024,256]{1,0:T(8,128)S(1)}, f32[1024,256]{1,0:T(8,128)}, u32[]{:S(2)}) copy-start(f32[1024,256]{1,0:T(8,128)} %fusion.10) | copy-start | bytes 3145732
  188.0 2.4 %copy-start.5 = (f32[1024,256]{1,0:T(8,128)S(1)}, f32[1024,256]{1,0:T(8,128)}, u32[]{:S(2)}) copy-start(f32[1024,256]{1,0:T(8,128)} %fusion.12) | copy-start | bytes 3145732
  (2 other events, 4.6 us)
Sparse Core Ops, SparseCore 0:
  122.2 34.4 all-gather.1

commit v4 on v3

--- a/solution.py
+++ b/solution.py
@@ -130,22 +130,26 @@
     blocks[0] = pick(inputs, 0, rows)
     both = jnp.concatenate([sent, shift(sent, 1, 0)], axis=0)
 
-    frag_rows = frag_inner.shape[1] // replicas
+    mates = replicas // 2
+    rep_groups = [list(range(mates)), list(range(mates, replicas))]
+    across = [(r, (r + mates) % replicas) for r in range(replicas)]
+    frag_rows = frag_inner.shape[1] // mates
     pieces = lax.all_to_all(
-        frag_inner[0].reshape(replicas, frag_rows, -1), "rep", 0, 0
+        frag_inner[0].reshape(mates, frag_rows, -1), "rep", 0, 0, axis_index_groups=rep_groups
     )
     blocks[1], blocks[2], blocks[3], pieces = tie(blocks[1], blocks[2], blocks[3], pieces)
-    inner_sum = lax.all_gather(jnp.sum(f32(pieces), axis=0), "rep", axis=0, tiled=True)
+    piece_sum = jnp.sum(f32(pieces), axis=0)
+    piece_sum = piece_sum + lax.ppermute(piece_sum, "rep", across)
 
     teacher = f32(targets[0])
-    (own,) = tie(dot(blocks[0], both))
-    part = {dx: dot(blocks[dx], both) for dx in (1, 2, 3)}
-    arrived_a = send_parts({dx: bf16(part[dx][:, span_a]) for dx in (1, 2, 3)})
-    resid_a = bf16(add_parts(own[:, span_a], arrived_a) - teacher[:, span_a])
-    part_b = {dx: bf16(part[dx][:, span_b]) for dx in (1, 2, 3)}
-    part_b[1], part_b[2], part_b[3], resid_a = tie(part_b[1], part_b[2], part_b[3], resid_a)
-    arrived_b = send_parts(part_b)
-    resid_b = bf16(add_parts(own[:, span_b], arrived_b) - teacher[:, span_b])
+    part = {dx: bf16(dot(blocks[dx], both)) for dx in (1, 2, 3)}
+    arrived = send_parts(part)
+    blocks[0], part[1], part[2], part[3] = tie(blocks[0], part[1], part[2], part[3])
+    own = dot(blocks[0], both)
+    own, *blocks = tie(own, *blocks)
+    outputs = add_parts(own, arrived)
+    resid_a = bf16(outputs[:, span_a] - teacher[:, span_a])
+    resid_b = bf16(outputs[:, span_b] - teacher[:, span_b])
     (held,) = tie(jnp.concatenate(blocks, axis=0))
 
     def state(span):
@@ -181,20 +185,34 @@
     *state_b, update_b = adam_update(*state(span_b), grad_b)
     sent_b = bf16(state_b[0])
     other_b = shift(sent_b, 1, 0)
-    sent_a, sent_b = tie(sent_a, sent_b)
-
-    both_a = jnp.concatenate([sent_a, other_a], axis=0)
-    part_a = dot(held, both_a).reshape(NX, tok_local, half)
-    arrived_a = send_parts({dx: bf16(part_a[dx]) for dx in (2, 1, 3)})
-    both_b = jnp.concatenate([sent_b, other_b], axis=0)
-    part_b = dot(held, both_b).reshape(NX, tok_local, half)
-    arrived_b = send_parts({dx: bf16(part_b[dx]) for dx in (2, 1, 3)})
-    resid_a = bf16(add_parts(part_a[0], arrived_a) - teacher[:, span_a])
-    arrived_b[1], resid_a = tie(arrived_b[1], resid_a)
-    resid_b = bf16(add_parts(part_b[0], arrived_b) - teacher[:, span_b])
+    sent_a, sent_b, piece_sum = tie(sent_a, sent_b, piece_sum)
+    inner_sum = lax.all_to_all(
+        jnp.broadcast_to(piece_sum[None], (mates, *piece_sum.shape)),
+        "rep",
+        0,
+        0,
+        axis_index_groups=rep_groups,
+    ).reshape(frag_outer.shape)
     delta = frag_outer - inner_sum / replicas
     frag_params, momentum_out = outer_nesterov(frag_outer, frag_momentum, delta)
-    own_a, own_b, got_a, got_b = step_one(resid_a, resid_b)
+
+    both_a = jnp.concatenate([sent_a, other_a], axis=0)
+    part_a = bf16(dot(held, both_a)).reshape(NX, tok_local, half)
+    arrived_a = send_parts({dx: part_a[dx] for dx in (2, 1, 3)})
+    both_b = jnp.concatenate([sent_b, other_b], axis=0)
+    part_b = bf16(dot(held, both_b)).reshape(NX, tok_local, half)
+    arrived_b = send_parts({dx: part_b[dx] for dx in (2, 1, 3)})
+    resid_a = bf16(add_parts(f32(part_a[0]), arrived_a) - teacher[:, span_a])
+    row_a = jnp.concatenate(gather(resid_a), axis=0)
+    away_a = away(row_a)
+    got_a = shift(away_a, 1, 0)
+    own_b, away_a = tie(part_b[0], away_a)
+    resid_b = bf16(add_parts(f32(own_b), arrived_b) - teacher[:, span_b])
+    row_b = jnp.concatenate(gather(resid_b), axis=0)
+    away_b = away(row_b)
+    got_b = shift(away_b, 1, 0)
+    row_a, row_b, away_b = tie(row_a, row_b, away_b)
+    own_a, own_b = near(row_a), near(row_b)
     own_a, own_b, frag_params, momentum_out = tie(own_a, own_b, frag_params, momentum_out)
     grad_a = (own_a + f32(got_a)) / tok_all
     total_a = update_a + adam_update(*state_a, grad_a)[3]

time: 201 us -> 193 us (0.960)
  between operations: 14.5 us -> 0.94 us
  local copies, waits for them, and re-layouts: 0.26 us -> 4.02 us
  waiting for transfers between devices: 60.4 us -> 63.8 us
    ppermute x34 -> x31, waiting for transfers between devices: 33.8 us -> 50.1 us  [shift(): return lax.ppermute(value, 'fsdp', pairs)]
    all_to_all x1 -> x2, waiting for transfers between devices: 26.5 us -> 13.8 us  [the longest x1 13.8 us: shards(): lax.all_to_all(frag_inner[0].reshape(mates, frag_rows, -1), 'rep', 0, 0,...]
    ppermute x34 -> x31, starting transfers between devices: 64.6 us -> 57.6 us  [shift(): return lax.ppermute(value, 'fsdp', pairs)]
    all_to_all x1 -> x2, starting transfers between devices: 5.08 us -> 8.94 us  [the longest x1 4.47 us: shards(): lax.all_to_all(jnp.broadcast_to(piece_sum[None], (mates, *piece_sum.shape...]
    add x1, other arithmetic: 5.85 us -> 2.95 us  [outer_nesterov(): momentum_new = 0.9 * momentum + delta]
    dot_general x6, matrix products: 13.6 us -> 16.2 us  [dot(): return jnp.dot(a, b, preferred_element_type=jnp.float32)]
    unnamed x34 -> x36, local copies, waits for them, and re-layouts: 0.12 us -> 2.37 us
    dot_general x8, matrix products: 13.5 us -> 11.4 us  [dot_t(): lax.dot_general(a, b, (((0,), (0,)), ((), ())), preferred_element_type=jn...]
  transfers between devices with their start and end apart: 36 -> 34, of which waited for: 12 -> 20; matrix products, arithmetic and copies ran while one was open for 21% -> 21% of each run, Pallas kernels for 3% -> 3%
where the time goes in v4:
time: 193 us; the launch traced here: 192 us
  starting transfers between devices  68.5 us (35%)
  waiting for transfers between devices  63.8 us (33%)
  matrix products  27.6 us (14%)
  other arithmetic  18.9 us (10%)
  Pallas kernels  8.48 us (4%)
  local copies, waits for them, and re-layouts  4.02 us (2%)
    ppermute x31, starting transfers between devices, shift(): return lax.ppermute(value, 'fsdp', pairs)  57.6 us
    ppermute x31, waiting for transfers between devices, shift(): return lax.ppermute(value, 'fsdp', pairs)  50.1 us
    dot_general x6, matrix products, dot(): return jnp.dot(a, b, preferred_element_type=jnp.float32)  16.2 us
    all_to_all x1, waiting for transfers between devices, shards(): lax.all_to_all(frag_inner[0].reshape(mates, frag_rows, -1), 'rep', 0, 0,...  13.8 us
    dot_general x8, matrix products, dot_t(): lax.dot_general(a, b, (((0,), (0,)), ((), ())), preferred_element_type=jn...  11.4 us
    pallas_call x4, Pallas kernels, pick(): pl.pallas_call(functools.partial(pick_kernel, dx), out_shape=jax.ShapeDty...  8.48 us
    all_to_all x1, starting transfers between devices, shards(): lax.all_to_all(jnp.broadcast_to(piece_sum[None], (mates, *piece_sum.shape...  4.47 us
    all_to_all x1, starting transfers between devices, shards(): lax.all_to_all(frag_inner[0].reshape(mates, frag_rows, -1), 'rep', 0, 0,...  4.47 us
  transfers between devices with their start and end apart: 34, of which 20 were waited for; matrix products, arithmetic and copies ran while one was open for 21% of the time, Pallas kernels for 3%

profile of v4, /device:TPU:0, one launch (start us, length us, event | category | flops | bytes accessed | tf_op | source)
XLA Modules:
  0.0 192.3 jit_solution(3054104556358343751)
XLA Ops:
  0.6 2.1 %shard_map.104 = bf16[256,2048]{1,0:T(8,128)(2,1)} custom-call(bf16[256,8192]{1,0:T(8,128)(2,1)} %bitcast.77), custom_call_target="tpu_custom_call" | custom-call | bytes 2097152 | tf_op jit(solution)/shard_map/pallas_call | solution.py:86
  4.4 2.1 %shard_map.105 = bf16[256,2048]{1,0:T(8,128)(2,1)} custom-call(bf16[256,8192]{1,0:T(8,128)(2,1)} %bitcast.78), custom_call_target="tpu_custom_call" | custom-call | bytes 2097152 | tf_op jit(solution)/shard_map/pallas_call | solution.py:86
  6.5 2.8 %collective-permute-start.1 = (bf16[256,2048]{1,0:T(8,128)(2,1)}, bf16[256,2048]{1,0:T(8,128)(2,1)}, u32[]{:S(2)}, u32[]{:S(2)}) collective-permute-start(bf16[256,2048]{1,0:T(8,128)(2,1)} %shard_map.105), channel_id=1, source_target_pairs={{0,2},{1,3},{2,0},{3,1},{4,6},{5,7},{6,4},{7,5},{8,10},{9,11},{10,... | collective-permute-start | bytes 3145736 | tf_op jit(solution)/shard_map/ppermute | solution.py:30
  9.3 2.1 %shard_map.106 = bf16[256,2048]{1,0:T(8,128)(2,1)} custom-call(bf16[256,8192]{1,0:T(8,128)(2,1)} %bitcast.79), custom_call_target="tpu_custom_call" | custom-call | bytes 2097152 | tf_op jit(solution)/shard_map/pallas_call | solution.py:86
  14.0 3.9 %collective-permute-start.3 = (bf16[1024,512]{1,0:T(8,128)(2,1)}, bf16[1024,512]{1,0:T(8,128)(2,1)}, u32[]{:S(2)}, u32[]{:S(2)}) collective-permute-start(bf16[1024,512]{1,0:T(8,128)(2,1)} %convert_element_type.102), channel_id=1, source_target_pairs={{0,4},{1,5},{2,6},{3,7},{4,0},{5,1},{6,2},{7,3},{8,12},{9,13},{10,... | collective-permute-start | bytes 3145736 | tf_op jit(solution)/shard_map/ppermute | solution.py:30
  17.9 4.5 %all-to-all-start = ((bf16[8,128,512]{2,1,0:T(8,128)(2,1)}), bf16[8,128,512]{2,1,0:T(8,128)(2,1)}, u32[]{:S(2)}, u32[]{:S(2)}) async-start(bf16[8,128,512]{2,1,0:T(8,128)(2,1)} %bitcast.2), calls=%async_computation | async-start | bytes 2097152 | tf_op jit(solution)/shard_map/all_to_all | solution.py:137
  22.4 2.2 %shard_map.103 = bf16[256,2048]{1,0:T(8,128)(2,1)} custom-call(bf16[256,8192]{1,0:T(8,128)(2,1)} %bitcast.80), custom_call_target="tpu_custom_call" | custom-call | bytes 2097152 | tf_op jit(solution)/shard_map/pallas_call | solution.py:86
  24.7 13.8 %all-to-all-done = bf16[8,128,512]{2,1,0:T(8,128)(2,1)} async-done(((bf16[8,128,512]{2,1,0:T(8,128)(2,1)}), bf16[8,128,512]{2,1,0:T(8,128)(2,1)}, u32[]{:S(2)}, u32[]{:S(2)}) %all-to-all-start) | async-done | bytes 1048608 | tf_op jit(solution)/shard_map/all_to_all | solution.py:137
  38.4 14.3 %collective-permute-done.1 = bf16[256,2048]{1,0:T(8,128)(2,1)} collective-permute-done((bf16[256,2048]{1,0:T(8,128)(2,1)}, bf16[256,2048]{1,0:T(8,128)(2,1)}, u32[]{:S(2)}, u32[]{:S(2)}) %collective-permute-start.1) | collective-permute-done | bytes 1048608 | tf_op jit(solution)/shard_map/ppermute | solution.py:30
  52.8 1.7 collective-permute-done.2
  54.4 2.6 %convolution_convert_fusion.2 = bf16[256,512]{1,0:T(8,128)(2,1)S(1)} fusion(bf16[256,2048]{1,0:T(8,128)(2,1)} %collective-permute-done.2, bf16[1024,512]{1,0:T(8,128)(2,1)} %collective-permute-done.3, bf16[1024,512]{1,0:T(8,128)(2,1)} %convert_element_type.102), kind=kOutput, calls=%fused_computation.29 | convolution fusion | flops 541196288 | bytes 3407872 | tf_op jit(solution)/shard_map/dot_general | solution.py:42
  57.0 2.6 %collective-permute-start.5 = (bf16[256,512]{1,0:T(8,128)(2,1)S(1)}, bf16[256,512]{1,0:T(8,128)(2,1)S(1)}, u32[]{:S(2)}, u32[]{:S(2)}) collective-permute-start(bf16[256,512]{1,0:T(8,128)(2,1)S(1)} %convolution_convert_fusion.2), channel_id=1, source_target_pairs={{0,1},{1,2},{2,3},{3,0},{4,5},{5,6},{6,7},{7,4},{8,9},{9,10},{10,1... | collective-permute-start | bytes 786440 | tf_op jit(solution)/shard_map/ppermute | solution.py:30
  59.6 2.6 %convolution_convert_fusion.3 = bf16[256,512]{1,0:T(8,128)(2,1)S(1)} fusion(bf16[256,2048]{1,0:T(8,128)(2,1)} %collective-permute-done.1, bf16[1024,512]{1,0:T(8,128)(2,1)} %collective-permute-done.3, bf16[1024,512]{1,0:T(8,128)(2,1)} %convert_element_type.102), kind=kOutput, calls=%fused_computation.30 | convolution fusion | flops 541196288 | bytes 3407872 | tf_op jit(solution)/shard_map/dot_general | solution.py:42
  63.8 2.6 %convolution_convert_fusion.4 = bf16[256,512]{1,0:T(8,128)(2,1)S(1)} fusion(bf16[256,2048]{1,0:T(8,128)(2,1)} %collective-permute-done, bf16[1024,512]{1,0:T(8,128)(2,1)} %collective-permute-done.3, bf16[1024,512]{1,0:T(8,128)(2,1)} %convert_element_type.102), kind=kOutput, calls=%fused_computation.31 | convolution fusion | flops 541196288 | bytes 3407872 | tf_op jit(solution)/shard_map/dot_general | solution.py:42
  66.4 1.8 collective-permute-start.4
  68.2 2.2 %fusion.42 = f32[256,512]{1,0:T(8,128)S(1)} fusion(bf16[256,2048]{1,0:T(8,128)(2,1)S(1)} %copy-done.9, bf16[1024,512]{1,0:T(8,128)(2,1)} %collective-permute-done.3, bf16[1024,512]{1,0:T(8,128)(2,1)} %convert_element_type.102), kind=kOutput, calls=%fused_computation.69 | convolution fusion | flops 541065216 | bytes 3670016 | tf_op jit(solution)/shard_map/dot_general | solution.py:42
  70.4 2.1 %pad_maximum_fusion = bf16[1024,2048]{1,0:T(8,128)(2,1)S(1)} fusion(bf16[256,2048]{1,0:T(8,128)(2,1)} %collective-permute-done.2, bf16[256,2048]{1,0:T(8,128)(2,1)} %collective-permute-done.1, bf16[256,2048]{1,0:T(8,128)(2,1)} %collective-permute-done, bf16[256,2048]{1,0:T(8,128)(2,1)S(1)} %copy-done.9), kind=kLoop, calls=%fused_computation | loop fusion | flops 16777216 | bytes 8388608 | tf_op jit(solution)/shard_map/concatenate | solution.py:153
  73.0 2.1 %collective-permute-done.4 = bf16[256,512]{1,0:T(8,128)(2,1)S(1)} collective-permute-done((bf16[256,512]{1,0:T(8,128)(2,1)S(1)}, bf16[256,512]{1,0:T(8,128)(2,1)S(1)}, u32[]{:S(2)}, u32[]{:S(2)}) %collective-permute-start.4) | collective-permute-done | bytes 262176 | tf_op jit(solution)/shard_map/ppermute | solution.py:30
  75.3 2.7 %collective-permute-start.9 = (bf16[256,256]{1,0:T(8,128)(2,1)S(1)}, bf16[256,256]{1,0:T(8,128)(2,1)S(1)}, u32[]{:S(2)}, u32[]{:S(2)}) collective-permute-start(bf16[256,256]{1,0:T(8,128)(2,1)S(1)} %get-tuple-element.62), channel_id=1, source_target_pairs={{0,3},{1,0},{2,1},{3,2},{4,7},{5,4},{6,5},{7,6},{8,11},{9,8},{10,9... | collective-permute-start | bytes 393224 | tf_op jit(solution)/shard_map/ppermute | solution.py:30
  78.0 2.0 %collective-permute-start.8 = (bf16[256,256]{1,0:T(8,128)(2,1)S(1)}, bf16[256,256]{1,0:T(8,128)(2,1)S(1)}, u32[]{:S(2)}, u32[]{:S(2)}) collective-permute-start(bf16[256,256]{1,0:T(8,128)(2,1)S(1)} %get-tuple-element.62), channel_id=1, source_target_pairs={{0,2},{1,3},{2,0},{3,1},{4,6},{5,7},{6,4},{7,5},{8,10},{9,11},{10,... | collective-permute-start | bytes 393224 | tf_op jit(solution)/shard_map/ppermute | solution.py:30
  81.4 2.0 %collective-permute-start.15 = (f32[128,512]{1,0:T(8,128)S(1)}, f32[128,512]{1,0:T(8,128)S(1)}, u32[]{:S(2)}, u32[]{:S(2)}) collective-permute-start(f32[128,512]{1,0:T(8,128)S(1)} %convert_reduce_fusion), channel_id=1, source_target_pairs={{0,64},{8,72},{16,80},{24,88},{32,96},{40,104},{48,112},{56,120},{... | collective-permute-start | bytes 786440 | tf_op jit(solution)/shard_map/ppermute | solution.py:142
  83.4 3.2 %collective-permute-start.12 = (bf16[256,256]{1,0:T(8,128)(2,1)S(1)}, bf16[256,256]{1,0:T(8,128)(2,1)S(1)}, u32[]{:S(2)}, u32[]{:S(2)}) collective-permute-start(bf16[256,256]{1,0:T(8,128)(2,1)S(1)} %get-tuple-element.61), channel_id=1, source_target_pairs={{0,3},{1,0},{2,1},{3,2},{4,7},{5,4},{6,5},{7,6},{8,11},{9,8},{10,9... | collective-permute-start | bytes 393224 | tf_op jit(solution)/shard_map/ppermute | solution.py:30
  88.3 3.9 %collective-permute-start.13 = (bf16[1024,256]{1,0:T(8,128)(2,1)S(1)}, bf16[1024,256]{1,0:T(8,128)(2,1)S(1)}, u32[]{:S(2)}, u32[]{:S(2)}) collective-permute-start(bf16[1024,256]{1,0:T(8,128)(2,1)S(1)} %fusion.16), channel_id=1, source_target_pairs={{0,4},{1,5},{2,6},{3,7},{4,0},{5,1},{6,2},{7,3},{8,12},{9,13},{10,... | collective-permute-start | bytes 1572872 | tf_op jit(solution)/shard_map/ppermute | solution.py:30
  95.5 3.8 %collective-permute-start.14 = (bf16[1024,256]{1,0:T(8,128)(2,1)S(1)}, bf16[1024,256]{1,0:T(8,128)(2,1)S(1)}, u32[]{:S(2)}, u32[]{:S(2)}) collective-permute-start(bf16[1024,256]{1,0:T(8,128)(2,1)S(1)} %fusion.19), channel_id=1, source_target_pairs={{0,4},{1,5},{2,6},{3,7},{4,0},{5,1},{6,2},{7,3},{8,12},{9,13},{10,... | collective-permute-start | bytes 1572872 | tf_op jit(solution)/shard_map/ppermute | solution.py:30
  100.2 4.8 %collective-permute-done.13 = bf16[1024,256]{1,0:T(8,128)(2,1)S(1)} collective-permute-done((bf16[1024,256]{1,0:T(8,128)(2,1)S(1)}, bf16[1024,256]{1,0:T(8,128)(2,1)S(1)}, u32[]{:S(2)}, u32[]{:S(2)}) %collective-permute-start.13) | collective-permute-done | bytes 524320 | tf_op jit(solution)/shard_map/ppermute | solution.py:30
  105.0 2.5 %fusion.36 = (bf16[1024,256]{1,0:T(8,128)(2,1)}, f32[1024,256]{1,0:T(8,128)}) fusion(f32[1,1024,512]{2,1,0:T(8,128)S(1)} %copy-done, bf16[1024,256]{1,0:T(8,128)(2,1)S(1)} %collective-permute-done.13, f32[1,1024,512]{2,1,0:T(8,128)S(1)} %copy-done.1, f32[1,1024,512]{2,1,0:T(8,128)S(1)} %copy-done.3, bf16[1024,256]{1,0:T(8,128)(2,1)S(1)} %pad_maximum_fusion.2, ...), kind=kOutput, calls=%fused_computation.53 | convolution fusion | flops 541327360 | bytes 7864320 | tf_op jit(solution)/shard_map/dot_general | solution.py:50
  107.6 3.5 %collective-permute-start.16 = (bf16[1024,256]{1,0:T(8,128)(2,1)}, bf16[1024,256]{1,0:T(8,128)(2,1)}, u32[]{:S(2)}, u32[]{:S(2)}) collective-permute-start(bf16[1024,256]{1,0:T(8,128)(2,1)} %get-tuple-element.47), channel_id=1, source_target_pairs={{0,4},{1,5},{2,6},{3,7},{4,0},{5,1},{6,2},{7,3},{8,12},{9,13},{10,... | collective-permute-start | bytes 1572872 | tf_op jit(solution)/shard_map/ppermute | solution.py:30
  111.1 5.1 %collective-permute-done.14 = bf16[1024,256]{1,0:T(8,128)(2,1)S(1)} collective-permute-done((bf16[1024,256]{1,0:T(8,128)(2,1)S(1)}, bf16[1024,256]{1,0:T(8,128)(2,1)S(1)}, u32[]{:S(2)}, u32[]{:S(2)}) %collective-permute-start.14) | collective-permute-done | bytes 524320 | tf_op jit(solution)/shard_map/ppermute | solution.py:30
  117.9 3.5 %collective-permute-start.23 = (bf16[1024,256]{1,0:T(8,128)(2,1)}, bf16[1024,256]{1,0:T(8,128)(2,1)}, u32[]{:S(2)}, u32[]{:S(2)}) collective-permute-start(bf16[1024,256]{1,0:T(8,128)(2,1)} %fusion.37), channel_id=1, source_target_pairs={{0,4},{1,5},{2,6},{3,7},{4,0},{5,1},{6,2},{7,3},{8,12},{9,13},{10,... | collective-permute-start | bytes 1572872 | tf_op jit(solution)/shard_map/ppermute | solution.py:30
  123.0 4.5 %all-to-all-start.1 = ((f32[8,128,512]{2,1,0:T(8,128)}), f32[8,128,512]{2,1,0:T(8,128)}, u32[]{:S(2)}, u32[]{:S(2)}) async-start(f32[8,128,512]{2,1,0:T(8,128)} %broadcast_in_dim.4), calls=%async_computation.1 | async-start | bytes 4194304 | tf_op jit(solution)/shard_map/all_to_all | solution.py:189
  127.6 3.9 %convolution_convert_fusion.1 = bf16[1024,256]{1,0:T(8,128)(2,1)S(1)} fusion(bf16[1024,2048]{1,0:T(8,128)(2,1)} %copy-done.7, bf16[1024,256]{1,0:T(8,128)(2,1)} %collective-permute-done.16, bf16[1024,256]{1,0:T(8,128)(2,1)} %get-tuple-element.47), kind=kOutput, calls=%fused_computation.28 | convolution fusion | flops 1076101120 | bytes 5767168 | tf_op jit(solution)/shard_map/dot_general | solution.py:42
  131.5 3.7 %collective-permute-start.17 = (bf16[256,256]{1,0:T(8,128)(2,1)S(1)}, bf16[256,256]{1,0:T(8,128)(2,1)S(1)}, u32[]{:S(2)}, u32[]{:S(2)}) collective-permute-start(bf16[256,256]{1,0:T(8,128)(2,1)S(1)} %get-tuple-element.67), channel_id=1, source_target_pairs={{0,3},{1,0},{2,1},{3,2},{4,7},{5,4},{6,5},{7,6},{8,11},{9,8},{10,9... | collective-permute-start | bytes 393224 | tf_op jit(solution)/shard_map/ppermute | solution.py:30
  137.7 2.5 %convolution_convert_fusion = bf16[1024,256]{1,0:T(8,128)(2,1)S(1)} fusion(bf16[1024,2048]{1,0:T(8,128)(2,1)S(1)} %copy-done.8, bf16[1024,256]{1,0:T(8,128)(2,1)} %collective-permute-done.23, bf16[1024,256]{1,0:T(8,128)(2,1)} %fusion.37), kind=kOutput, calls=%fused_computation.27 | convolution fusion | flops 1076101120 | bytes 5767168 | tf_op jit(solution)/shard_map/dot_general | solution.py:42
  140.5 2.2 %collective-permute-done.19 = bf16[256,256]{1,0:T(8,128)(2,1)S(1)} collective-permute-done((bf16[256,256]{1,0:T(8,128)(2,1)S(1)}, bf16[256,256]{1,0:T(8,128)(2,1)S(1)}, u32[]{:S(2)}, u32[]{:S(2)}) %collective-permute-start.19) | collective-permute-done | bytes 131104 | tf_op jit(solution)/shard_map/ppermute | solution.py:30
  144.8 1.9 collective-permute-start.21
  147.4 3.1 %collective-permute-start.26 = (bf16[256,256]{1,0:T(8,128)(2,1)S(1)}, bf16[256,256]{1,0:T(8,128)(2,1)S(1)}, u32[]{:S(2)}, u32[]{:S(2)}) collective-permute-start(bf16[256,256]{1,0:T(8,128)(2,1)S(1)} %get-tuple-element.64), channel_id=1, source_target_pairs={{0,2},{1,3},{2,0},{3,1},{4,6},{5,7},{6,4},{7,5},{8,10},{9,11},{10,... | collective-permute-start | bytes 393224 | tf_op jit(solution)/shard_map/ppermute | solution.py:30
  150.9 2.9 %collective-permute-start.24 = (bf16[256,256]{1,0:T(8,128)(2,1)S(1)}, bf16[256,256]{1,0:T(8,128)(2,1)S(1)}, u32[]{:S(2)}, u32[]{:S(2)}) collective-permute-start(bf16[256,256]{1,0:T(8,128)(2,1)S(1)} %get-tuple-element.66), channel_id=1, source_target_pairs={{0,3},{1,0},{2,1},{3,2},{4,7},{5,4},{6,5},{7,6},{8,11},{9,8},{10,9... | collective-permute-start | bytes 393224 | tf_op jit(solution)/shard_map/ppermute | solution.py:30
  153.7 3.4 %collective-permute-done.20 = bf16[256,256]{1,0:T(8,128)(2,1)S(1)} collective-permute-done((bf16[256,256]{1,0:T(8,128)(2,1)S(1)}, bf16[256,256]{1,0:T(8,128)(2,1)S(1)}, u32[]{:S(2)}, u32[]{:S(2)}) %collective-permute-start.20) | collective-permute-done | bytes 131104 | tf_op jit(solution)/shard_map/ppermute | solution.py:30
  160.4 1.8 collective-permute-start.28
  162.9 2.5 %collective-permute-done.29 = bf16[256,256]{1,0:T(8,128)(2,1)S(1)} collective-permute-done((bf16[256,256]{1,0:T(8,128)(2,1)S(1)}, bf16[256,256]{1,0:T(8,128)(2,1)S(1)}, u32[]{:S(2)}, u32[]{:S(2)}) %collective-permute-start.29) | collective-permute-done | bytes 131104 | tf_op jit(solution)/shard_map/ppermute | solution.py:30
  165.4 2.2 %collective-permute-done.28 = bf16[256,256]{1,0:T(8,128)(2,1)S(1)} collective-permute-done((bf16[256,256]{1,0:T(8,128)(2,1)S(1)}, bf16[256,256]{1,0:T(8,128)(2,1)S(1)}, u32[]{:S(2)}, u32[]{:S(2)}) %collective-permute-start.28) | collective-permute-done | bytes 131104 | tf_op jit(solution)/shard_map/ppermute | solution.py:30
  171.1 1.8 fusion.10
  172.8 1.7 fusion.8
  174.6 2.0 %broadcast_multiply_fusion = f32[8,128,512]{2,1,0:T(8,128)S(1)} fusion(f32[8,128,512]{2,1,0:T(8,128)} %all-to-all-done.1), kind=kLoop, calls=%fused_computation.50 | loop fusion | flops 524288 | bytes 4194304 | tf_op jit(solution)/shard_map/div | solution.py:196
  177.4 2.9 %multiply_add_fusion = (f32[1024,512]{1,0:T(8,128)}, f32[1024,512]{1,0:T(8,128)}) fusion(f32[1024,512]{1,0:T(8,128)S(1)} %copy-done.10, f32[1024,512]{1,0:T(8,128)S(1)} %copy-done.11, f32[8,128,512]{2,1,0:T(8,128)S(1)} %broadcast_multiply_fusion), kind=kLoop, calls=%fused_computation.5 | loop fusion | flops 3670016 | bytes 10485760 | tf_op jit(solution)/shard_map/add | solution.py:22
  181.8 2.8 %add_add_fusion.1 = f32[1024,256]{1,0:T(8,128)S(1)} fusion(f32[1024,256]{1,0:T(8,128)S(1)} %copy-done.14, bf16[1024,256]{1,0:T(8,128)(2,1)} %collective-permute-done.30, f32[1,1024,512]{2,1,0:T(8,128)S(1)} %copy-done, f32[1024,256]{1,0:T(8,128)S(1)} %copy-done.12, bf16[1024,256]{1,0:T(8,128)(2,1)S(1)} %copy-done.16, f32[1,1024,512]{2,1,0:T(8,128)S(1)} %copy-done.2, ...), kind=kLoop, calls=%fused_computation.49 | loop fusion | flops 8126464 | bytes 7340032 | tf_op jit(solution)/shard_map/add | solution.py:218
  184.6 3.4 %collective-permute-done.31 = bf16[1024,256]{1,0:T(8,128)(2,1)} collective-permute-done((bf16[1024,256]{1,0:T(8,128)(2,1)}, bf16[1024,256]{1,0:T(8,128)(2,1)}, u32[]{:S(2)}, u32[]{:S(2)}) %collective-permute-start.31) | collective-permute-done | bytes 524320 | tf_op jit(solution)/shard_map/ppermute | solution.py:30
  188.0 2.7 %add_add_fusion = f32[1024,256]{1,0:T(8,128)S(1)} fusion(f32[1024,256]{1,0:T(8,128)S(1)} %copy-done.13, bf16[1024,256]{1,0:T(8,128)(2,1)} %collective-permute-done.31, f32[1,1024,512]{2,1,0:T(8,128)S(1)} %copy-done, f32[1024,256]{1,0:T(8,128)S(1)} %copy-done.6, bf16[1024,256]{1,0:T(8,128)(2,1)S(1)} %collective-permute-done.14, ...), kind=kLoop, calls=%fused_computation.48 | loop fusion | flops 8126464 | bytes 7340032 | tf_op jit(solution)/shard_map/add | solution.py:221
  (96 shorter events, 34.5 us)
Async XLA Ops:
  2.7 35.7 %collective-permute-start = (bf16[256,2048]{1,0:T(8,128)(2,1)}, bf16[256,2048]{1,0:T(8,128)(2,1)}, u32[]{:S(2)}, u32[]{:S(2)}) collective-permute-start(bf16[256,2048]{1,0:T(8,128)(2,1)} %shard_map.104), channel_id=1, source_target_pairs={{0,1},{1,2},{2,3},{3,0},{4,5},{5,6},{6,7},{7,4},{8,9},{9,10},{10,1... | collective-permute-start | bytes 3145736 | tf_op jit(solution)/shard_map/ppermute | solution.py:30
  6.5 6.4 %copy-start = (f32[1,1024,512]{2,1,0:T(8,128)S(1)}, f32[1,1024,512]{2,1,0:T(8,128)}, u32[]{:S(2)}) copy-start(f32[1,1024,512]{2,1,0:T(8,128)} %param.10) | copy-start | bytes 6291460
  6.5 46.3 %collective-permute-start.1 = (bf16[256,2048]{1,0:T(8,128)(2,1)}, bf16[256,2048]{1,0:T(8,128)(2,1)}, u32[]{:S(2)}, u32[]{:S(2)}) collective-permute-start(bf16[256,2048]{1,0:T(8,128)(2,1)} %shard_map.105), channel_id=1, source_target_pairs={{0,2},{1,3},{2,0},{3,1},{4,6},{5,7},{6,4},{7,5},{8,10},{9,11},{10,... | collective-permute-start | bytes 3145736 | tf_op jit(solution)/shard_map/ppermute | solution.py:30
  11.4 43.0 %collective-permute-start.2 = (bf16[256,2048]{1,0:T(8,128)(2,1)}, bf16[256,2048]{1,0:T(8,128)(2,1)}, u32[]{:S(2)}, u32[]{:S(2)}) collective-permute-start(bf16[256,2048]{1,0:T(8,128)(2,1)} %shard_map.106), channel_id=1, source_target_pairs={{0,3},{1,0},{2,1},{3,2},{4,7},{5,4},{6,5},{7,6},{8,11},{9,8},{10,9... | collective-permute-start | bytes 3145736 | tf_op jit(solution)/shard_map/ppermute | solution.py:30
  14.0 40.4 %collective-permute-start.3 = (bf16[1024,512]{1,0:T(8,128)(2,1)}, bf16[1024,512]{1,0:T(8,128)(2,1)}, u32[]{:S(2)}, u32[]{:S(2)}) collective-permute-start(bf16[1024,512]{1,0:T(8,128)(2,1)} %convert_element_type.102), channel_id=1, source_target_pairs={{0,4},{1,5},{2,6},{3,7},{4,0},{5,1},{6,2},{7,3},{8,12},{9,13},{10,... | collective-permute-start | bytes 3145736 | tf_op jit(solution)/shard_map/ppermute | solution.py:30
  17.9 20.5 %all-to-all-start = ((bf16[8,128,512]{2,1,0:T(8,128)(2,1)}), bf16[8,128,512]{2,1,0:T(8,128)(2,1)}, u32[]{:S(2)}, u32[]{:S(2)}) async-start(bf16[8,128,512]{2,1,0:T(8,128)(2,1)} %bitcast.2), calls=%async_computation | async-start | bytes 2097152 | tf_op jit(solution)/shard_map/all_to_all | solution.py:137
  57.0 15.6 %collective-permute-start.5 = (bf16[256,512]{1,0:T(8,128)(2,1)S(1)}, bf16[256,512]{1,0:T(8,128)(2,1)S(1)}, u32[]{:S(2)}, u32[]{:S(2)}) collective-permute-start(bf16[256,512]{1,0:T(8,128)(2,1)S(1)} %convolution_convert_fusion.2), channel_id=1, source_target_pairs={{0,1},{1,2},{2,3},{3,0},{4,5},{5,6},{6,7},{7,4},{8,9},{9,10},{10,1... | collective-permute-start | bytes 786440 | tf_op jit(solution)/shard_map/ppermute | solution.py:30
  62.2 6.0 %copy-start.9 = (bf16[256,2048]{1,0:T(8,128)(2,1)S(1)}, bf16[256,2048]{1,0:T(8,128)(2,1)}, u32[]{:S(2)}) copy-start(bf16[256,2048]{1,0:T(8,128)(2,1)} %shard_map.103) | copy-start | bytes 3145732
  62.2 10.8 %collective-permute-start.6 = (bf16[256,512]{1,0:T(8,128)(2,1)S(1)}, bf16[256,512]{1,0:T(8,128)(2,1)S(1)}, u32[]{:S(2)}, u32[]{:S(2)}) collective-permute-start(bf16[256,512]{1,0:T(8,128)(2,1)S(1)} %convolution_convert_fusion.3), channel_id=1, source_target_pairs={{0,2},{1,3},{2,0},{3,1},{4,6},{5,7},{6,4},{7,5},{8,10},{9,11},{10,... | collective-permute-start | bytes 786440 | tf_op jit(solution)/shard_map/ppermute | solution.py:30
  66.4 8.7 %collective-permute-start.4 = (bf16[256,512]{1,0:T(8,128)(2,1)S(1)}, bf16[256,512]{1,0:T(8,128)(2,1)S(1)}, u32[]{:S(2)}, u32[]{:S(2)}) collective-permute-start(bf16[256,512]{1,0:T(8,128)(2,1)S(1)} %convolution_convert_fusion.4), channel_id=1, source_target_pairs={{0,3},{1,0},{2,1},{3,2},{4,7},{5,4},{6,5},{7,6},{8,11},{9,8},{10,9... | collective-permute-start | bytes 786440 | tf_op jit(solution)/shard_map/ppermute | solution.py:30
  72.6 32.5 %copy-start.7 = (bf16[1024,2048]{1,0:T(8,128)(2,1)}, bf16[1024,2048]{1,0:T(8,128)(2,1)S(1)}, u32[]{:S(2)}) copy-start(bf16[1024,2048]{1,0:T(8,128)(2,1)S(1)} %pad_maximum_fusion) | copy-start | bytes 12582916
  75.3 11.3 %collective-permute-start.9 = (bf16[256,256]{1,0:T(8,128)(2,1)S(1)}, bf16[256,256]{1,0:T(8,128)(2,1)S(1)}, u32[]{:S(2)}, u32[]{:S(2)}) collective-permute-start(bf16[256,256]{1,0:T(8,128)(2,1)S(1)} %get-tuple-element.62), channel_id=1, source_target_pairs={{0,3},{1,0},{2,1},{3,2},{4,7},{5,4},{6,5},{7,6},{8,11},{9,8},{10,9... | collective-permute-start | bytes 393224 | tf_op jit(solution)/shard_map/ppermute | solution.py:30
  78.0 9.1 %collective-permute-start.8 = (bf16[256,256]{1,0:T(8,128)(2,1)S(1)}, bf16[256,256]{1,0:T(8,128)(2,1)S(1)}, u32[]{:S(2)}, u32[]{:S(2)}) collective-permute-start(bf16[256,256]{1,0:T(8,128)(2,1)S(1)} %get-tuple-element.62), channel_id=1, source_target_pairs={{0,2},{1,3},{2,0},{3,1},{4,6},{5,7},{6,4},{7,5},{8,10},{9,11},{10,... | collective-permute-start | bytes 393224 | tf_op jit(solution)/shard_map/ppermute | solution.py:30
  80.0 7.5 %collective-permute-start.7 = (bf16[256,256]{1,0:T(8,128)(2,1)S(1)}, bf16[256,256]{1,0:T(8,128)(2,1)S(1)}, u32[]{:S(2)}, u32[]{:S(2)}) collective-permute-start(bf16[256,256]{1,0:T(8,128)(2,1)S(1)} %get-tuple-element.62), channel_id=1, source_target_pairs={{0,1},{1,2},{2,3},{3,0},{4,5},{5,6},{6,7},{7,4},{8,9},{9,10},{10,1... | collective-permute-start | bytes 393224 | tf_op jit(solution)/shard_map/ppermute | solution.py:30
  81.4 29.7 %collective-permute-start.15 = (f32[128,512]{1,0:T(8,128)S(1)}, f32[128,512]{1,0:T(8,128)S(1)}, u32[]{:S(2)}, u32[]{:S(2)}) collective-permute-start(f32[128,512]{1,0:T(8,128)S(1)} %convert_reduce_fusion), channel_id=1, source_target_pairs={{0,64},{8,72},{16,80},{24,88},{32,96},{40,104},{48,112},{56,120},{... | collective-permute-start | bytes 786440 | tf_op jit(solution)/shard_map/ppermute | solution.py:142
  83.4 8.8 %collective-permute-start.12 = (bf16[256,256]{1,0:T(8,128)(2,1)S(1)}, bf16[256,256]{1,0:T(8,128)(2,1)S(1)}, u32[]{:S(2)}, u32[]{:S(2)}) collective-permute-start(bf16[256,256]{1,0:T(8,128)(2,1)S(1)} %get-tuple-element.61), channel_id=1, source_target_pairs={{0,3},{1,0},{2,1},{3,2},{4,7},{5,4},{6,5},{7,6},{8,11},{9,8},{10,9... | collective-permute-start | bytes 393224 | tf_op jit(solution)/shard_map/ppermute | solution.py:30
  86.6 7.0 %collective-permute-start.11 = (bf16[256,256]{1,0:T(8,128)(2,1)S(1)}, bf16[256,256]{1,0:T(8,128)(2,1)S(1)}, u32[]{:S(2)}, u32[]{:S(2)}) collective-permute-start(bf16[256,256]{1,0:T(8,128)(2,1)S(1)} %get-tuple-element.61), channel_id=1, source_target_pairs={{0,2},{1,3},{2,0},{3,1},{4,6},{5,7},{6,4},{7,5},{8,10},{9,11},{10,... | collective-permute-start | bytes 393224 | tf_op jit(solution)/shard_map/ppermute | solution.py:30
  87.1 7.6 %collective-permute-start.10 = (bf16[256,256]{1,0:T(8,128)(2,1)S(1)}, bf16[256,256]{1,0:T(8,128)(2,1)S(1)}, u32[]{:S(2)}, u32[]{:S(2)}) collective-permute-start(bf16[256,256]{1,0:T(8,128)(2,1)S(1)} %get-tuple-element.61), channel_id=1, source_target_pairs={{0,1},{1,2},{2,3},{3,0},{4,5},{5,6},{6,7},{7,4},{8,9},{9,10},{10,1... | collective-permute-start | bytes 393224 | tf_op jit(solution)/shard_map/ppermute | solution.py:30
  88.3 16.8 %collective-permute-start.13 = (bf16[1024,256]{1,0:T(8,128)(2,1)S(1)}, bf16[1024,256]{1,0:T(8,128)(2,1)S(1)}, u32[]{:S(2)}, u32[]{:S(2)}) collective-permute-start(bf16[1024,256]{1,0:T(8,128)(2,1)S(1)} %fusion.16), channel_id=1, source_target_pairs={{0,4},{1,5},{2,6},{3,7},{4,0},{5,1},{6,2},{7,3},{8,12},{9,13},{10,... | collective-permute-start | bytes 1572872 | tf_op jit(solution)/shard_map/ppermute | solution.py:30
  95.5 20.7 %collective-permute-start.14 = (bf16[1024,256]{1,0:T(8,128)(2,1)S(1)}, bf16[1024,256]{1,0:T(8,128)(2,1)S(1)}, u32[]{:S(2)}, u32[]{:S(2)}) collective-permute-start(bf16[1024,256]{1,0:T(8,128)(2,1)S(1)} %fusion.19), channel_id=1, source_target_pairs={{0,4},{1,5},{2,6},{3,7},{4,0},{5,1},{6,2},{7,3},{8,12},{9,13},{10,... | collective-permute-start | bytes 1572872 | tf_op jit(solution)/shard_map/ppermute | solution.py:30
  99.4 5.6 %copy-start.1 = (f32[1,1024,512]{2,1,0:T(8,128)S(1)}, f32[1,1024,512]{2,1,0:T(8,128)}, u32[]{:S(2)}) copy-start(f32[1,1024,512]{2,1,0:T(8,128)} %param.11) | copy-start | bytes 6291460
  99.4 5.6 %copy-start.3 = (f32[1,1024,512]{2,1,0:T(8,128)S(1)}, f32[1,1024,512]{2,1,0:T(8,128)}, u32[]{:S(2)}) copy-start(f32[1,1024,512]{2,1,0:T(8,128)} %param.12) | copy-start | bytes 6291460
  100.2 16.1 %copy-start.5 = (f32[1024,256]{1,0:T(8,128)}, f32[1024,256]{1,0:T(8,128)S(1)}, u32[]{:S(2)}) copy-start(f32[1024,256]{1,0:T(8,128)S(1)} %fusion.12) | copy-start | bytes 3145732
  107.6 20.0 %collective-permute-start.16 = (bf16[1024,256]{1,0:T(8,128)(2,1)}, bf16[1024,256]{1,0:T(8,128)(2,1)}, u32[]{:S(2)}, u32[]{:S(2)}) collective-permute-start(bf16[1024,256]{1,0:T(8,128)(2,1)} %get-tuple-element.47), channel_id=1, source_target_pairs={{0,4},{1,5},{2,6},{3,7},{4,0},{5,1},{6,2},{7,3},{8,12},{9,13},{10,... | collective-permute-start | bytes 1572872 | tf_op jit(solution)/shard_map/ppermute | solution.py:30
  117.9 19.7 %collective-permute-start.23 = (bf16[1024,256]{1,0:T(8,128)(2,1)}, bf16[1024,256]{1,0:T(8,128)(2,1)}, u32[]{:S(2)}, u32[]{:S(2)}) collective-permute-start(bf16[1024,256]{1,0:T(8,128)(2,1)} %fusion.37), channel_id=1, source_target_pairs={{0,4},{1,5},{2,6},{3,7},{4,0},{5,1},{6,2},{7,3},{8,12},{9,13},{10,... | collective-permute-start | bytes 1572872 | tf_op jit(solution)/shard_map/ppermute | solution.py:30
  123.0 51.5 %all-to-all-start.1 = ((f32[8,128,512]{2,1,0:T(8,128)}), f32[8,128,512]{2,1,0:T(8,128)}, u32[]{:S(2)}, u32[]{:S(2)}) async-start(f32[8,128,512]{2,1,0:T(8,128)} %broadcast_in_dim.4), calls=%async_computation.1 | async-start | bytes 4194304 | tf_op jit(solution)/shard_map/all_to_all | solution.py:189
  127.5 10.1 %copy-start.8 = (bf16[1024,2048]{1,0:T(8,128)(2,1)S(1)}, bf16[1024,2048]{1,0:T(8,128)(2,1)}, u32[]{:S(2)}) copy-start(bf16[1024,2048]{1,0:T(8,128)(2,1)} %copy-done.7) | copy-start | bytes 12582916
  131.5 9.0 %collective-permute-start.17 = (bf16[256,256]{1,0:T(8,128)(2,1)S(1)}, bf16[256,256]{1,0:T(8,128)(2,1)S(1)}, u32[]{:S(2)}, u32[]{:S(2)}) collective-permute-start(bf16[256,256]{1,0:T(8,128)(2,1)S(1)} %get-tuple-element.67), channel_id=1, source_target_pairs={{0,3},{1,0},{2,1},{3,2},{4,7},{5,4},{6,5},{7,6},{8,11},{9,8},{10,9... | collective-permute-start | bytes 393224 | tf_op jit(solution)/shard_map/ppermute | solution.py:30
  135.2 7.5 %collective-permute-start.19 = (bf16[256,256]{1,0:T(8,128)(2,1)S(1)}, bf16[256,256]{1,0:T(8,128)(2,1)S(1)}, u32[]{:S(2)}, u32[]{:S(2)}) collective-permute-start(bf16[256,256]{1,0:T(8,128)(2,1)S(1)} %get-tuple-element.68), channel_id=1, source_target_pairs={{0,2},{1,3},{2,0},{3,1},{4,6},{5,7},{6,4},{7,5},{8,10},{9,11},{10,... | collective-permute-start | bytes 393224 | tf_op jit(solution)/shard_map/ppermute | solution.py:30
  136.0 8.0 %collective-permute-start.18 = (bf16[256,256]{1,0:T(8,128)(2,1)S(1)}, bf16[256,256]{1,0:T(8,128)(2,1)S(1)}, u32[]{:S(2)}, u32[]{:S(2)}) collective-permute-start(bf16[256,256]{1,0:T(8,128)(2,1)S(1)} %get-tuple-element.69), channel_id=1, source_target_pairs={{0,1},{1,2},{2,3},{3,0},{4,5},{5,6},{6,7},{7,4},{8,9},{9,10},{10,1... | collective-permute-start | bytes 393224 | tf_op jit(solution)/shard_map/ppermute | solution.py:30
  144.1 6.7 %collective-permute-start.22 = (bf16[256,256]{1,0:T(8,128)(2,1)S(1)}, bf16[256,256]{1,0:T(8,128)(2,1)S(1)}, u32[]{:S(2)}, u32[]{:S(2)}) collective-permute-start(bf16[256,256]{1,0:T(8,128)(2,1)S(1)} %subtract_convert_fusion.1), channel_id=1, source_target_pairs={{0,3},{1,0},{2,1},{3,2},{4,7},{5,4},{6,5},{7,6},{8,11},{9,8},{10,9... | collective-permute-start | bytes 393224 | tf_op jit(solution)/shard_map/ppermute | solution.py:30
  144.8 9.0 %collective-permute-start.21 = (bf16[256,256]{1,0:T(8,128)(2,1)S(1)}, bf16[256,256]{1,0:T(8,128)(2,1)S(1)}, u32[]{:S(2)}, u32[]{:S(2)}) collective-permute-start(bf16[256,256]{1,0:T(8,128)(2,1)S(1)} %subtract_convert_fusion.1), channel_id=1, source_target_pairs={{0,2},{1,3},{2,0},{3,1},{4,6},{5,7},{6,4},{7,5},{8,10},{9,11},{10,... | collective-permute-start | bytes 393224 | tf_op jit(solution)/shard_map/ppermute | solution.py:30
  146.7 10.5 %collective-permute-start.20 = (bf16[256,256]{1,0:T(8,128)(2,1)S(1)}, bf16[256,256]{1,0:T(8,128)(2,1)S(1)}, u32[]{:S(2)}, u32[]{:S(2)}) collective-permute-start(bf16[256,256]{1,0:T(8,128)(2,1)S(1)} %subtract_convert_fusion.1), channel_id=1, source_target_pairs={{0,1},{1,2},{2,3},{3,0},{4,5},{5,6},{6,7},{7,4},{8,9},{9,10},{10,1... | collective-permute-start | bytes 393224 | tf_op jit(solution)/shard_map/ppermute | solution.py:30
  147.4 11.3 %collective-permute-start.26 = (bf16[256,256]{1,0:T(8,128)(2,1)S(1)}, bf16[256,256]{1,0:T(8,128)(2,1)S(1)}, u32[]{:S(2)}, u32[]{:S(2)}) collective-permute-start(bf16[256,256]{1,0:T(8,128)(2,1)S(1)} %get-tuple-element.64), channel_id=1, source_target_pairs={{0,2},{1,3},{2,0},{3,1},{4,6},{5,7},{6,4},{7,5},{8,10},{9,11},{10,... | collective-permute-start | bytes 393224 | tf_op jit(solution)/shard_map/ppermute | solution.py:30
  150.5 8.9 %collective-permute-start.25 = (bf16[256,256]{1,0:T(8,128)(2,1)S(1)}, bf16[256,256]{1,0:T(8,128)(2,1)S(1)}, u32[]{:S(2)}, u32[]{:S(2)}) collective-permute-start(bf16[256,256]{1,0:T(8,128)(2,1)S(1)} %get-tuple-element.65), channel_id=1, source_target_pairs={{0,1},{1,2},{2,3},{3,0},{4,5},{5,6},{6,7},{7,4},{8,9},{9,10},{10,1... | collective-permute-start | bytes 393224 | tf_op jit(solution)/shard_map/ppermute | solution.py:30
  150.9 8.6 %collective-permute-start.24 = (bf16[256,256]{1,0:T(8,128)(2,1)S(1)}, bf16[256,256]{1,0:T(8,128)(2,1)S(1)}, u32[]{:S(2)}, u32[]{:S(2)}) collective-permute-start(bf16[256,256]{1,0:T(8,128)(2,1)S(1)} %get-tuple-element.66), channel_id=1, source_target_pairs={{0,3},{1,0},{2,1},{3,2},{4,7},{5,4},{6,5},{7,6},{8,11},{9,8},{10,9... | collective-permute-start | bytes 393224 | tf_op jit(solution)/shard_map/ppermute | solution.py:30
  159.5 5.9 %collective-permute-start.29 = (bf16[256,256]{1,0:T(8,128)(2,1)S(1)}, bf16[256,256]{1,0:T(8,128)(2,1)S(1)}, u32[]{:S(2)}, u32[]{:S(2)}) collective-permute-start(bf16[256,256]{1,0:T(8,128)(2,1)S(1)} %subtract_convert_fusion), channel_id=1, source_target_pairs={{0,3},{1,0},{2,1},{3,2},{4,7},{5,4},{6,5},{7,6},{8,11},{9,8},{10,9... | collective-permute-start | bytes 393224 | tf_op jit(solution)/shard_map/ppermute | solution.py:30
  160.4 7.3 %collective-permute-start.28 = (bf16[256,256]{1,0:T(8,128)(2,1)S(1)}, bf16[256,256]{1,0:T(8,128)(2,1)S(1)}, u32[]{:S(2)}, u32[]{:S(2)}) collective-permute-start(bf16[256,256]{1,0:T(8,128)(2,1)S(1)} %subtract_convert_fusion), channel_id=1, source_target_pairs={{0,2},{1,3},{2,0},{3,1},{4,6},{5,7},{6,4},{7,5},{8,10},{9,11},{10,... | collective-permute-start | bytes 393224 | tf_op jit(solution)/shard_map/ppermute | solution.py:30
  162.2 6.8 %collective-permute-start.27 = (bf16[256,256]{1,0:T(8,128)(2,1)S(1)}, bf16[256,256]{1,0:T(8,128)(2,1)S(1)}, u32[]{:S(2)}, u32[]{:S(2)}) collective-permute-start(bf16[256,256]{1,0:T(8,128)(2,1)S(1)} %subtract_convert_fusion), channel_id=1, source_target_pairs={{0,1},{1,2},{2,3},{3,0},{4,5},{5,6},{6,7},{7,4},{8,9},{9,10},{10,1... | collective-permute-start | bytes 393224 | tf_op jit(solution)/shard_map/ppermute | solution.py:30
  162.6 17.8 %collective-permute-start.30 = (bf16[1024,256]{1,0:T(8,128)(2,1)}, bf16[1024,256]{1,0:T(8,128)(2,1)}, u32[]{:S(2)}, u32[]{:S(2)}) collective-permute-start(bf16[1024,256]{1,0:T(8,128)(2,1)} %fusion.22), channel_id=1, source_target_pairs={{0,4},{1,5},{2,6},{3,7},{4,0},{5,1},{6,2},{7,3},{8,12},{9,13},{10,... | collective-permute-start | bytes 1572872 | tf_op jit(solution)/shard_map/ppermute | solution.py:30
  170.6 17.5 %collective-permute-start.31 = (bf16[1024,256]{1,0:T(8,128)(2,1)}, bf16[1024,256]{1,0:T(8,128)(2,1)}, u32[]{:S(2)}, u32[]{:S(2)}) collective-permute-start(bf16[1024,256]{1,0:T(8,128)(2,1)} %fusion.25), channel_id=1, source_target_pairs={{0,4},{1,5},{2,6},{3,7},{4,0},{5,1},{6,2},{7,3},{8,12},{9,13},{10,... | collective-permute-start | bytes 1572872 | tf_op jit(solution)/shard_map/ppermute | solution.py:30
  177.4 3.0 %copy-start.2 = (f32[1,1024,512]{2,1,0:T(8,128)S(1)}, f32[1,1024,512]{2,1,0:T(8,128)}, u32[]{:S(2)}) copy-start(f32[1,1024,512]{2,1,0:T(8,128)} %param.11) | copy-start | bytes 6291460
  177.4 3.2 %copy-start.4 = (f32[1,1024,512]{2,1,0:T(8,128)S(1)}, f32[1,1024,512]{2,1,0:T(8,128)}, u32[]{:S(2)}) copy-start(f32[1,1024,512]{2,1,0:T(8,128)} %param.12) | copy-start | bytes 6291460
  177.4 4.0 %copy-start.12 = (f32[1024,256]{1,0:T(8,128)S(1)}, f32[1024,256]{1,0:T(8,128)}, u32[]{:S(2)}) copy-start(f32[1024,256]{1,0:T(8,128)} %get-tuple-element.71) | copy-start | bytes 3145732
  177.4 4.3 %copy-start.14 = (f32[1024,256]{1,0:T(8,128)S(1)}, f32[1024,256]{1,0:T(8,128)}, u32[]{:S(2)}) copy-start(f32[1024,256]{1,0:T(8,128)} %fusion.10) | copy-start | bytes 3145732
  177.4 4.4 %copy-start.16 = (bf16[1024,256]{1,0:T(8,128)(2,1)S(1)}, bf16[1024,256]{1,0:T(8,128)(2,1)}, u32[]{:S(2)}) copy-start(bf16[1024,256]{1,0:T(8,128)(2,1)} %copy-done.15) | copy-start | bytes 1572868
  181.8 6.2 %copy-start.6 = (f32[1024,256]{1,0:T(8,128)S(1)}, f32[1024,256]{1,0:T(8,128)}, u32[]{:S(2)}) copy-start(f32[1024,256]{1,0:T(8,128)} %copy-done.5) | copy-start | bytes 3145732
  181.8 6.2 %copy-start.13 = (f32[1024,256]{1,0:T(8,128)S(1)}, f32[1024,256]{1,0:T(8,128)}, u32[]{:S(2)}) copy-start(f32[1024,256]{1,0:T(8,128)} %fusion.8) | copy-start | bytes 3145732
  (4 other events, 9.8 us)

commit v5 on v4

--- a/solution.py
+++ b/solution.py
@@ -137,9 +137,9 @@
     pieces = lax.all_to_all(
         frag_inner[0].reshape(mates, frag_rows, -1), "rep", 0, 0, axis_index_groups=rep_groups
     )
-    blocks[1], blocks[2], blocks[3], pieces = tie(blocks[1], blocks[2], blocks[3], pieces)
+    blocks[1], blocks[3], pieces = tie(blocks[1], blocks[3], pieces)
     piece_sum = jnp.sum(f32(pieces), axis=0)
-    piece_sum = piece_sum + lax.ppermute(piece_sum, "rep", across)
+    piece_sum = (piece_sum + lax.ppermute(piece_sum, "rep", across)) / replicas
 
     teacher = f32(targets[0])
     part = {dx: bf16(dot(blocks[dx], both)) for dx in (1, 2, 3)}
@@ -193,7 +193,7 @@
         0,
         axis_index_groups=rep_groups,
     ).reshape(frag_outer.shape)
-    delta = frag_outer - inner_sum / replicas
+    delta = frag_outer - inner_sum
     frag_params, momentum_out = outer_nesterov(frag_outer, frag_momentum, delta)
 
     both_a = jnp.concatenate([sent_a, other_a], axis=0)

time: 193 us -> 187 us (0.969)
  starting transfers between devices: 68.5 us -> 64.9 us
  local copies, waits for them, and re-layouts: 4.02 us -> 1.72 us
    all_to_all x1, waiting for transfers between devices: 13.8 us -> 0.01 us  [shards(): lax.all_to_all(frag_inner[0].reshape(mates, frag_rows, -1), 'rep', 0, 0,...]
    ppermute x31, waiting for transfers between devices: 50.1 us -> 62 us  [shift(): return lax.ppermute(value, 'fsdp', pairs)]
    ppermute x31, starting transfers between devices: 57.6 us -> 54 us  [shift(): return lax.ppermute(value, 'fsdp', pairs)]
    add x1, other arithmetic: 2.95 us -> 5.85 us  [outer_nesterov(): momentum_new = 0.9 * momentum + delta]
    unnamed x36 -> x32, local copies, waits for them, and re-layouts: 2.37 us -> 0.07 us
    div x1, other arithmetic: 1.99 us -> 0.04 us  [shards(): piece_sum = (piece_sum + lax.ppermute(piece_sum, 'rep', across)) / replicas]
  transfers between devices with their start and end apart: 34 -> 34, of which waited for: 20 -> 22; matrix products, arithmetic and copies ran while one was open for 21% -> 24% of each run, Pallas kernels for 3% -> 3%
where the time goes in v5:
time: 187 us; the launch traced here: 185 us
  starting transfers between devices  64.9 us (35%)
  waiting for transfers between devices  62 us (33%)
  matrix products  27.6 us (15%)
  other arithmetic  19.8 us (11%)
  Pallas kernels  8.47 us (5%)
    ppermute x31, waiting for transfers between devices, shift(): return lax.ppermute(value, 'fsdp', pairs)  62 us
    ppermute x31, starting transfers between devices, shift(): return lax.ppermute(value, 'fsdp', pairs)  54 us
    dot_general x6, matrix products, dot(): return jnp.dot(a, b, preferred_element_type=jnp.float32)  16.2 us
    dot_general x8, matrix products, dot_t(): lax.dot_general(a, b, (((0,), (0,)), ((), ())), preferred_element_type=jn...  11.4 us
    pallas_call x4, Pallas kernels, pick(): pl.pallas_call(functools.partial(pick_kernel, dx), out_shape=jax.ShapeDty...  8.47 us
    add x1, other arithmetic, outer_nesterov(): momentum_new = 0.9 * momentum + delta  5.85 us
    all_to_all x1, starting transfers between devices, shards(): lax.all_to_all(frag_inner[0].reshape(mates, frag_rows, -1), 'rep', 0, 0,...  4.47 us
    all_to_all x1, starting transfers between devices, shards(): lax.all_to_all(jnp.broadcast_to(piece_sum[None], (mates, *piece_sum.shape...  4.47 us
  transfers between devices with their start and end apart: 34, of which 22 were waited for; matrix products, arithmetic and copies ran while one was open for 24% of the time, Pallas kernels for 3%

profile of v5, /device:TPU:0, one launch (start us, length us, event | category | flops | bytes accessed | tf_op | source)
XLA Modules:
  0.0 185.5 jit_solution(12972321785975710992)
XLA Ops:
  0.6 2.1 %shard_map.106 = bf16[256,2048]{1,0:T(8,128)(2,1)} custom-call(bf16[256,8192]{1,0:T(8,128)(2,1)} %bitcast.79), custom_call_target="tpu_custom_call" | custom-call | bytes 2097152 | tf_op jit(solution)/shard_map/pallas_call | solution.py:86
  2.8 3.2 %collective-permute-start.3 = (bf16[256,2048]{1,0:T(8,128)(2,1)}, bf16[256,2048]{1,0:T(8,128)(2,1)}, u32[]{:S(2)}, u32[]{:S(2)}) collective-permute-start(bf16[256,2048]{1,0:T(8,128)(2,1)} %shard_map.106), channel_id=1, source_target_pairs={{0,2},{1,3},{2,0},{3,1},{4,6},{5,7},{6,4},{7,5},{8,10},{9,11},{10,... | collective-permute-start | bytes 3145736 | tf_op jit(solution)/shard_map/ppermute | solution.py:30
  5.9 2.1 %shard_map.105 = bf16[256,2048]{1,0:T(8,128)(2,1)} custom-call(bf16[256,8192]{1,0:T(8,128)(2,1)} %bitcast.80), custom_call_target="tpu_custom_call" | custom-call | bytes 2097152 | tf_op jit(solution)/shard_map/pallas_call | solution.py:86
  9.2 3.9 %collective-permute-start.2 = (bf16[1024,512]{1,0:T(8,128)(2,1)}, bf16[1024,512]{1,0:T(8,128)(2,1)}, u32[]{:S(2)}, u32[]{:S(2)}) collective-permute-start(bf16[1024,512]{1,0:T(8,128)(2,1)} %convert_element_type.105), channel_id=1, source_target_pairs={{0,4},{1,5},{2,6},{3,7},{4,0},{5,1},{6,2},{7,3},{8,12},{9,13},{10,... | collective-permute-start | bytes 3145736 | tf_op jit(solution)/shard_map/ppermute | solution.py:30
  13.0 2.1 %shard_map.104 = bf16[256,2048]{1,0:T(8,128)(2,1)} custom-call(bf16[256,8192]{1,0:T(8,128)(2,1)} %bitcast.81), custom_call_target="tpu_custom_call" | custom-call | bytes 2097152 | tf_op jit(solution)/shard_map/pallas_call | solution.py:86
  15.8 2.6 %collective-permute-start.1 = (bf16[256,2048]{1,0:T(8,128)(2,1)}, bf16[256,2048]{1,0:T(8,128)(2,1)}, u32[]{:S(2)}, u32[]{:S(2)}) collective-permute-start(bf16[256,2048]{1,0:T(8,128)(2,1)} %shard_map.105), channel_id=1, source_target_pairs={{0,3},{1,0},{2,1},{3,2},{4,7},{5,4},{6,5},{7,6},{8,11},{9,8},{10,9... | collective-permute-start | bytes 3145736 | tf_op jit(solution)/shard_map/ppermute | solution.py:30
  18.4 4.5 %all-to-all-start = ((bf16[8,128,512]{2,1,0:T(8,128)(2,1)}), bf16[8,128,512]{2,1,0:T(8,128)(2,1)}, u32[]{:S(2)}, u32[]{:S(2)}) async-start(bf16[8,128,512]{2,1,0:T(8,128)(2,1)} %bitcast.2), calls=%async_computation | async-start | bytes 2097152 | tf_op jit(solution)/shard_map/all_to_all | solution.py:137
  22.9 2.2 %shard_map.103 = bf16[256,2048]{1,0:T(8,128)(2,1)} custom-call(bf16[256,8192]{1,0:T(8,128)(2,1)} %bitcast.82), custom_call_target="tpu_custom_call" | custom-call | bytes 2097152 | tf_op jit(solution)/shard_map/pallas_call | solution.py:86
  25.2 5.6 %collective-permute-done.3 = bf16[256,2048]{1,0:T(8,128)(2,1)} collective-permute-done((bf16[256,2048]{1,0:T(8,128)(2,1)}, bf16[256,2048]{1,0:T(8,128)(2,1)}, u32[]{:S(2)}, u32[]{:S(2)}) %collective-permute-start.3) | collective-permute-done | bytes 1048608 | tf_op jit(solution)/shard_map/ppermute | solution.py:30
  30.8 5.5 %collective-permute-done.2 = bf16[1024,512]{1,0:T(8,128)(2,1)} collective-permute-done((bf16[1024,512]{1,0:T(8,128)(2,1)}, bf16[1024,512]{1,0:T(8,128)(2,1)}, u32[]{:S(2)}, u32[]{:S(2)}) %collective-permute-start.2) | collective-permute-done | bytes 1048608 | tf_op jit(solution)/shard_map/ppermute | solution.py:30
  36.2 2.6 %fusion.28 = bf16[256,512]{1,0:T(8,128)(2,1)S(1)} fusion(bf16[256,2048]{1,0:T(8,128)(2,1)} %collective-permute-done.3, bf16[1024,512]{1,0:T(8,128)(2,1)} %collective-permute-done.2, bf16[1024,512]{1,0:T(8,128)(2,1)} %convert_element_type.105), kind=kOutput, calls=%fused_computation.32 | convolution fusion | flops 541196288 | bytes 3407872 | tf_op jit(solution)/shard_map/dot_general | solution.py:42
  39.5 13.6 %collective-permute-done = bf16[256,2048]{1,0:T(8,128)(2,1)} collective-permute-done((bf16[256,2048]{1,0:T(8,128)(2,1)}, bf16[256,2048]{1,0:T(8,128)(2,1)}, u32[]{:S(2)}, u32[]{:S(2)}) %collective-permute-start) | collective-permute-done | bytes 1048608 | tf_op jit(solution)/shard_map/ppermute | solution.py:30
  53.4 2.6 %convolution_convert_fusion.3 = bf16[256,512]{1,0:T(8,128)(2,1)S(1)} fusion(bf16[256,2048]{1,0:T(8,128)(2,1)} %collective-permute-done.1, bf16[1024,512]{1,0:T(8,128)(2,1)} %collective-permute-done.2, bf16[1024,512]{1,0:T(8,128)(2,1)} %convert_element_type.105), kind=kOutput, calls=%fused_computation.30 | convolution fusion | flops 541196288 | bytes 3407872 | tf_op jit(solution)/shard_map/dot_general | solution.py:42
  57.5 2.6 %convolution_convert_fusion.4 = bf16[256,512]{1,0:T(8,128)(2,1)S(1)} fusion(bf16[256,2048]{1,0:T(8,128)(2,1)} %collective-permute-done, bf16[1024,512]{1,0:T(8,128)(2,1)} %collective-permute-done.2, bf16[1024,512]{1,0:T(8,128)(2,1)} %convert_element_type.105), kind=kOutput, calls=%fused_computation.31 | convolution fusion | flops 541196288 | bytes 3407872 | tf_op jit(solution)/shard_map/dot_general | solution.py:42
  60.0 1.9 %collective-permute-start.4 = (bf16[256,512]{1,0:T(8,128)(2,1)S(1)}, bf16[256,512]{1,0:T(8,128)(2,1)S(1)}, u32[]{:S(2)}, u32[]{:S(2)}) collective-permute-start(bf16[256,512]{1,0:T(8,128)(2,1)S(1)} %convolution_convert_fusion.4), channel_id=1, source_target_pairs={{0,3},{1,0},{2,1},{3,2},{4,7},{5,4},{6,5},{7,6},{8,11},{9,8},{10,9... | collective-permute-start | bytes 786440 | tf_op jit(solution)/shard_map/ppermute | solution.py:30
  61.9 2.2 %fusion.43 = f32[256,512]{1,0:T(8,128)S(1)} fusion(bf16[256,2048]{1,0:T(8,128)(2,1)S(1)} %copy-done.9, bf16[1024,512]{1,0:T(8,128)(2,1)} %collective-permute-done.2, bf16[1024,512]{1,0:T(8,128)(2,1)} %convert_element_type.105), kind=kOutput, calls=%fused_computation.70 | convolution fusion | flops 541065216 | bytes 3670016 | tf_op jit(solution)/shard_map/dot_general | solution.py:42
  64.1 2.1 %pad_maximum_fusion = bf16[1024,2048]{1,0:T(8,128)(2,1)S(1)} fusion(bf16[256,2048]{1,0:T(8,128)(2,1)} %collective-permute-done.1, bf16[256,2048]{1,0:T(8,128)(2,1)} %collective-permute-done.3, bf16[256,2048]{1,0:T(8,128)(2,1)} %collective-permute-done, bf16[256,2048]{1,0:T(8,128)(2,1)S(1)} %copy-done.9), kind=kLoop, calls=%fused_computation | loop fusion | flops 16777216 | bytes 8388608 | tf_op jit(solution)/shard_map/concatenate | solution.py:153
  68.1 3.1 %collective-permute-start.9 = (bf16[256,256]{1,0:T(8,128)(2,1)S(1)}, bf16[256,256]{1,0:T(8,128)(2,1)S(1)}, u32[]{:S(2)}, u32[]{:S(2)}) collective-permute-start(bf16[256,256]{1,0:T(8,128)(2,1)S(1)} %get-tuple-element.60), channel_id=1, source_target_pairs={{0,3},{1,0},{2,1},{3,2},{4,7},{5,4},{6,5},{7,6},{8,11},{9,8},{10,9... | collective-permute-start | bytes 393224 | tf_op jit(solution)/shard_map/ppermute | solution.py:30
  73.7 2.0 %collective-permute-start.15 = (f32[128,512]{1,0:T(8,128)S(1)}, f32[128,512]{1,0:T(8,128)S(1)}, u32[]{:S(2)}, u32[]{:S(2)}) collective-permute-start(f32[128,512]{1,0:T(8,128)S(1)} %convert_reduce_fusion), channel_id=1, source_target_pairs={{0,64},{8,72},{16,80},{24,88},{32,96},{40,104},{48,112},{56,120},{... | collective-permute-start | bytes 786440 | tf_op jit(solution)/shard_map/ppermute | solution.py:142
  75.7 2.6 %collective-permute-start.12 = (bf16[256,256]{1,0:T(8,128)(2,1)S(1)}, bf16[256,256]{1,0:T(8,128)(2,1)S(1)}, u32[]{:S(2)}, u32[]{:S(2)}) collective-permute-start(bf16[256,256]{1,0:T(8,128)(2,1)S(1)} %get-tuple-element.59), channel_id=1, source_target_pairs={{0,3},{1,0},{2,1},{3,2},{4,7},{5,4},{6,5},{7,6},{8,11},{9,8},{10,9... | collective-permute-start | bytes 393224 | tf_op jit(solution)/shard_map/ppermute | solution.py:30
  78.3 1.8 collective-permute-start.11
  80.9 3.9 %collective-permute-start.13 = (bf16[1024,256]{1,0:T(8,128)(2,1)S(1)}, bf16[1024,256]{1,0:T(8,128)(2,1)S(1)}, u32[]{:S(2)}, u32[]{:S(2)}) collective-permute-start(bf16[1024,256]{1,0:T(8,128)(2,1)S(1)} %fusion.16), channel_id=1, source_target_pairs={{0,4},{1,5},{2,6},{3,7},{4,0},{5,1},{6,2},{7,3},{8,12},{9,13},{10,... | collective-permute-start | bytes 1572872 | tf_op jit(solution)/shard_map/ppermute | solution.py:30
  87.1 3.8 %collective-permute-start.14 = (bf16[1024,256]{1,0:T(8,128)(2,1)S(1)}, bf16[1024,256]{1,0:T(8,128)(2,1)S(1)}, u32[]{:S(2)}, u32[]{:S(2)}) collective-permute-start(bf16[1024,256]{1,0:T(8,128)(2,1)S(1)} %fusion.19), channel_id=1, source_target_pairs={{0,4},{1,5},{2,6},{3,7},{4,0},{5,1},{6,2},{7,3},{8,12},{9,13},{10,... | collective-permute-start | bytes 1572872 | tf_op jit(solution)/shard_map/ppermute | solution.py:30
  91.7 5.8 %collective-permute-done.13 = bf16[1024,256]{1,0:T(8,128)(2,1)S(1)} collective-permute-done((bf16[1024,256]{1,0:T(8,128)(2,1)S(1)}, bf16[1024,256]{1,0:T(8,128)(2,1)S(1)}, u32[]{:S(2)}, u32[]{:S(2)}) %collective-permute-start.13) | collective-permute-done | bytes 524320 | tf_op jit(solution)/shard_map/ppermute | solution.py:30
  97.6 2.5 %fusion.37 = (bf16[1024,256]{1,0:T(8,128)(2,1)}, f32[1024,256]{1,0:T(8,128)}) fusion(f32[1,1024,512]{2,1,0:T(8,128)S(1)} %copy-done, bf16[1024,256]{1,0:T(8,128)(2,1)S(1)} %collective-permute-done.13, f32[1,1024,512]{2,1,0:T(8,128)S(1)} %copy-done.1, f32[1,1024,512]{2,1,0:T(8,128)S(1)} %copy-done.3, bf16[1024,256]{1,0:T(8,128)(2,1)S(1)} %pad_maximum_fusion.2, ...), kind=kOutput, calls=%fused_computation.53 | convolution fusion | flops 541327360 | bytes 7864320 | tf_op jit(solution)/shard_map/dot_general | solution.py:50
  100.1 3.5 %collective-permute-start.16 = (bf16[1024,256]{1,0:T(8,128)(2,1)}, bf16[1024,256]{1,0:T(8,128)(2,1)}, u32[]{:S(2)}, u32[]{:S(2)}) collective-permute-start(bf16[1024,256]{1,0:T(8,128)(2,1)} %get-tuple-element.45), channel_id=1, source_target_pairs={{0,4},{1,5},{2,6},{3,7},{4,0},{5,1},{6,2},{7,3},{8,12},{9,13},{10,... | collective-permute-start | bytes 1572872 | tf_op jit(solution)/shard_map/ppermute | solution.py:30
  103.7 5.1 %collective-permute-done.14 = bf16[1024,256]{1,0:T(8,128)(2,1)S(1)} collective-permute-done((bf16[1024,256]{1,0:T(8,128)(2,1)S(1)}, bf16[1024,256]{1,0:T(8,128)(2,1)S(1)}, u32[]{:S(2)}, u32[]{:S(2)}) %collective-permute-start.14) | collective-permute-done | bytes 524320 | tf_op jit(solution)/shard_map/ppermute | solution.py:30
  108.8 1.7 fusion.38
  110.5 3.5 %collective-permute-start.23 = (bf16[1024,256]{1,0:T(8,128)(2,1)}, bf16[1024,256]{1,0:T(8,128)(2,1)}, u32[]{:S(2)}, u32[]{:S(2)}) collective-permute-start(bf16[1024,256]{1,0:T(8,128)(2,1)} %fusion.38), channel_id=1, source_target_pairs={{0,4},{1,5},{2,6},{3,7},{4,0},{5,1},{6,2},{7,3},{8,12},{9,13},{10,... | collective-permute-start | bytes 1572872 | tf_op jit(solution)/shard_map/ppermute | solution.py:30
  115.6 4.5 %all-to-all-start.1 = ((f32[8,128,512]{2,1,0:T(8,128)}), f32[8,128,512]{2,1,0:T(8,128)}, u32[]{:S(2)}, u32[]{:S(2)}) async-start(f32[8,128,512]{2,1,0:T(8,128)} %broadcast_in_dim.4), calls=%async_computation.1 | async-start | bytes 4194304 | tf_op jit(solution)/shard_map/all_to_all | solution.py:189
  120.1 3.9 %convolution_convert_fusion.1 = bf16[1024,256]{1,0:T(8,128)(2,1)S(1)} fusion(bf16[1024,2048]{1,0:T(8,128)(2,1)} %copy-done.7, bf16[1024,256]{1,0:T(8,128)(2,1)} %collective-permute-done.16, bf16[1024,256]{1,0:T(8,128)(2,1)} %get-tuple-element.45), kind=kOutput, calls=%fused_computation.28 | convolution fusion | flops 1076101120 | bytes 5767168 | tf_op jit(solution)/shard_map/dot_general | solution.py:42
  124.0 3.1 %collective-permute-start.17 = (bf16[256,256]{1,0:T(8,128)(2,1)S(1)}, bf16[256,256]{1,0:T(8,128)(2,1)S(1)}, u32[]{:S(2)}, u32[]{:S(2)}) collective-permute-start(bf16[256,256]{1,0:T(8,128)(2,1)S(1)} %get-tuple-element.65), channel_id=1, source_target_pairs={{0,3},{1,0},{2,1},{3,2},{4,7},{5,4},{6,5},{7,6},{8,11},{9,8},{10,9... | collective-permute-start | bytes 393224 | tf_op jit(solution)/shard_map/ppermute | solution.py:30
  128.6 2.5 %convolution_convert_fusion = bf16[1024,256]{1,0:T(8,128)(2,1)S(1)} fusion(bf16[1024,2048]{1,0:T(8,128)(2,1)S(1)} %copy-done.8, bf16[1024,256]{1,0:T(8,128)(2,1)} %collective-permute-done.23, bf16[1024,256]{1,0:T(8,128)(2,1)} %fusion.38), kind=kOutput, calls=%fused_computation.27 | convolution fusion | flops 1076101120 | bytes 5767168 | tf_op jit(solution)/shard_map/dot_general | solution.py:42
  131.1 2.2 %collective-permute-done.17 = bf16[256,256]{1,0:T(8,128)(2,1)S(1)} collective-permute-done((bf16[256,256]{1,0:T(8,128)(2,1)S(1)}, bf16[256,256]{1,0:T(8,128)(2,1)S(1)}, u32[]{:S(2)}, u32[]{:S(2)}) %collective-permute-start.17) | collective-permute-done | bytes 131104 | tf_op jit(solution)/shard_map/ppermute | solution.py:30
  133.3 1.7 collective-permute-done.19
  135.0 2.0 %collective-permute-done.18 = bf16[256,256]{1,0:T(8,128)(2,1)S(1)} collective-permute-done((bf16[256,256]{1,0:T(8,128)(2,1)S(1)}, bf16[256,256]{1,0:T(8,128)(2,1)S(1)}, u32[]{:S(2)}, u32[]{:S(2)}) %collective-permute-start.18) | collective-permute-done | bytes 131104 | tf_op jit(solution)/shard_map/ppermute | solution.py:30
  139.2 4.2 %collective-permute-start.26 = (bf16[256,256]{1,0:T(8,128)(2,1)S(1)}, bf16[256,256]{1,0:T(8,128)(2,1)S(1)}, u32[]{:S(2)}, u32[]{:S(2)}) collective-permute-start(bf16[256,256]{1,0:T(8,128)(2,1)S(1)} %get-tuple-element.62), channel_id=1, source_target_pairs={{0,2},{1,3},{2,0},{3,1},{4,6},{5,7},{6,4},{7,5},{8,10},{9,11},{10,... | collective-permute-start | bytes 393224 | tf_op jit(solution)/shard_map/ppermute | solution.py:30
  143.5 3.2 %collective-permute-start.24 = (bf16[256,256]{1,0:T(8,128)(2,1)S(1)}, bf16[256,256]{1,0:T(8,128)(2,1)S(1)}, u32[]{:S(2)}, u32[]{:S(2)}) collective-permute-start(bf16[256,256]{1,0:T(8,128)(2,1)S(1)} %get-tuple-element.64), channel_id=1, source_target_pairs={{0,3},{1,0},{2,1},{3,2},{4,7},{5,4},{6,5},{7,6},{8,11},{9,8},{10,9... | collective-permute-start | bytes 393224 | tf_op jit(solution)/shard_map/ppermute | solution.py:30
  146.7 2.5 %collective-permute-done.20 = bf16[256,256]{1,0:T(8,128)(2,1)S(1)} collective-permute-done((bf16[256,256]{1,0:T(8,128)(2,1)S(1)}, bf16[256,256]{1,0:T(8,128)(2,1)S(1)}, u32[]{:S(2)}, u32[]{:S(2)}) %collective-permute-start.20) | collective-permute-done | bytes 131104 | tf_op jit(solution)/shard_map/ppermute | solution.py:30
  150.8 1.9 %collective-permute-done.25 = bf16[256,256]{1,0:T(8,128)(2,1)S(1)} collective-permute-done((bf16[256,256]{1,0:T(8,128)(2,1)S(1)}, bf16[256,256]{1,0:T(8,128)(2,1)S(1)}, u32[]{:S(2)}, u32[]{:S(2)}) %collective-permute-start.25) | collective-permute-done | bytes 131104 | tf_op jit(solution)/shard_map/ppermute | solution.py:30
  155.4 3.8 %collective-permute-done.29 = bf16[256,256]{1,0:T(8,128)(2,1)S(1)} collective-permute-done((bf16[256,256]{1,0:T(8,128)(2,1)S(1)}, bf16[256,256]{1,0:T(8,128)(2,1)S(1)}, u32[]{:S(2)}, u32[]{:S(2)}) %collective-permute-start.29) | collective-permute-done | bytes 131104 | tf_op jit(solution)/shard_map/ppermute | solution.py:30
  159.2 2.5 %collective-permute-done.28 = bf16[256,256]{1,0:T(8,128)(2,1)S(1)} collective-permute-done((bf16[256,256]{1,0:T(8,128)(2,1)S(1)}, bf16[256,256]{1,0:T(8,128)(2,1)S(1)}, u32[]{:S(2)}, u32[]{:S(2)}) %collective-permute-start.28) | collective-permute-done | bytes 131104 | tf_op jit(solution)/shard_map/ppermute | solution.py:30
  164.3 1.7 fusion.10
  166.0 1.7 fusion.8
  167.8 5.8 %multiply_add_fusion = (f32[1024,512]{1,0:T(8,128)}, f32[1024,512]{1,0:T(8,128)}) fusion(f32[1024,512]{1,0:T(8,128)} %param.15, f32[1024,512]{1,0:T(8,128)} %param.13, f32[8,128,512]{2,1,0:T(8,128)} %all-to-all-done.1), kind=kLoop, calls=%fused_computation.5 | loop fusion | flops 3670016 | bytes 10485760 | tf_op jit(solution)/shard_map/add | solution.py:22
  173.7 2.8 %add_add_fusion.1 = f32[1024,256]{1,0:T(8,128)S(1)} fusion(f32[1024,256]{1,0:T(8,128)S(1)} %copy-done.12, bf16[1024,256]{1,0:T(8,128)(2,1)} %collective-permute-done.30, f32[1,1024,512]{2,1,0:T(8,128)S(1)} %copy-done, f32[1024,256]{1,0:T(8,128)S(1)} %copy-done.10, bf16[1024,256]{1,0:T(8,128)(2,1)S(1)} %copy-done.14, f32[1,1024,512]{2,1,0:T(8,128)S(1)} %copy-done.2, ...), kind=kLoop, calls=%fused_computation.50 | loop fusion | flops 8126464 | bytes 7340032 | tf_op jit(solution)/shard_map/add | solution.py:218
  176.5 4.7 %collective-permute-done.31 = bf16[1024,256]{1,0:T(8,128)(2,1)} collective-permute-done((bf16[1024,256]{1,0:T(8,128)(2,1)}, bf16[1024,256]{1,0:T(8,128)(2,1)}, u32[]{:S(2)}, u32[]{:S(2)}) %collective-permute-start.31) | collective-permute-done | bytes 524320 | tf_op jit(solution)/shard_map/ppermute | solution.py:30
  181.2 2.7 %add_add_fusion = f32[1024,256]{1,0:T(8,128)S(1)} fusion(f32[1024,256]{1,0:T(8,128)S(1)} %copy-done.11, bf16[1024,256]{1,0:T(8,128)(2,1)} %collective-permute-done.31, f32[1,1024,512]{2,1,0:T(8,128)S(1)} %copy-done, f32[1024,256]{1,0:T(8,128)S(1)} %copy-done.6, bf16[1024,256]{1,0:T(8,128)(2,1)S(1)} %collective-permute-done.14, ...), kind=kLoop, calls=%fused_computation.49 | loop fusion | flops 8126464 | bytes 7340032 | tf_op jit(solution)/shard_map/add | solution.py:221
  (91 shorter events, 26.5 us)
Async XLA Ops:
  2.7 5.3 %copy-start = (f32[1,1024,512]{2,1,0:T(8,128)S(1)}, f32[1,1024,512]{2,1,0:T(8,128)}, u32[]{:S(2)}) copy-start(f32[1,1024,512]{2,1,0:T(8,128)} %param.10) | copy-start | bytes 6291460
  2.8 28.0 %collective-permute-start.3 = (bf16[256,2048]{1,0:T(8,128)(2,1)}, bf16[256,2048]{1,0:T(8,128)(2,1)}, u32[]{:S(2)}, u32[]{:S(2)}) collective-permute-start(bf16[256,2048]{1,0:T(8,128)(2,1)} %shard_map.106), channel_id=1, source_target_pairs={{0,2},{1,3},{2,0},{3,1},{4,6},{5,7},{6,4},{7,5},{8,10},{9,11},{10,... | collective-permute-start | bytes 3145736 | tf_op jit(solution)/shard_map/ppermute | solution.py:30
  9.2 27.1 %collective-permute-start.2 = (bf16[1024,512]{1,0:T(8,128)(2,1)}, bf16[1024,512]{1,0:T(8,128)(2,1)}, u32[]{:S(2)}, u32[]{:S(2)}) collective-permute-start(bf16[1024,512]{1,0:T(8,128)(2,1)} %convert_element_type.105), channel_id=1, source_target_pairs={{0,4},{1,5},{2,6},{3,7},{4,0},{5,1},{6,2},{7,3},{8,12},{9,13},{10,... | collective-permute-start | bytes 3145736 | tf_op jit(solution)/shard_map/ppermute | solution.py:30
  15.1 38.0 %collective-permute-start = (bf16[256,2048]{1,0:T(8,128)(2,1)}, bf16[256,2048]{1,0:T(8,128)(2,1)}, u32[]{:S(2)}, u32[]{:S(2)}) collective-permute-start(bf16[256,2048]{1,0:T(8,128)(2,1)} %shard_map.104), channel_id=1, source_target_pairs={{0,1},{1,2},{2,3},{3,0},{4,5},{5,6},{6,7},{7,4},{8,9},{9,10},{10,1... | collective-permute-start | bytes 3145736 | tf_op jit(solution)/shard_map/ppermute | solution.py:30
  15.8 37.6 %collective-permute-start.1 = (bf16[256,2048]{1,0:T(8,128)(2,1)}, bf16[256,2048]{1,0:T(8,128)(2,1)}, u32[]{:S(2)}, u32[]{:S(2)}) collective-permute-start(bf16[256,2048]{1,0:T(8,128)(2,1)} %shard_map.105), channel_id=1, source_target_pairs={{0,3},{1,0},{2,1},{3,2},{4,7},{5,4},{6,5},{7,6},{8,11},{9,8},{10,9... | collective-permute-start | bytes 3145736 | tf_op jit(solution)/shard_map/ppermute | solution.py:30
  18.4 21.1 %all-to-all-start = ((bf16[8,128,512]{2,1,0:T(8,128)(2,1)}), bf16[8,128,512]{2,1,0:T(8,128)(2,1)}, u32[]{:S(2)}, u32[]{:S(2)}) async-start(bf16[8,128,512]{2,1,0:T(8,128)(2,1)} %bitcast.2), calls=%async_computation | async-start | bytes 2097152 | tf_op jit(solution)/shard_map/all_to_all | solution.py:137
  38.8 27.5 %collective-permute-start.6 = (bf16[256,512]{1,0:T(8,128)(2,1)S(1)}, bf16[256,512]{1,0:T(8,128)(2,1)S(1)}, u32[]{:S(2)}, u32[]{:S(2)}) collective-permute-start(bf16[256,512]{1,0:T(8,128)(2,1)S(1)} %fusion.28), channel_id=1, source_target_pairs={{0,2},{1,3},{2,0},{3,1},{4,6},{5,7},{6,4},{7,5},{8,10},{9,11},{10,... | collective-permute-start | bytes 786440 | tf_op jit(solution)/shard_map/ppermute | solution.py:30
  55.9 6.0 %copy-start.9 = (bf16[256,2048]{1,0:T(8,128)(2,1)S(1)}, bf16[256,2048]{1,0:T(8,128)(2,1)}, u32[]{:S(2)}) copy-start(bf16[256,2048]{1,0:T(8,128)(2,1)} %shard_map.103) | copy-start | bytes 3145732
  56.0 10.3 %collective-permute-start.5 = (bf16[256,512]{1,0:T(8,128)(2,1)S(1)}, bf16[256,512]{1,0:T(8,128)(2,1)S(1)}, u32[]{:S(2)}, u32[]{:S(2)}) collective-permute-start(bf16[256,512]{1,0:T(8,128)(2,1)S(1)} %convolution_convert_fusion.3), channel_id=1, source_target_pairs={{0,1},{1,2},{2,3},{3,0},{4,5},{5,6},{6,7},{7,4},{8,9},{9,10},{10,1... | collective-permute-start | bytes 786440 | tf_op jit(solution)/shard_map/ppermute | solution.py:30
  60.0 7.8 %collective-permute-start.4 = (bf16[256,512]{1,0:T(8,128)(2,1)S(1)}, bf16[256,512]{1,0:T(8,128)(2,1)S(1)}, u32[]{:S(2)}, u32[]{:S(2)}) collective-permute-start(bf16[256,512]{1,0:T(8,128)(2,1)S(1)} %convolution_convert_fusion.4), channel_id=1, source_target_pairs={{0,3},{1,0},{2,1},{3,2},{4,7},{5,4},{6,5},{7,6},{8,11},{9,8},{10,9... | collective-permute-start | bytes 786440 | tf_op jit(solution)/shard_map/ppermute | solution.py:30
  66.3 31.3 %copy-start.7 = (bf16[1024,2048]{1,0:T(8,128)(2,1)}, bf16[1024,2048]{1,0:T(8,128)(2,1)S(1)}, u32[]{:S(2)}) copy-start(bf16[1024,2048]{1,0:T(8,128)(2,1)S(1)} %pad_maximum_fusion) | copy-start | bytes 12582916
  68.1 10.3 %collective-permute-start.9 = (bf16[256,256]{1,0:T(8,128)(2,1)S(1)}, bf16[256,256]{1,0:T(8,128)(2,1)S(1)}, u32[]{:S(2)}, u32[]{:S(2)}) collective-permute-start(bf16[256,256]{1,0:T(8,128)(2,1)S(1)} %get-tuple-element.60), channel_id=1, source_target_pairs={{0,3},{1,0},{2,1},{3,2},{4,7},{5,4},{6,5},{7,6},{8,11},{9,8},{10,9... | collective-permute-start | bytes 393224 | tf_op jit(solution)/shard_map/ppermute | solution.py:30
  71.1 9.0 %collective-permute-start.8 = (bf16[256,256]{1,0:T(8,128)(2,1)S(1)}, bf16[256,256]{1,0:T(8,128)(2,1)S(1)}, u32[]{:S(2)}, u32[]{:S(2)}) collective-permute-start(bf16[256,256]{1,0:T(8,128)(2,1)S(1)} %get-tuple-element.60), channel_id=1, source_target_pairs={{0,2},{1,3},{2,0},{3,1},{4,6},{5,7},{6,4},{7,5},{8,10},{9,11},{10,... | collective-permute-start | bytes 393224 | tf_op jit(solution)/shard_map/ppermute | solution.py:30
  71.7 8.4 %collective-permute-start.7 = (bf16[256,256]{1,0:T(8,128)(2,1)S(1)}, bf16[256,256]{1,0:T(8,128)(2,1)S(1)}, u32[]{:S(2)}, u32[]{:S(2)}) collective-permute-start(bf16[256,256]{1,0:T(8,128)(2,1)S(1)} %get-tuple-element.60), channel_id=1, source_target_pairs={{0,1},{1,2},{2,3},{3,0},{4,5},{5,6},{6,7},{7,4},{8,9},{9,10},{10,1... | collective-permute-start | bytes 393224 | tf_op jit(solution)/shard_map/ppermute | solution.py:30
  73.7 30.0 %collective-permute-start.15 = (f32[128,512]{1,0:T(8,128)S(1)}, f32[128,512]{1,0:T(8,128)S(1)}, u32[]{:S(2)}, u32[]{:S(2)}) collective-permute-start(f32[128,512]{1,0:T(8,128)S(1)} %convert_reduce_fusion), channel_id=1, source_target_pairs={{0,64},{8,72},{16,80},{24,88},{32,96},{40,104},{48,112},{56,120},{... | collective-permute-start | bytes 786440 | tf_op jit(solution)/shard_map/ppermute | solution.py:142
  75.7 9.1 %collective-permute-start.12 = (bf16[256,256]{1,0:T(8,128)(2,1)S(1)}, bf16[256,256]{1,0:T(8,128)(2,1)S(1)}, u32[]{:S(2)}, u32[]{:S(2)}) collective-permute-start(bf16[256,256]{1,0:T(8,128)(2,1)S(1)} %get-tuple-element.59), channel_id=1, source_target_pairs={{0,3},{1,0},{2,1},{3,2},{4,7},{5,4},{6,5},{7,6},{8,11},{9,8},{10,9... | collective-permute-start | bytes 393224 | tf_op jit(solution)/shard_map/ppermute | solution.py:30
  78.3 6.5 %collective-permute-start.11 = (bf16[256,256]{1,0:T(8,128)(2,1)S(1)}, bf16[256,256]{1,0:T(8,128)(2,1)S(1)}, u32[]{:S(2)}, u32[]{:S(2)}) collective-permute-start(bf16[256,256]{1,0:T(8,128)(2,1)S(1)} %get-tuple-element.59), channel_id=1, source_target_pairs={{0,2},{1,3},{2,0},{3,1},{4,6},{5,7},{6,4},{7,5},{8,10},{9,11},{10,... | collective-permute-start | bytes 393224 | tf_op jit(solution)/shard_map/ppermute | solution.py:30
  80.1 6.2 %collective-permute-start.10 = (bf16[256,256]{1,0:T(8,128)(2,1)S(1)}, bf16[256,256]{1,0:T(8,128)(2,1)S(1)}, u32[]{:S(2)}, u32[]{:S(2)}) collective-permute-start(bf16[256,256]{1,0:T(8,128)(2,1)S(1)} %get-tuple-element.59), channel_id=1, source_target_pairs={{0,1},{1,2},{2,3},{3,0},{4,5},{5,6},{6,7},{7,4},{8,9},{9,10},{10,1... | collective-permute-start | bytes 393224 | tf_op jit(solution)/shard_map/ppermute | solution.py:30
  80.9 16.7 %collective-permute-start.13 = (bf16[1024,256]{1,0:T(8,128)(2,1)S(1)}, bf16[1024,256]{1,0:T(8,128)(2,1)S(1)}, u32[]{:S(2)}, u32[]{:S(2)}) collective-permute-start(bf16[1024,256]{1,0:T(8,128)(2,1)S(1)} %fusion.16), channel_id=1, source_target_pairs={{0,4},{1,5},{2,6},{3,7},{4,0},{5,1},{6,2},{7,3},{8,12},{9,13},{10,... | collective-permute-start | bytes 1572872 | tf_op jit(solution)/shard_map/ppermute | solution.py:30
  87.1 21.7 %collective-permute-start.14 = (bf16[1024,256]{1,0:T(8,128)(2,1)S(1)}, bf16[1024,256]{1,0:T(8,128)(2,1)S(1)}, u32[]{:S(2)}, u32[]{:S(2)}) collective-permute-start(bf16[1024,256]{1,0:T(8,128)(2,1)S(1)} %fusion.19), channel_id=1, source_target_pairs={{0,4},{1,5},{2,6},{3,7},{4,0},{5,1},{6,2},{7,3},{8,12},{9,13},{10,... | collective-permute-start | bytes 1572872 | tf_op jit(solution)/shard_map/ppermute | solution.py:30
  90.9 6.6 %copy-start.1 = (f32[1,1024,512]{2,1,0:T(8,128)S(1)}, f32[1,1024,512]{2,1,0:T(8,128)}, u32[]{:S(2)}) copy-start(f32[1,1024,512]{2,1,0:T(8,128)} %param.11) | copy-start | bytes 6291460
  91.0 6.6 %copy-start.3 = (f32[1,1024,512]{2,1,0:T(8,128)S(1)}, f32[1,1024,512]{2,1,0:T(8,128)}, u32[]{:S(2)}) copy-start(f32[1,1024,512]{2,1,0:T(8,128)} %param.12) | copy-start | bytes 6291460
  91.7 17.1 %copy-start.5 = (f32[1024,256]{1,0:T(8,128)}, f32[1024,256]{1,0:T(8,128)S(1)}, u32[]{:S(2)}) copy-start(f32[1024,256]{1,0:T(8,128)S(1)} %fusion.12) | copy-start | bytes 3145732
  100.1 20.0 %collective-permute-start.16 = (bf16[1024,256]{1,0:T(8,128)(2,1)}, bf16[1024,256]{1,0:T(8,128)(2,1)}, u32[]{:S(2)}, u32[]{:S(2)}) collective-permute-start(bf16[1024,256]{1,0:T(8,128)(2,1)} %get-tuple-element.45), channel_id=1, source_target_pairs={{0,4},{1,5},{2,6},{3,7},{4,0},{5,1},{6,2},{7,3},{8,12},{9,13},{10,... | collective-permute-start | bytes 1572872 | tf_op jit(solution)/shard_map/ppermute | solution.py:30
  110.5 18.2 %collective-permute-start.23 = (bf16[1024,256]{1,0:T(8,128)(2,1)}, bf16[1024,256]{1,0:T(8,128)(2,1)}, u32[]{:S(2)}, u32[]{:S(2)}) collective-permute-start(bf16[1024,256]{1,0:T(8,128)(2,1)} %fusion.38), channel_id=1, source_target_pairs={{0,4},{1,5},{2,6},{3,7},{4,0},{5,1},{6,2},{7,3},{8,12},{9,13},{10,... | collective-permute-start | bytes 1572872 | tf_op jit(solution)/shard_map/ppermute | solution.py:30
  115.6 52.2 %all-to-all-start.1 = ((f32[8,128,512]{2,1,0:T(8,128)}), f32[8,128,512]{2,1,0:T(8,128)}, u32[]{:S(2)}, u32[]{:S(2)}) async-start(f32[8,128,512]{2,1,0:T(8,128)} %broadcast_in_dim.4), calls=%async_computation.1 | async-start | bytes 4194304 | tf_op jit(solution)/shard_map/all_to_all | solution.py:189
  120.0 8.6 %copy-start.8 = (bf16[1024,2048]{1,0:T(8,128)(2,1)S(1)}, bf16[1024,2048]{1,0:T(8,128)(2,1)}, u32[]{:S(2)}) copy-start(bf16[1024,2048]{1,0:T(8,128)(2,1)} %copy-done.7) | copy-start | bytes 12582916
  124.0 9.3 %collective-permute-start.17 = (bf16[256,256]{1,0:T(8,128)(2,1)S(1)}, bf16[256,256]{1,0:T(8,128)(2,1)S(1)}, u32[]{:S(2)}, u32[]{:S(2)}) collective-permute-start(bf16[256,256]{1,0:T(8,128)(2,1)S(1)} %get-tuple-element.65), channel_id=1, source_target_pairs={{0,3},{1,0},{2,1},{3,2},{4,7},{5,4},{6,5},{7,6},{8,11},{9,8},{10,9... | collective-permute-start | bytes 393224 | tf_op jit(solution)/shard_map/ppermute | solution.py:30
  127.1 7.9 %collective-permute-start.19 = (bf16[256,256]{1,0:T(8,128)(2,1)S(1)}, bf16[256,256]{1,0:T(8,128)(2,1)S(1)}, u32[]{:S(2)}, u32[]{:S(2)}) collective-permute-start(bf16[256,256]{1,0:T(8,128)(2,1)S(1)} %get-tuple-element.66), channel_id=1, source_target_pairs={{0,2},{1,3},{2,0},{3,1},{4,6},{5,7},{6,4},{7,5},{8,10},{9,11},{10,... | collective-permute-start | bytes 393224 | tf_op jit(solution)/shard_map/ppermute | solution.py:30
  127.8 9.1 %collective-permute-start.18 = (bf16[256,256]{1,0:T(8,128)(2,1)S(1)}, bf16[256,256]{1,0:T(8,128)(2,1)S(1)}, u32[]{:S(2)}, u32[]{:S(2)}) collective-permute-start(bf16[256,256]{1,0:T(8,128)(2,1)S(1)} %get-tuple-element.67), channel_id=1, source_target_pairs={{0,1},{1,2},{2,3},{3,0},{4,5},{5,6},{6,7},{7,4},{8,9},{9,10},{10,1... | collective-permute-start | bytes 393224 | tf_op jit(solution)/shard_map/ppermute | solution.py:30
  137.1 6.4 %collective-permute-start.22 = (bf16[256,256]{1,0:T(8,128)(2,1)S(1)}, bf16[256,256]{1,0:T(8,128)(2,1)S(1)}, u32[]{:S(2)}, u32[]{:S(2)}) collective-permute-start(bf16[256,256]{1,0:T(8,128)(2,1)S(1)} %subtract_convert_fusion.1), channel_id=1, source_target_pairs={{0,3},{1,0},{2,1},{3,2},{4,7},{5,4},{6,5},{7,6},{8,11},{9,8},{10,9... | collective-permute-start | bytes 393224 | tf_op jit(solution)/shard_map/ppermute | solution.py:30
  137.8 8.9 %collective-permute-start.21 = (bf16[256,256]{1,0:T(8,128)(2,1)S(1)}, bf16[256,256]{1,0:T(8,128)(2,1)S(1)}, u32[]{:S(2)}, u32[]{:S(2)}) collective-permute-start(bf16[256,256]{1,0:T(8,128)(2,1)S(1)} %subtract_convert_fusion.1), channel_id=1, source_target_pairs={{0,2},{1,3},{2,0},{3,1},{4,6},{5,7},{6,4},{7,5},{8,10},{9,11},{10,... | collective-permute-start | bytes 393224 | tf_op jit(solution)/shard_map/ppermute | solution.py:30
  138.3 10.9 %collective-permute-start.20 = (bf16[256,256]{1,0:T(8,128)(2,1)S(1)}, bf16[256,256]{1,0:T(8,128)(2,1)S(1)}, u32[]{:S(2)}, u32[]{:S(2)}) collective-permute-start(bf16[256,256]{1,0:T(8,128)(2,1)S(1)} %subtract_convert_fusion.1), channel_id=1, source_target_pairs={{0,1},{1,2},{2,3},{3,0},{4,5},{5,6},{6,7},{7,4},{8,9},{9,10},{10,1... | collective-permute-start | bytes 393224 | tf_op jit(solution)/shard_map/ppermute | solution.py:30
  139.2 11.5 %collective-permute-start.26 = (bf16[256,256]{1,0:T(8,128)(2,1)S(1)}, bf16[256,256]{1,0:T(8,128)(2,1)S(1)}, u32[]{:S(2)}, u32[]{:S(2)}) collective-permute-start(bf16[256,256]{1,0:T(8,128)(2,1)S(1)} %get-tuple-element.62), channel_id=1, source_target_pairs={{0,2},{1,3},{2,0},{3,1},{4,6},{5,7},{6,4},{7,5},{8,10},{9,11},{10,... | collective-permute-start | bytes 393224 | tf_op jit(solution)/shard_map/ppermute | solution.py:30
  143.4 9.2 %collective-permute-start.25 = (bf16[256,256]{1,0:T(8,128)(2,1)S(1)}, bf16[256,256]{1,0:T(8,128)(2,1)S(1)}, u32[]{:S(2)}, u32[]{:S(2)}) collective-permute-start(bf16[256,256]{1,0:T(8,128)(2,1)S(1)} %get-tuple-element.63), channel_id=1, source_target_pairs={{0,1},{1,2},{2,3},{3,0},{4,5},{5,6},{6,7},{7,4},{8,9},{9,10},{10,1... | collective-permute-start | bytes 393224 | tf_op jit(solution)/shard_map/ppermute | solution.py:30
  143.5 9.2 %collective-permute-start.24 = (bf16[256,256]{1,0:T(8,128)(2,1)S(1)}, bf16[256,256]{1,0:T(8,128)(2,1)S(1)}, u32[]{:S(2)}, u32[]{:S(2)}) collective-permute-start(bf16[256,256]{1,0:T(8,128)(2,1)S(1)} %get-tuple-element.64), channel_id=1, source_target_pairs={{0,3},{1,0},{2,1},{3,2},{4,7},{5,4},{6,5},{7,6},{8,11},{9,8},{10,9... | collective-permute-start | bytes 393224 | tf_op jit(solution)/shard_map/ppermute | solution.py:30
  152.8 6.4 %collective-permute-start.29 = (bf16[256,256]{1,0:T(8,128)(2,1)S(1)}, bf16[256,256]{1,0:T(8,128)(2,1)S(1)}, u32[]{:S(2)}, u32[]{:S(2)}) collective-permute-start(bf16[256,256]{1,0:T(8,128)(2,1)S(1)} %subtract_convert_fusion), channel_id=1, source_target_pairs={{0,3},{1,0},{2,1},{3,2},{4,7},{5,4},{6,5},{7,6},{8,11},{9,8},{10,9... | collective-permute-start | bytes 393224 | tf_op jit(solution)/shard_map/ppermute | solution.py:30
  153.9 7.8 %collective-permute-start.28 = (bf16[256,256]{1,0:T(8,128)(2,1)S(1)}, bf16[256,256]{1,0:T(8,128)(2,1)S(1)}, u32[]{:S(2)}, u32[]{:S(2)}) collective-permute-start(bf16[256,256]{1,0:T(8,128)(2,1)S(1)} %subtract_convert_fusion), channel_id=1, source_target_pairs={{0,2},{1,3},{2,0},{3,1},{4,6},{5,7},{6,4},{7,5},{8,10},{9,11},{10,... | collective-permute-start | bytes 393224 | tf_op jit(solution)/shard_map/ppermute | solution.py:30
  153.9 8.8 %collective-permute-start.27 = (bf16[256,256]{1,0:T(8,128)(2,1)S(1)}, bf16[256,256]{1,0:T(8,128)(2,1)S(1)}, u32[]{:S(2)}, u32[]{:S(2)}) collective-permute-start(bf16[256,256]{1,0:T(8,128)(2,1)S(1)} %subtract_convert_fusion), channel_id=1, source_target_pairs={{0,1},{1,2},{2,3},{3,0},{4,5},{5,6},{6,7},{7,4},{8,9},{9,10},{10,1... | collective-permute-start | bytes 393224 | tf_op jit(solution)/shard_map/ppermute | solution.py:30
  154.9 18.8 %collective-permute-start.30 = (bf16[1024,256]{1,0:T(8,128)(2,1)}, bf16[1024,256]{1,0:T(8,128)(2,1)}, u32[]{:S(2)}, u32[]{:S(2)}) collective-permute-start(bf16[1024,256]{1,0:T(8,128)(2,1)} %fusion.22), channel_id=1, source_target_pairs={{0,4},{1,5},{2,6},{3,7},{4,0},{5,1},{6,2},{7,3},{8,12},{9,13},{10,... | collective-permute-start | bytes 1572872 | tf_op jit(solution)/shard_map/ppermute | solution.py:30
  164.2 16.9 %collective-permute-start.31 = (bf16[1024,256]{1,0:T(8,128)(2,1)}, bf16[1024,256]{1,0:T(8,128)(2,1)}, u32[]{:S(2)}, u32[]{:S(2)}) collective-permute-start(bf16[1024,256]{1,0:T(8,128)(2,1)} %fusion.25), channel_id=1, source_target_pairs={{0,4},{1,5},{2,6},{3,7},{4,0},{5,1},{6,2},{7,3},{8,12},{9,13},{10,... | collective-permute-start | bytes 1572872 | tf_op jit(solution)/shard_map/ppermute | solution.py:30
  167.8 5.9 %copy-start.14 = (bf16[1024,256]{1,0:T(8,128)(2,1)S(1)}, bf16[1024,256]{1,0:T(8,128)(2,1)}, u32[]{:S(2)}) copy-start(bf16[1024,256]{1,0:T(8,128)(2,1)} %copy-done.13) | copy-start | bytes 1572868
  167.8 5.9 %copy-start.2 = (f32[1,1024,512]{2,1,0:T(8,128)S(1)}, f32[1,1024,512]{2,1,0:T(8,128)}, u32[]{:S(2)}) copy-start(f32[1,1024,512]{2,1,0:T(8,128)} %param.11) | copy-start | bytes 6291460
  167.8 5.9 %copy-start.4 = (f32[1,1024,512]{2,1,0:T(8,128)S(1)}, f32[1,1024,512]{2,1,0:T(8,128)}, u32[]{:S(2)}) copy-start(f32[1,1024,512]{2,1,0:T(8,128)} %param.12) | copy-start | bytes 6291460
  167.8 5.9 %copy-start.10 = (f32[1024,256]{1,0:T(8,128)S(1)}, f32[1024,256]{1,0:T(8,128)}, u32[]{:S(2)}) copy-start(f32[1024,256]{1,0:T(8,128)} %get-tuple-element.69) | copy-start | bytes 3145732
  167.8 5.9 %copy-start.12 = (f32[1024,256]{1,0:T(8,128)S(1)}, f32[1024,256]{1,0:T(8,128)}, u32[]{:S(2)}) copy-start(f32[1024,256]{1,0:T(8,128)} %fusion.10) | copy-start | bytes 3145732
  173.7 7.5 %copy-start.6 = (f32[1024,256]{1,0:T(8,128)S(1)}, f32[1024,256]{1,0:T(8,128)}, u32[]{:S(2)}) copy-start(f32[1024,256]{1,0:T(8,128)} %copy-done.5) | copy-start | bytes 3145732
  173.7 7.5 %copy-start.11 = (f32[1024,256]{1,0:T(8,128)S(1)}, f32[1024,256]{1,0:T(8,128)}, u32[]{:S(2)}) copy-start(f32[1024,256]{1,0:T(8,128)} %fusion.8) | copy-start | bytes 3145732
  (2 other events, 4.7 us)

commit v6 on v5

--- a/solution.py
+++ b/solution.py
@@ -144,7 +144,6 @@
     teacher = f32(targets[0])
     part = {dx: bf16(dot(blocks[dx], both)) for dx in (1, 2, 3)}
     arrived = send_parts(part)
-    blocks[0], part[1], part[2], part[3] = tie(blocks[0], part[1], part[2], part[3])
     own = dot(blocks[0], both)
     own, *blocks = tie(own, *blocks)
     outputs = add_parts(own, arrived)
@@ -213,10 +212,9 @@
     got_b = shift(away_b, 1, 0)
     row_a, row_b, away_b = tie(row_a, row_b, away_b)
     own_a, own_b = near(row_a), near(row_b)
-    own_a, own_b, frag_params, momentum_out = tie(own_a, own_b, frag_params, momentum_out)
     grad_a = (own_a + f32(got_a)) / tok_all
     total_a = update_a + adam_update(*state_a, grad_a)[3]
-    total_a, own_b = tie(total_a, own_b)
+    total_a, own_b, frag_params, momentum_out = tie(total_a, own_b, frag_params, momentum_out)
     grad_b = (own_b + f32(got_b)) / tok_all
     total_b = update_b + adam_update(*state_b, grad_b)[3]
     block_shift = jnp.concatenate([total_a, total_b], axis=1)

time: 187 us -> 185 us (0.989)
  waiting for transfers between devices: 62 us -> 55.9 us
  starting transfers between devices: 64.9 us -> 70.4 us
  other arithmetic: 19.8 us -> 16.3 us
    ppermute x31, waiting for transfers between devices: 62 us -> 55.9 us  [shift(): return lax.ppermute(value, 'fsdp', pairs)]
    ppermute x31, starting transfers between devices: 54 us -> 59.5 us  [shift(): return lax.ppermute(value, 'fsdp', pairs)]
    add x1 -> x0, other arithmetic: 2.79 us -> none  [shards(): total_a = update_a + adam_update(*state_a, grad_a)[3]]
  transfers between devices with their start and end apart: 34 -> 34, of which waited for: 22 -> 20; matrix products, arithmetic and copies ran while one was open for 24% -> 23% of each run, Pallas kernels for 3% -> 3%
where the time goes in v6:
time: 185 us; the launch traced here: 183 us
  starting transfers between devices  70.4 us (38%)
  waiting for transfers between devices  55.9 us (30%)
  matrix products  29.1 us (16%)
  other arithmetic  16.3 us (9%)
  Pallas kernels  8.48 us (5%)
  local copies, waits for them, and re-layouts  1.88 us (1%)
    ppermute x31, starting transfers between devices, shift(): return lax.ppermute(value, 'fsdp', pairs)  59.5 us
    ppermute x31, waiting for transfers between devices, shift(): return lax.ppermute(value, 'fsdp', pairs)  55.9 us
    dot_general x6, matrix products, dot(): return jnp.dot(a, b, preferred_element_type=jnp.float32)  16.9 us
    dot_general x8, matrix products, dot_t(): lax.dot_general(a, b, (((0,), (0,)), ((), ())), preferred_element_type=jn...  12.2 us
    pallas_call x4, Pallas kernels, pick(): pl.pallas_call(functools.partial(pick_kernel, dx), out_shape=jax.ShapeDty...  8.48 us
    add x1, other arithmetic, outer_nesterov(): momentum_new = 0.9 * momentum + delta  5.85 us
    all_to_all x1, starting transfers between devices, shards(): lax.all_to_all(frag_inner[0].reshape(mates, frag_rows, -1), 'rep', 0, 0,...  4.47 us
    all_to_all x1, starting transfers between devices, shards(): lax.all_to_all(jnp.broadcast_to(piece_sum[None], (mates, *piece_sum.shape...  4.46 us
  transfers between devices with their start and end apart: 34, of which 20 were waited for; matrix products, arithmetic and copies ran while one was open for 23% of the time, Pallas kernels for 3%

profile of v6, /device:TPU:0, one launch (start us, length us, event | category | flops | bytes accessed | tf_op | source)
XLA Modules:
  0.0 183.2 jit_solution(1607044027740767792)
XLA Ops:
  0.6 2.1 %shard_map.106 = bf16[256,2048]{1,0:T(8,128)(2,1)} custom-call(bf16[256,8192]{1,0:T(8,128)(2,1)} %bitcast.81), custom_call_target="tpu_custom_call" | custom-call | bytes 2097152 | tf_op jit(solution)/shard_map/pallas_call | solution.py:86
  2.8 3.2 %collective-permute-start.3 = (bf16[256,2048]{1,0:T(8,128)(2,1)}, bf16[256,2048]{1,0:T(8,128)(2,1)}, u32[]{:S(2)}, u32[]{:S(2)}) collective-permute-start(bf16[256,2048]{1,0:T(8,128)(2,1)} %shard_map.106), channel_id=1, source_target_pairs={{0,2},{1,3},{2,0},{3,1},{4,6},{5,7},{6,4},{7,5},{8,10},{9,11},{10,... | collective-permute-start | bytes 3145736 | tf_op jit(solution)/shard_map/ppermute | solution.py:30
  5.9 2.1 %shard_map.103 = bf16[256,2048]{1,0:T(8,128)(2,1)} custom-call(bf16[256,8192]{1,0:T(8,128)(2,1)} %bitcast.82), custom_call_target="tpu_custom_call" | custom-call | bytes 2097152 | tf_op jit(solution)/shard_map/pallas_call | solution.py:86
  9.2 3.9 %collective-permute-start = (bf16[1024,512]{1,0:T(8,128)(2,1)}, bf16[1024,512]{1,0:T(8,128)(2,1)}, u32[]{:S(2)}, u32[]{:S(2)}) collective-permute-start(bf16[1024,512]{1,0:T(8,128)(2,1)} %convert_element_type.105), channel_id=1, source_target_pairs={{0,4},{1,5},{2,6},{3,7},{4,0},{5,1},{6,2},{7,3},{8,12},{9,13},{10,... | collective-permute-start | bytes 3145736 | tf_op jit(solution)/shard_map/ppermute | solution.py:30
  13.0 2.1 %shard_map.105 = bf16[256,2048]{1,0:T(8,128)(2,1)} custom-call(bf16[256,8192]{1,0:T(8,128)(2,1)} %bitcast.83), custom_call_target="tpu_custom_call" | custom-call | bytes 2097152 | tf_op jit(solution)/shard_map/pallas_call | solution.py:86
  15.8 2.6 %collective-permute-start.2 = (bf16[256,2048]{1,0:T(8,128)(2,1)}, bf16[256,2048]{1,0:T(8,128)(2,1)}, u32[]{:S(2)}, u32[]{:S(2)}) collective-permute-start(bf16[256,2048]{1,0:T(8,128)(2,1)} %shard_map.103), channel_id=1, source_target_pairs={{0,3},{1,0},{2,1},{3,2},{4,7},{5,4},{6,5},{7,6},{8,11},{9,8},{10,9... | collective-permute-start | bytes 3145736 | tf_op jit(solution)/shard_map/ppermute | solution.py:30
  18.4 4.5 %all-to-all-start = ((bf16[8,128,512]{2,1,0:T(8,128)(2,1)}), bf16[8,128,512]{2,1,0:T(8,128)(2,1)}, u32[]{:S(2)}, u32[]{:S(2)}) async-start(bf16[8,128,512]{2,1,0:T(8,128)(2,1)} %bitcast.4), calls=%async_computation | async-start | bytes 2097152 | tf_op jit(solution)/shard_map/all_to_all | solution.py:137
  22.9 2.2 %shard_map.104 = bf16[256,2048]{1,0:T(8,128)(2,1)} custom-call(bf16[256,8192]{1,0:T(8,128)(2,1)} %bitcast.84), custom_call_target="tpu_custom_call" | custom-call | bytes 2097152 | tf_op jit(solution)/shard_map/pallas_call | solution.py:86
  25.3 5.5 %collective-permute-done.3 = bf16[256,2048]{1,0:T(8,128)(2,1)} collective-permute-done((bf16[256,2048]{1,0:T(8,128)(2,1)}, bf16[256,2048]{1,0:T(8,128)(2,1)}, u32[]{:S(2)}, u32[]{:S(2)}) %collective-permute-start.3) | collective-permute-done | bytes 1048608 | tf_op jit(solution)/shard_map/ppermute | solution.py:30
  30.8 5.5 %collective-permute-done = bf16[1024,512]{1,0:T(8,128)(2,1)} collective-permute-done((bf16[1024,512]{1,0:T(8,128)(2,1)}, bf16[1024,512]{1,0:T(8,128)(2,1)}, u32[]{:S(2)}, u32[]{:S(2)}) %collective-permute-start) | collective-permute-done | bytes 1048608 | tf_op jit(solution)/shard_map/ppermute | solution.py:30
  36.2 2.6 %fusion.28 = bf16[256,512]{0,1:T(8,128)(2,1)S(1)} fusion(bf16[256,2048]{1,0:T(8,128)(2,1)} %collective-permute-done.3, bf16[1024,512]{1,0:T(8,128)(2,1)} %collective-permute-done, bf16[1024,512]{1,0:T(8,128)(2,1)} %convert_element_type.105), kind=kOutput, calls=%fused_computation.33 | convolution fusion | flops 541196288 | bytes 3407872 | tf_op jit(solution)/shard_map/dot_general | solution.py:42
  39.6 13.6 %collective-permute-done.1 = bf16[256,2048]{1,0:T(8,128)(2,1)} collective-permute-done((bf16[256,2048]{1,0:T(8,128)(2,1)}, bf16[256,2048]{1,0:T(8,128)(2,1)}, u32[]{:S(2)}, u32[]{:S(2)}) %collective-permute-start.1) | collective-permute-done | bytes 1048608 | tf_op jit(solution)/shard_map/ppermute | solution.py:30
  53.4 2.8 %convolution_convert_fusion.3 = bf16[256,512]{0,1:T(8,128)(2,1)S(1)} fusion(bf16[256,2048]{1,0:T(8,128)(2,1)} %collective-permute-done.2, bf16[1024,512]{1,0:T(8,128)(2,1)} %collective-permute-done, bf16[1024,512]{1,0:T(8,128)(2,1)} %convert_element_type.105), kind=kOutput, calls=%fused_computation.31 | convolution fusion | flops 541196288 | bytes 3407872 | tf_op jit(solution)/shard_map/dot_general | solution.py:42
  57.7 2.8 %convolution_convert_fusion.4 = bf16[256,512]{0,1:T(8,128)(2,1)S(1)} fusion(bf16[256,2048]{1,0:T(8,128)(2,1)} %collective-permute-done.1, bf16[1024,512]{1,0:T(8,128)(2,1)} %collective-permute-done, bf16[1024,512]{1,0:T(8,128)(2,1)} %convert_element_type.105), kind=kOutput, calls=%fused_computation.32 | convolution fusion | flops 541196288 | bytes 3407872 | tf_op jit(solution)/shard_map/dot_general | solution.py:42
  60.5 1.9 %collective-permute-start.4 = (bf16[256,512]{0,1:T(8,128)(2,1)S(1)}, bf16[256,512]{0,1:T(8,128)(2,1)S(1)}, u32[]{:S(2)}, u32[]{:S(2)}) collective-permute-start(bf16[256,512]{0,1:T(8,128)(2,1)S(1)} %convolution_convert_fusion.4), channel_id=1, source_target_pairs={{0,3},{1,0},{2,1},{3,2},{4,7},{5,4},{6,5},{7,6},{8,11},{9,8},{10,9... | collective-permute-start | bytes 786440 | tf_op jit(solution)/shard_map/ppermute | solution.py:30
  62.3 2.3 %convolution_bitcast_fusion = f32[256,512]{0,1:T(8,128)S(1)} fusion(bf16[256,2048]{1,0:T(8,128)(2,1)S(1)} %copy-done.5, bf16[1024,512]{1,0:T(8,128)(2,1)} %collective-permute-done, bf16[1024,512]{1,0:T(8,128)(2,1)} %convert_element_type.105), kind=kOutput, calls=%fused_computation.29 | convolution fusion | flops 541065216 | bytes 3670016 | tf_op jit(solution)/shard_map/dot_general | solution.py:42
  66.0 2.0 %collective-permute-start.15 = (f32[128,512]{1,0:T(8,128)S(1)}, f32[128,512]{1,0:T(8,128)S(1)}, u32[]{:S(2)}, u32[]{:S(2)}) collective-permute-start(f32[128,512]{1,0:T(8,128)S(1)} %convert_reduce_fusion), channel_id=1, source_target_pairs={{0,64},{8,72},{16,80},{24,88},{32,96},{40,104},{48,112},{56,120},{... | collective-permute-start | bytes 786440 | tf_op jit(solution)/shard_map/ppermute | solution.py:142
  68.5 3.1 %collective-permute-start.9 = (bf16[256,256]{0,1:T(8,128)(2,1)S(1)}, bf16[256,256]{0,1:T(8,128)(2,1)S(1)}, u32[]{:S(2)}, u32[]{:S(2)}) collective-permute-start(bf16[256,256]{0,1:T(8,128)(2,1)S(1)} %get-tuple-element.54), channel_id=1, source_target_pairs={{0,3},{1,0},{2,1},{3,2},{4,7},{5,4},{6,5},{7,6},{8,11},{9,8},{10,9... | collective-permute-start | bytes 393224 | tf_op jit(solution)/shard_map/ppermute | solution.py:30
  72.7 2.1 %pad_maximum_fusion = bf16[1024,2048]{1,0:T(8,128)(2,1)S(1)} fusion(bf16[256,2048]{1,0:T(8,128)(2,1)} %collective-permute-done.2, bf16[256,2048]{1,0:T(8,128)(2,1)} %collective-permute-done.3, bf16[256,2048]{1,0:T(8,128)(2,1)} %collective-permute-done.1, bf16[256,2048]{1,0:T(8,128)(2,1)S(1)} %copy-done.5), kind=kLoop, calls=%fused_computation | loop fusion | flops 16777216 | bytes 8388608 | tf_op jit(solution)/shard_map/concatenate | solution.py:152
  74.9 2.7 %collective-permute-start.12 = (bf16[256,256]{0,1:T(8,128)(2,1)S(1)}, bf16[256,256]{0,1:T(8,128)(2,1)S(1)}, u32[]{:S(2)}, u32[]{:S(2)}) collective-permute-start(bf16[256,256]{0,1:T(8,128)(2,1)S(1)} %get-tuple-element.53), channel_id=1, source_target_pairs={{0,3},{1,0},{2,1},{3,2},{4,7},{5,4},{6,5},{7,6},{8,11},{9,8},{10,9... | collective-permute-start | bytes 393224 | tf_op jit(solution)/shard_map/ppermute | solution.py:30
  77.6 1.8 collective-permute-start.11
  81.4 4.0 %collective-permute-start.13 = (bf16[1024,256]{1,0:T(8,128)(2,1)S(1)}, bf16[1024,256]{1,0:T(8,128)(2,1)S(1)}, u32[]{:S(2)}, u32[]{:S(2)}) collective-permute-start(bf16[1024,256]{1,0:T(8,128)(2,1)S(1)} %fusion.16), channel_id=1, source_target_pairs={{0,4},{1,5},{2,6},{3,7},{4,0},{5,1},{6,2},{7,3},{8,12},{9,13},{10,... | collective-permute-start | bytes 1572872 | tf_op jit(solution)/shard_map/ppermute | solution.py:30
  86.4 4.1 %collective-permute-start.14 = (bf16[1024,256]{1,0:T(8,128)(2,1)S(1)}, bf16[1024,256]{1,0:T(8,128)(2,1)S(1)}, u32[]{:S(2)}, u32[]{:S(2)}) collective-permute-start(bf16[1024,256]{1,0:T(8,128)(2,1)S(1)} %fusion.19), channel_id=1, source_target_pairs={{0,4},{1,5},{2,6},{3,7},{4,0},{5,1},{6,2},{7,3},{8,12},{9,13},{10,... | collective-permute-start | bytes 1572872 | tf_op jit(solution)/shard_map/ppermute | solution.py:30
  91.4 6.8 %collective-permute-done.13 = bf16[1024,256]{1,0:T(8,128)(2,1)S(1)} collective-permute-done((bf16[1024,256]{1,0:T(8,128)(2,1)S(1)}, bf16[1024,256]{1,0:T(8,128)(2,1)S(1)}, u32[]{:S(2)}, u32[]{:S(2)}) %collective-permute-start.13) | collective-permute-done | bytes 524320 | tf_op jit(solution)/shard_map/ppermute | solution.py:30
  98.3 2.5 %fusion.37 = (bf16[1024,256]{1,0:T(8,128)(2,1)}, f32[1024,256]{1,0:T(8,128)}) fusion(f32[1,1024,512]{2,1,0:T(8,128)S(1)} %copy-done, bf16[1024,256]{1,0:T(8,128)(2,1)S(1)} %collective-permute-done.13, f32[1,1024,512]{2,1,0:T(8,128)S(1)} %copy-done.8, f32[1,1024,512]{2,1,0:T(8,128)S(1)} %copy-done.11, bf16[1024,256]{0,1:T(8,128)(2,1)S(1)} %pad_maximum_fusion.2, ...), kind=kOutput, calls=%fused_computation.54 | convolution fusion | flops 541327360 | bytes 7864320 | tf_op jit(solution)/shard_map/dot_general | solution.py:50
  100.8 3.5 %collective-permute-start.16 = (bf16[1024,256]{1,0:T(8,128)(2,1)}, bf16[1024,256]{1,0:T(8,128)(2,1)}, u32[]{:S(2)}, u32[]{:S(2)}) collective-permute-start(bf16[1024,256]{1,0:T(8,128)(2,1)} %get-tuple-element.41), channel_id=1, source_target_pairs={{0,4},{1,5},{2,6},{3,7},{4,0},{5,1},{6,2},{7,3},{8,12},{9,13},{10,... | collective-permute-start | bytes 1572872 | tf_op jit(solution)/shard_map/ppermute | solution.py:30
  104.3 5.1 %collective-permute-done.14 = bf16[1024,256]{1,0:T(8,128)(2,1)S(1)} collective-permute-done((bf16[1024,256]{1,0:T(8,128)(2,1)S(1)}, bf16[1024,256]{1,0:T(8,128)(2,1)S(1)}, u32[]{:S(2)}, u32[]{:S(2)}) %collective-permute-start.14) | collective-permute-done | bytes 524320 | tf_op jit(solution)/shard_map/ppermute | solution.py:30
  110.4 3.6 %collective-permute-start.23 = (bf16[1024,256]{1,0:T(8,128)(2,1)S(1)}, bf16[1024,256]{1,0:T(8,128)(2,1)}, u32[]{:S(2)}, u32[]{:S(2)}) collective-permute-start(bf16[1024,256]{1,0:T(8,128)(2,1)S(1)} %fusion.38), channel_id=1, source_target_pairs={{0,4},{1,5},{2,6},{3,7},{4,0},{5,1},{6,2},{7,3},{8,12},{9,13},{10,... | collective-permute-start | bytes 1572872 | tf_op jit(solution)/shard_map/ppermute | solution.py:30
  114.0 1.6 broadcast_in_dim.4
  115.6 4.5 %all-to-all-start.1 = ((f32[8,128,512]{2,1,0:T(8,128)}), f32[8,128,512]{2,1,0:T(8,128)}, u32[]{:S(2)}, u32[]{:S(2)}) async-start(f32[8,128,512]{2,1,0:T(8,128)} %broadcast_in_dim.4), calls=%async_computation.1 | async-start | bytes 4194304 | tf_op jit(solution)/shard_map/all_to_all | solution.py:188
  120.8 4.1 %convolution_convert_fusion.1 = bf16[1024,256]{0,1:T(8,128)(2,1)S(1)} fusion(bf16[1024,2048]{1,0:T(8,128)(2,1)} %copy-done.3, bf16[1024,256]{1,0:T(8,128)(2,1)} %collective-permute-done.16, bf16[1024,256]{1,0:T(8,128)(2,1)} %get-tuple-element.41), kind=kOutput, calls=%fused_computation.28 | convolution fusion | flops 1076101120 | bytes 5767168 | tf_op jit(solution)/shard_map/dot_general | solution.py:42
  125.0 2.0 %collective-permute-start.17 = (bf16[256,256]{0,1:T(8,128)(2,1)S(1)}, bf16[256,256]{0,1:T(8,128)(2,1)S(1)}, u32[]{:S(2)}, u32[]{:S(2)}) collective-permute-start(bf16[256,256]{0,1:T(8,128)(2,1)S(1)} %get-tuple-element.59), channel_id=1, source_target_pairs={{0,3},{1,0},{2,1},{3,2},{4,7},{5,4},{6,5},{7,6},{8,11},{9,8},{10,9... | collective-permute-start | bytes 393224 | tf_op jit(solution)/shard_map/ppermute | solution.py:30
  127.9 2.3 %convolution_convert_fusion = bf16[1024,256]{0,1:T(8,128)(2,1)S(1)} fusion(bf16[1024,2048]{1,0:T(8,128)(2,1)S(1)} %copy-done.4, bf16[1024,256]{1,0:T(8,128)(2,1)} %collective-permute-done.23, bf16[1024,256]{1,0:T(8,128)(2,1)S(1)} %fusion.38), kind=kOutput, calls=%fused_computation.27 | convolution fusion | flops 1076101120 | bytes 5767168 | tf_op jit(solution)/shard_map/dot_general | solution.py:42
  130.3 2.0 %collective-permute-done.17 = bf16[256,256]{0,1:T(8,128)(2,1)S(1)} collective-permute-done((bf16[256,256]{0,1:T(8,128)(2,1)S(1)}, bf16[256,256]{0,1:T(8,128)(2,1)S(1)}, u32[]{:S(2)}, u32[]{:S(2)}) %collective-permute-start.17) | collective-permute-done | bytes 131104 | tf_op jit(solution)/shard_map/ppermute | solution.py:30
  132.2 2.4 %collective-permute-done.19 = bf16[256,256]{0,1:T(8,128)(2,1)S(1)} collective-permute-done((bf16[256,256]{0,1:T(8,128)(2,1)S(1)}, bf16[256,256]{0,1:T(8,128)(2,1)S(1)}, u32[]{:S(2)}, u32[]{:S(2)}) %collective-permute-start.19) | collective-permute-done | bytes 131104 | tf_op jit(solution)/shard_map/ppermute | solution.py:30
  138.1 4.2 %collective-permute-start.26 = (bf16[256,256]{0,1:T(8,128)(2,1)S(1)}, bf16[256,256]{0,1:T(8,128)(2,1)S(1)}, u32[]{:S(2)}, u32[]{:S(2)}) collective-permute-start(bf16[256,256]{0,1:T(8,128)(2,1)S(1)} %get-tuple-element.56), channel_id=1, source_target_pairs={{0,2},{1,3},{2,0},{3,1},{4,6},{5,7},{6,4},{7,5},{8,10},{9,11},{10,... | collective-permute-start | bytes 393224 | tf_op jit(solution)/shard_map/ppermute | solution.py:30
  142.5 3.1 %collective-permute-start.24 = (bf16[256,256]{0,1:T(8,128)(2,1)S(1)}, bf16[256,256]{0,1:T(8,128)(2,1)S(1)}, u32[]{:S(2)}, u32[]{:S(2)}) collective-permute-start(bf16[256,256]{0,1:T(8,128)(2,1)S(1)} %get-tuple-element.58), channel_id=1, source_target_pairs={{0,3},{1,0},{2,1},{3,2},{4,7},{5,4},{6,5},{7,6},{8,11},{9,8},{10,9... | collective-permute-start | bytes 393224 | tf_op jit(solution)/shard_map/ppermute | solution.py:30
  145.6 2.5 %collective-permute-done.20 = bf16[256,256]{0,1:T(8,128)(2,1)S(1)} collective-permute-done((bf16[256,256]{0,1:T(8,128)(2,1)S(1)}, bf16[256,256]{0,1:T(8,128)(2,1)S(1)}, u32[]{:S(2)}, u32[]{:S(2)}) %collective-permute-start.20) | collective-permute-done | bytes 131104 | tf_op jit(solution)/shard_map/ppermute | solution.py:30
  153.3 3.0 %collective-permute-start.30 = (bf16[1024,256]{1,0:T(8,128)(2,1)S(1)}, bf16[1024,256]{1,0:T(8,128)(2,1)S(1)}, u32[]{:S(2)}, u32[]{:S(2)}) collective-permute-start(bf16[1024,256]{1,0:T(8,128)(2,1)S(1)} %fusion.22), channel_id=1, source_target_pairs={{0,4},{1,5},{2,6},{3,7},{4,0},{5,1},{6,2},{7,3},{8,12},{9,13},{10,... | collective-permute-start | bytes 1572872 | tf_op jit(solution)/shard_map/ppermute | solution.py:30
  157.5 2.2 %collective-permute-done.28 = bf16[256,256]{0,1:T(8,128)(2,1)S(1)} collective-permute-done((bf16[256,256]{0,1:T(8,128)(2,1)S(1)}, bf16[256,256]{0,1:T(8,128)(2,1)S(1)}, u32[]{:S(2)}, u32[]{:S(2)}) %collective-permute-start.28) | collective-permute-done | bytes 131104 | tf_op jit(solution)/shard_map/ppermute | solution.py:30
  160.7 1.6 fusion.25
  162.3 2.3 %collective-permute-start.31 = (bf16[1024,256]{1,0:T(8,128)(2,1)}, bf16[1024,256]{1,0:T(8,128)(2,1)}, u32[]{:S(2)}, u32[]{:S(2)}) collective-permute-start(bf16[1024,256]{1,0:T(8,128)(2,1)} %fusion.25), channel_id=1, source_target_pairs={{0,4},{1,5},{2,6},{3,7},{4,0},{5,1},{6,2},{7,3},{8,12},{9,13},{10,... | collective-permute-start | bytes 1572872 | tf_op jit(solution)/shard_map/ppermute | solution.py:30
  164.7 1.8 fusion.8
  166.4 3.2 %collective-permute-done.30 = bf16[1024,256]{1,0:T(8,128)(2,1)S(1)} collective-permute-done((bf16[1024,256]{1,0:T(8,128)(2,1)S(1)}, bf16[1024,256]{1,0:T(8,128)(2,1)S(1)}, u32[]{:S(2)}, u32[]{:S(2)}) %collective-permute-start.30) | collective-permute-done | bytes 524320 | tf_op jit(solution)/shard_map/ppermute | solution.py:30
  169.7 3.2 %add_add_fusion.1 = f32[1024,256]{1,0:T(8,128)} fusion(bf16[1024,256]{1,0:T(8,128)(2,1)S(1)} %collective-permute-done.30, f32[1,1024,512]{2,1,0:T(8,128)S(1)} %copy-done, f32[1024,256]{1,0:T(8,128)S(1)} %copy-done.19, bf16[1024,256]{1,0:T(8,128)(2,1)S(1)} %copy-done.18, f32[1,1024,512]{2,1,0:T(8,128)S(1)} %copy-done.9, f32[1,1024,512]{2,1,0:T(8,128)S(1)} %copy-done.12, ...), kind=kOutput, calls=%fused_computation.51 | convolution fusion | flops 544997376 | bytes 8912896 | tf_op jit(solution)/shard_map/dot_general | solution.py:50
  172.9 5.8 %multiply_add_fusion = (f32[1024,512]{1,0:T(8,128)}, f32[1024,512]{1,0:T(8,128)}) fusion(f32[1024,512]{1,0:T(8,128)} %param.15, f32[1024,512]{1,0:T(8,128)} %param.13, f32[8,128,512]{2,1,0:T(8,128)} %all-to-all-done.1), kind=kLoop, calls=%fused_computation.5 | loop fusion | flops 3670016 | bytes 10485760 | tf_op jit(solution)/shard_map/add | solution.py:22
  178.8 2.7 %add_add_fusion = f32[1024,256]{1,0:T(8,128)S(1)} fusion(f32[1024,256]{1,0:T(8,128)S(1)} %copy-done.14, bf16[1024,256]{1,0:T(8,128)(2,1)} %collective-permute-done.31, f32[1,1024,512]{2,1,0:T(8,128)S(1)} %copy-done, f32[1024,256]{1,0:T(8,128)S(1)} %copy-done.2, bf16[1024,256]{1,0:T(8,128)(2,1)S(1)} %copy-done.7, f32[1,1024,512]{2,1,0:T(8,128)S(1)} %copy-done.10, ...), kind=kLoop, calls=%fused_computation.50 | loop fusion | flops 8126464 | bytes 7340032 | tf_op jit(solution)/shard_map/add | solution.py:219
  181.6 1.6 maximum_bitcast_fusion
  (99 shorter events, 25.2 us)
Async XLA Ops:
  2.7 5.3 %copy-start = (f32[1,1024,512]{2,1,0:T(8,128)S(1)}, f32[1,1024,512]{2,1,0:T(8,128)}, u32[]{:S(2)}) copy-start(f32[1,1024,512]{2,1,0:T(8,128)} %param.10) | copy-start | bytes 6291460
  2.8 28.0 %collective-permute-start.3 = (bf16[256,2048]{1,0:T(8,128)(2,1)}, bf16[256,2048]{1,0:T(8,128)(2,1)}, u32[]{:S(2)}, u32[]{:S(2)}) collective-permute-start(bf16[256,2048]{1,0:T(8,128)(2,1)} %shard_map.106), channel_id=1, source_target_pairs={{0,2},{1,3},{2,0},{3,1},{4,6},{5,7},{6,4},{7,5},{8,10},{9,11},{10,... | collective-permute-start | bytes 3145736 | tf_op jit(solution)/shard_map/ppermute | solution.py:30
  9.2 27.1 %collective-permute-start = (bf16[1024,512]{1,0:T(8,128)(2,1)}, bf16[1024,512]{1,0:T(8,128)(2,1)}, u32[]{:S(2)}, u32[]{:S(2)}) collective-permute-start(bf16[1024,512]{1,0:T(8,128)(2,1)} %convert_element_type.105), channel_id=1, source_target_pairs={{0,4},{1,5},{2,6},{3,7},{4,0},{5,1},{6,2},{7,3},{8,12},{9,13},{10,... | collective-permute-start | bytes 3145736 | tf_op jit(solution)/shard_map/ppermute | solution.py:30
  15.1 38.0 %collective-permute-start.1 = (bf16[256,2048]{1,0:T(8,128)(2,1)}, bf16[256,2048]{1,0:T(8,128)(2,1)}, u32[]{:S(2)}, u32[]{:S(2)}) collective-permute-start(bf16[256,2048]{1,0:T(8,128)(2,1)} %shard_map.105), channel_id=1, source_target_pairs={{0,1},{1,2},{2,3},{3,0},{4,5},{5,6},{6,7},{7,4},{8,9},{9,10},{10,1... | collective-permute-start | bytes 3145736 | tf_op jit(solution)/shard_map/ppermute | solution.py:30
  15.8 37.6 %collective-permute-start.2 = (bf16[256,2048]{1,0:T(8,128)(2,1)}, bf16[256,2048]{1,0:T(8,128)(2,1)}, u32[]{:S(2)}, u32[]{:S(2)}) collective-permute-start(bf16[256,2048]{1,0:T(8,128)(2,1)} %shard_map.103), channel_id=1, source_target_pairs={{0,3},{1,0},{2,1},{3,2},{4,7},{5,4},{6,5},{7,6},{8,11},{9,8},{10,9... | collective-permute-start | bytes 3145736 | tf_op jit(solution)/shard_map/ppermute | solution.py:30
  18.4 21.1 %all-to-all-start = ((bf16[8,128,512]{2,1,0:T(8,128)(2,1)}), bf16[8,128,512]{2,1,0:T(8,128)(2,1)}, u32[]{:S(2)}, u32[]{:S(2)}) async-start(bf16[8,128,512]{2,1,0:T(8,128)(2,1)} %bitcast.4), calls=%async_computation | async-start | bytes 2097152 | tf_op jit(solution)/shard_map/all_to_all | solution.py:137
  38.8 29.2 %collective-permute-start.6 = (bf16[256,512]{0,1:T(8,128)(2,1)S(1)}, bf16[256,512]{0,1:T(8,128)(2,1)S(1)}, u32[]{:S(2)}, u32[]{:S(2)}) collective-permute-start(bf16[256,512]{0,1:T(8,128)(2,1)S(1)} %fusion.28), channel_id=1, source_target_pairs={{0,2},{1,3},{2,0},{3,1},{4,6},{5,7},{6,4},{7,5},{8,10},{9,11},{10,... | collective-permute-start | bytes 786440 | tf_op jit(solution)/shard_map/ppermute | solution.py:30
  56.2 6.2 %copy-start.5 = (bf16[256,2048]{1,0:T(8,128)(2,1)S(1)}, bf16[256,2048]{1,0:T(8,128)(2,1)}, u32[]{:S(2)}) copy-start(bf16[256,2048]{1,0:T(8,128)(2,1)} %shard_map.104) | copy-start | bytes 3145732
  56.2 11.9 %collective-permute-start.5 = (bf16[256,512]{0,1:T(8,128)(2,1)S(1)}, bf16[256,512]{0,1:T(8,128)(2,1)S(1)}, u32[]{:S(2)}, u32[]{:S(2)}) collective-permute-start(bf16[256,512]{0,1:T(8,128)(2,1)S(1)} %convolution_convert_fusion.3), channel_id=1, source_target_pairs={{0,1},{1,2},{2,3},{3,0},{4,5},{5,6},{6,7},{7,4},{8,9},{9,10},{10,1... | collective-permute-start | bytes 786440 | tf_op jit(solution)/shard_map/ppermute | solution.py:30
  60.5 7.8 %collective-permute-start.4 = (bf16[256,512]{0,1:T(8,128)(2,1)S(1)}, bf16[256,512]{0,1:T(8,128)(2,1)S(1)}, u32[]{:S(2)}, u32[]{:S(2)}) collective-permute-start(bf16[256,512]{0,1:T(8,128)(2,1)S(1)} %convolution_convert_fusion.4), channel_id=1, source_target_pairs={{0,3},{1,0},{2,1},{3,2},{4,7},{5,4},{6,5},{7,6},{8,11},{9,8},{10,9... | collective-permute-start | bytes 786440 | tf_op jit(solution)/shard_map/ppermute | solution.py:30
  66.0 38.3 %collective-permute-start.15 = (f32[128,512]{1,0:T(8,128)S(1)}, f32[128,512]{1,0:T(8,128)S(1)}, u32[]{:S(2)}, u32[]{:S(2)}) collective-permute-start(f32[128,512]{1,0:T(8,128)S(1)} %convert_reduce_fusion), channel_id=1, source_target_pairs={{0,64},{8,72},{16,80},{24,88},{32,96},{40,104},{48,112},{56,120},{... | collective-permute-start | bytes 786440 | tf_op jit(solution)/shard_map/ppermute | solution.py:142
  68.5 9.1 %collective-permute-start.9 = (bf16[256,256]{0,1:T(8,128)(2,1)S(1)}, bf16[256,256]{0,1:T(8,128)(2,1)S(1)}, u32[]{:S(2)}, u32[]{:S(2)}) collective-permute-start(bf16[256,256]{0,1:T(8,128)(2,1)S(1)} %get-tuple-element.54), channel_id=1, source_target_pairs={{0,3},{1,0},{2,1},{3,2},{4,7},{5,4},{6,5},{7,6},{8,11},{9,8},{10,9... | collective-permute-start | bytes 393224 | tf_op jit(solution)/shard_map/ppermute | solution.py:30
  71.6 7.8 %collective-permute-start.8 = (bf16[256,256]{0,1:T(8,128)(2,1)S(1)}, bf16[256,256]{0,1:T(8,128)(2,1)S(1)}, u32[]{:S(2)}, u32[]{:S(2)}) collective-permute-start(bf16[256,256]{0,1:T(8,128)(2,1)S(1)} %get-tuple-element.54), channel_id=1, source_target_pairs={{0,2},{1,3},{2,0},{3,1},{4,6},{5,7},{6,4},{7,5},{8,10},{9,11},{10,... | collective-permute-start | bytes 393224 | tf_op jit(solution)/shard_map/ppermute | solution.py:30
  72.1 8.5 %collective-permute-start.7 = (bf16[256,256]{0,1:T(8,128)(2,1)S(1)}, bf16[256,256]{0,1:T(8,128)(2,1)S(1)}, u32[]{:S(2)}, u32[]{:S(2)}) collective-permute-start(bf16[256,256]{0,1:T(8,128)(2,1)S(1)} %get-tuple-element.54), channel_id=1, source_target_pairs={{0,1},{1,2},{2,3},{3,0},{4,5},{5,6},{6,7},{7,4},{8,9},{9,10},{10,1... | collective-permute-start | bytes 393224 | tf_op jit(solution)/shard_map/ppermute | solution.py:30
  74.8 23.4 %copy-start.3 = (bf16[1024,2048]{1,0:T(8,128)(2,1)}, bf16[1024,2048]{1,0:T(8,128)(2,1)S(1)}, u32[]{:S(2)}) copy-start(bf16[1024,2048]{1,0:T(8,128)(2,1)S(1)} %pad_maximum_fusion) | copy-start | bytes 12582916
  74.9 10.5 %collective-permute-start.12 = (bf16[256,256]{0,1:T(8,128)(2,1)S(1)}, bf16[256,256]{0,1:T(8,128)(2,1)S(1)}, u32[]{:S(2)}, u32[]{:S(2)}) collective-permute-start(bf16[256,256]{0,1:T(8,128)(2,1)S(1)} %get-tuple-element.53), channel_id=1, source_target_pairs={{0,3},{1,0},{2,1},{3,2},{4,7},{5,4},{6,5},{7,6},{8,11},{9,8},{10,9... | collective-permute-start | bytes 393224 | tf_op jit(solution)/shard_map/ppermute | solution.py:30
  77.6 7.8 %collective-permute-start.11 = (bf16[256,256]{0,1:T(8,128)(2,1)S(1)}, bf16[256,256]{0,1:T(8,128)(2,1)S(1)}, u32[]{:S(2)}, u32[]{:S(2)}) collective-permute-start(bf16[256,256]{0,1:T(8,128)(2,1)S(1)} %get-tuple-element.53), channel_id=1, source_target_pairs={{0,2},{1,3},{2,0},{3,1},{4,6},{5,7},{6,4},{7,5},{8,10},{9,11},{10,... | collective-permute-start | bytes 393224 | tf_op jit(solution)/shard_map/ppermute | solution.py:30
  79.3 6.2 %collective-permute-start.10 = (bf16[256,256]{0,1:T(8,128)(2,1)S(1)}, bf16[256,256]{0,1:T(8,128)(2,1)S(1)}, u32[]{:S(2)}, u32[]{:S(2)}) collective-permute-start(bf16[256,256]{0,1:T(8,128)(2,1)S(1)} %get-tuple-element.53), channel_id=1, source_target_pairs={{0,1},{1,2},{2,3},{3,0},{4,5},{5,6},{6,7},{7,4},{8,9},{9,10},{10,1... | collective-permute-start | bytes 393224 | tf_op jit(solution)/shard_map/ppermute | solution.py:30
  81.4 16.8 %collective-permute-start.13 = (bf16[1024,256]{1,0:T(8,128)(2,1)S(1)}, bf16[1024,256]{1,0:T(8,128)(2,1)S(1)}, u32[]{:S(2)}, u32[]{:S(2)}) collective-permute-start(bf16[1024,256]{1,0:T(8,128)(2,1)S(1)} %fusion.16), channel_id=1, source_target_pairs={{0,4},{1,5},{2,6},{3,7},{4,0},{5,1},{6,2},{7,3},{8,12},{9,13},{10,... | collective-permute-start | bytes 1572872 | tf_op jit(solution)/shard_map/ppermute | solution.py:30
  86.4 23.1 %collective-permute-start.14 = (bf16[1024,256]{1,0:T(8,128)(2,1)S(1)}, bf16[1024,256]{1,0:T(8,128)(2,1)S(1)}, u32[]{:S(2)}, u32[]{:S(2)}) collective-permute-start(bf16[1024,256]{1,0:T(8,128)(2,1)S(1)} %fusion.19), channel_id=1, source_target_pairs={{0,4},{1,5},{2,6},{3,7},{4,0},{5,1},{6,2},{7,3},{8,12},{9,13},{10,... | collective-permute-start | bytes 1572872 | tf_op jit(solution)/shard_map/ppermute | solution.py:30
  90.6 7.7 %copy-start.8 = (f32[1,1024,512]{2,1,0:T(8,128)S(1)}, f32[1,1024,512]{2,1,0:T(8,128)}, u32[]{:S(2)}) copy-start(f32[1,1024,512]{2,1,0:T(8,128)} %param.11) | copy-start | bytes 6291460
  90.6 7.7 %copy-start.11 = (f32[1,1024,512]{2,1,0:T(8,128)S(1)}, f32[1,1024,512]{2,1,0:T(8,128)}, u32[]{:S(2)}) copy-start(f32[1,1024,512]{2,1,0:T(8,128)} %param.12) | copy-start | bytes 6291460
  91.4 18.1 %copy-start.1 = (f32[1024,256]{1,0:T(8,128)}, f32[1024,256]{1,0:T(8,128)S(1)}, u32[]{:S(2)}) copy-start(f32[1024,256]{1,0:T(8,128)S(1)} %fusion.12) | copy-start | bytes 3145732
  100.8 20.0 %collective-permute-start.16 = (bf16[1024,256]{1,0:T(8,128)(2,1)}, bf16[1024,256]{1,0:T(8,128)(2,1)}, u32[]{:S(2)}, u32[]{:S(2)}) collective-permute-start(bf16[1024,256]{1,0:T(8,128)(2,1)} %get-tuple-element.41), channel_id=1, source_target_pairs={{0,4},{1,5},{2,6},{3,7},{4,0},{5,1},{6,2},{7,3},{8,12},{9,13},{10,... | collective-permute-start | bytes 1572872 | tf_op jit(solution)/shard_map/ppermute | solution.py:30
  110.4 17.6 %collective-permute-start.23 = (bf16[1024,256]{1,0:T(8,128)(2,1)S(1)}, bf16[1024,256]{1,0:T(8,128)(2,1)}, u32[]{:S(2)}, u32[]{:S(2)}) collective-permute-start(bf16[1024,256]{1,0:T(8,128)(2,1)S(1)} %fusion.38), channel_id=1, source_target_pairs={{0,4},{1,5},{2,6},{3,7},{4,0},{5,1},{6,2},{7,3},{8,12},{9,13},{10,... | collective-permute-start | bytes 1572872 | tf_op jit(solution)/shard_map/ppermute | solution.py:30
  115.6 57.3 %all-to-all-start.1 = ((f32[8,128,512]{2,1,0:T(8,128)}), f32[8,128,512]{2,1,0:T(8,128)}, u32[]{:S(2)}, u32[]{:S(2)}) async-start(f32[8,128,512]{2,1,0:T(8,128)} %broadcast_in_dim.4), calls=%async_computation.1 | async-start | bytes 4194304 | tf_op jit(solution)/shard_map/all_to_all | solution.py:188
  120.0 7.9 %copy-start.4 = (bf16[1024,2048]{1,0:T(8,128)(2,1)S(1)}, bf16[1024,2048]{1,0:T(8,128)(2,1)}, u32[]{:S(2)}) copy-start(bf16[1024,2048]{1,0:T(8,128)(2,1)} %copy-done.3) | copy-start | bytes 12582916
  125.0 7.2 %collective-permute-start.17 = (bf16[256,256]{0,1:T(8,128)(2,1)S(1)}, bf16[256,256]{0,1:T(8,128)(2,1)S(1)}, u32[]{:S(2)}, u32[]{:S(2)}) collective-permute-start(bf16[256,256]{0,1:T(8,128)(2,1)S(1)} %get-tuple-element.59), channel_id=1, source_target_pairs={{0,3},{1,0},{2,1},{3,2},{4,7},{5,4},{6,5},{7,6},{8,11},{9,8},{10,9... | collective-permute-start | bytes 393224 | tf_op jit(solution)/shard_map/ppermute | solution.py:30
  127.0 7.6 %collective-permute-start.19 = (bf16[256,256]{0,1:T(8,128)(2,1)S(1)}, bf16[256,256]{0,1:T(8,128)(2,1)S(1)}, u32[]{:S(2)}, u32[]{:S(2)}) collective-permute-start(bf16[256,256]{0,1:T(8,128)(2,1)S(1)} %get-tuple-element.60), channel_id=1, source_target_pairs={{0,2},{1,3},{2,0},{3,1},{4,6},{5,7},{6,4},{7,5},{8,10},{9,11},{10,... | collective-permute-start | bytes 393224 | tf_op jit(solution)/shard_map/ppermute | solution.py:30
  127.5 8.4 %collective-permute-start.18 = (bf16[256,256]{0,1:T(8,128)(2,1)S(1)}, bf16[256,256]{0,1:T(8,128)(2,1)S(1)}, u32[]{:S(2)}, u32[]{:S(2)}) collective-permute-start(bf16[256,256]{0,1:T(8,128)(2,1)S(1)} %get-tuple-element.61), channel_id=1, source_target_pairs={{0,1},{1,2},{2,3},{3,0},{4,5},{5,6},{6,7},{7,4},{8,9},{9,10},{10,1... | collective-permute-start | bytes 393224 | tf_op jit(solution)/shard_map/ppermute | solution.py:30
  136.0 6.5 %collective-permute-start.22 = (bf16[256,256]{0,1:T(8,128)(2,1)S(1)}, bf16[256,256]{0,1:T(8,128)(2,1)S(1)}, u32[]{:S(2)}, u32[]{:S(2)}) collective-permute-start(bf16[256,256]{0,1:T(8,128)(2,1)S(1)} %subtract_convert_fusion.1), channel_id=1, source_target_pairs={{0,3},{1,0},{2,1},{3,2},{4,7},{5,4},{6,5},{7,6},{8,11},{9,8},{10,9... | collective-permute-start | bytes 393224 | tf_op jit(solution)/shard_map/ppermute | solution.py:30
  136.7 8.9 %collective-permute-start.21 = (bf16[256,256]{0,1:T(8,128)(2,1)S(1)}, bf16[256,256]{0,1:T(8,128)(2,1)S(1)}, u32[]{:S(2)}, u32[]{:S(2)}) collective-permute-start(bf16[256,256]{0,1:T(8,128)(2,1)S(1)} %subtract_convert_fusion.1), channel_id=1, source_target_pairs={{0,2},{1,3},{2,0},{3,1},{4,6},{5,7},{6,4},{7,5},{8,10},{9,11},{10,... | collective-permute-start | bytes 393224 | tf_op jit(solution)/shard_map/ppermute | solution.py:30
  137.2 10.8 %collective-permute-start.20 = (bf16[256,256]{0,1:T(8,128)(2,1)S(1)}, bf16[256,256]{0,1:T(8,128)(2,1)S(1)}, u32[]{:S(2)}, u32[]{:S(2)}) collective-permute-start(bf16[256,256]{0,1:T(8,128)(2,1)S(1)} %subtract_convert_fusion.1), channel_id=1, source_target_pairs={{0,1},{1,2},{2,3},{3,0},{4,5},{5,6},{6,7},{7,4},{8,9},{9,10},{10,1... | collective-permute-start | bytes 393224 | tf_op jit(solution)/shard_map/ppermute | solution.py:30
  138.1 11.9 %collective-permute-start.26 = (bf16[256,256]{0,1:T(8,128)(2,1)S(1)}, bf16[256,256]{0,1:T(8,128)(2,1)S(1)}, u32[]{:S(2)}, u32[]{:S(2)}) collective-permute-start(bf16[256,256]{0,1:T(8,128)(2,1)S(1)} %get-tuple-element.56), channel_id=1, source_target_pairs={{0,2},{1,3},{2,0},{3,1},{4,6},{5,7},{6,4},{7,5},{8,10},{9,11},{10,... | collective-permute-start | bytes 393224 | tf_op jit(solution)/shard_map/ppermute | solution.py:30
  142.3 8.8 %collective-permute-start.25 = (bf16[256,256]{0,1:T(8,128)(2,1)S(1)}, bf16[256,256]{0,1:T(8,128)(2,1)S(1)}, u32[]{:S(2)}, u32[]{:S(2)}) collective-permute-start(bf16[256,256]{0,1:T(8,128)(2,1)S(1)} %get-tuple-element.57), channel_id=1, source_target_pairs={{0,1},{1,2},{2,3},{3,0},{4,5},{5,6},{6,7},{7,4},{8,9},{9,10},{10,1... | collective-permute-start | bytes 393224 | tf_op jit(solution)/shard_map/ppermute | solution.py:30
  142.5 8.7 %collective-permute-start.24 = (bf16[256,256]{0,1:T(8,128)(2,1)S(1)}, bf16[256,256]{0,1:T(8,128)(2,1)S(1)}, u32[]{:S(2)}, u32[]{:S(2)}) collective-permute-start(bf16[256,256]{0,1:T(8,128)(2,1)S(1)} %get-tuple-element.58), channel_id=1, source_target_pairs={{0,3},{1,0},{2,1},{3,2},{4,7},{5,4},{6,5},{7,6},{8,11},{9,8},{10,9... | collective-permute-start | bytes 393224 | tf_op jit(solution)/shard_map/ppermute | solution.py:30
  151.2 6.3 %collective-permute-start.29 = (bf16[256,256]{0,1:T(8,128)(2,1)S(1)}, bf16[256,256]{0,1:T(8,128)(2,1)S(1)}, u32[]{:S(2)}, u32[]{:S(2)}) collective-permute-start(bf16[256,256]{0,1:T(8,128)(2,1)S(1)} %subtract_convert_fusion), channel_id=1, source_target_pairs={{0,3},{1,0},{2,1},{3,2},{4,7},{5,4},{6,5},{7,6},{8,11},{9,8},{10,9... | collective-permute-start | bytes 393224 | tf_op jit(solution)/shard_map/ppermute | solution.py:30
  152.4 7.4 %collective-permute-start.28 = (bf16[256,256]{0,1:T(8,128)(2,1)S(1)}, bf16[256,256]{0,1:T(8,128)(2,1)S(1)}, u32[]{:S(2)}, u32[]{:S(2)}) collective-permute-start(bf16[256,256]{0,1:T(8,128)(2,1)S(1)} %subtract_convert_fusion), channel_id=1, source_target_pairs={{0,2},{1,3},{2,0},{3,1},{4,6},{5,7},{6,4},{7,5},{8,10},{9,11},{10,... | collective-permute-start | bytes 393224 | tf_op jit(solution)/shard_map/ppermute | solution.py:30
  152.4 8.3 %collective-permute-start.27 = (bf16[256,256]{0,1:T(8,128)(2,1)S(1)}, bf16[256,256]{0,1:T(8,128)(2,1)S(1)}, u32[]{:S(2)}, u32[]{:S(2)}) collective-permute-start(bf16[256,256]{0,1:T(8,128)(2,1)S(1)} %subtract_convert_fusion), channel_id=1, source_target_pairs={{0,1},{1,2},{2,3},{3,0},{4,5},{5,6},{6,7},{7,4},{8,9},{9,10},{10,1... | collective-permute-start | bytes 393224 | tf_op jit(solution)/shard_map/ppermute | solution.py:30
  153.3 16.4 %collective-permute-start.30 = (bf16[1024,256]{1,0:T(8,128)(2,1)S(1)}, bf16[1024,256]{1,0:T(8,128)(2,1)S(1)}, u32[]{:S(2)}, u32[]{:S(2)}) collective-permute-start(bf16[1024,256]{1,0:T(8,128)(2,1)S(1)} %fusion.22), channel_id=1, source_target_pairs={{0,4},{1,5},{2,6},{3,7},{4,0},{5,1},{6,2},{7,3},{8,12},{9,13},{10,... | collective-permute-start | bytes 1572872 | tf_op jit(solution)/shard_map/ppermute | solution.py:30
  162.3 16.5 %collective-permute-start.31 = (bf16[1024,256]{1,0:T(8,128)(2,1)}, bf16[1024,256]{1,0:T(8,128)(2,1)}, u32[]{:S(2)}, u32[]{:S(2)}) collective-permute-start(bf16[1024,256]{1,0:T(8,128)(2,1)} %fusion.25), channel_id=1, source_target_pairs={{0,4},{1,5},{2,6},{3,7},{4,0},{5,1},{6,2},{7,3},{8,12},{9,13},{10,... | collective-permute-start | bytes 1572872 | tf_op jit(solution)/shard_map/ppermute | solution.py:30
  164.6 5.1 %copy-start.9 = (f32[1,1024,512]{2,1,0:T(8,128)S(1)}, f32[1,1024,512]{2,1,0:T(8,128)}, u32[]{:S(2)}) copy-start(f32[1,1024,512]{2,1,0:T(8,128)} %param.11) | copy-start | bytes 6291460
  164.6 5.0 %copy-start.12 = (f32[1,1024,512]{2,1,0:T(8,128)S(1)}, f32[1,1024,512]{2,1,0:T(8,128)}, u32[]{:S(2)}) copy-start(f32[1,1024,512]{2,1,0:T(8,128)} %param.12) | copy-start | bytes 6291460
  172.9 5.9 %copy-start.2 = (f32[1024,256]{1,0:T(8,128)S(1)}, f32[1024,256]{1,0:T(8,128)}, u32[]{:S(2)}) copy-start(f32[1024,256]{1,0:T(8,128)} %copy-done.1) | copy-start | bytes 3145732
  172.9 5.9 %copy-start.7 = (bf16[1024,256]{1,0:T(8,128)(2,1)S(1)}, bf16[1024,256]{1,0:T(8,128)(2,1)}, u32[]{:S(2)}) copy-start(bf16[1024,256]{1,0:T(8,128)(2,1)} %copy-done.6) | copy-start | bytes 1572868
  172.9 5.9 %copy-start.10 = (f32[1,1024,512]{2,1,0:T(8,128)S(1)}, f32[1,1024,512]{2,1,0:T(8,128)}, u32[]{:S(2)}) copy-start(f32[1,1024,512]{2,1,0:T(8,128)} %param.11) | copy-start | bytes 6291460
  172.9 5.9 %copy-start.13 = (f32[1,1024,512]{2,1,0:T(8,128)S(1)}, f32[1,1024,512]{2,1,0:T(8,128)}, u32[]{:S(2)}) copy-start(f32[1,1024,512]{2,1,0:T(8,128)} %param.12) | copy-start | bytes 6291460
  172.9 5.9 %copy-start.14 = (f32[1024,256]{1,0:T(8,128)S(1)}, f32[1024,256]{1,0:T(8,128)}, u32[]{:S(2)}) copy-start(f32[1024,256]{1,0:T(8,128)} %fusion.8) | copy-start | bytes 3145732
  (6 other events, 18.5 us)

commit v7 on v6

--- a/solution.py
+++ b/solution.py
@@ -203,6 +203,9 @@
     arrived_b = send_parts({dx: part_b[dx] for dx in (2, 1, 3)})
     resid_a = bf16(add_parts(f32(part_a[0]), arrived_a) - teacher[:, span_a])
     row_a = jnp.concatenate(gather(resid_a), axis=0)
+    row_a, arrived_b[1], arrived_b[2], arrived_b[3] = tie(
+        row_a, arrived_b[1], arrived_b[2], arrived_b[3]
+    )
     away_a = away(row_a)
     got_a = shift(away_a, 1, 0)
     own_b, away_a = tie(part_b[0], away_a)

time: 185 us -> 188 us (1.016)
  starting transfers between devices: 70.4 us -> 72.9 us
  matrix products: 29.1 us -> 26.8 us
    dot_general x6, matrix products: 16.9 us -> 13 us  [dot(): return jnp.dot(a, b, preferred_element_type=jnp.float32)]
    ppermute x31, starting transfers between devices: 59.5 us -> 62.1 us  [shift(): return lax.ppermute(value, 'fsdp', pairs)]
  transfers between devices with their start and end apart: 34 -> 34, of which waited for: 20 -> 18; matrix products, arithmetic and copies ran while one was open for 23% -> 23% of each run, Pallas kernels for 3% -> 3%
where the time goes in v7:
time: 188 us; the launch traced here: 187 us
  starting transfers between devices  72.9 us (39%)
  waiting for transfers between devices  57.5 us (31%)
  matrix products  26.8 us (14%)
  other arithmetic  17.2 us (9%)
  Pallas kernels  8.48 us (5%)
  local copies, waits for them, and re-layouts  2.78 us (1%)
    ppermute x31, starting transfers between devices, shift(): return lax.ppermute(value, 'fsdp', pairs)  62.1 us
    ppermute x31, waiting for transfers between devices, shift(): return lax.ppermute(value, 'fsdp', pairs)  56.4 us
    dot_general x8, matrix products, dot_t(): lax.dot_general(a, b, (((0,), (0,)), ((), ())), preferred_element_type=jn...  13.7 us
    dot_general x6, matrix products, dot(): return jnp.dot(a, b, preferred_element_type=jnp.float32)  13 us
    pallas_call x4, Pallas kernels, pick(): pl.pallas_call(functools.partial(pick_kernel, dx), out_shape=jax.ShapeDty...  8.48 us
    add x1, other arithmetic, outer_nesterov(): momentum_new = 0.9 * momentum + delta  5.81 us
    all_to_all x1, starting transfers between devices, shards(): lax.all_to_all(frag_inner[0].reshape(mates, frag_rows, -1), 'rep', 0, 0,...  4.47 us
    all_to_all x1, starting transfers between devices, shards(): lax.all_to_all(jnp.broadcast_to(piece_sum[None], (mates, *piece_sum.shape...  4.35 us
  transfers between devices with their start and end apart: 34, of which 18 were waited for; matrix products, arithmetic and copies ran while one was open for 23% of the time, Pallas kernels for 3%

profile of v7, /device:TPU:0, one launch (start us, length us, event | category | flops | bytes accessed | tf_op | source)
XLA Modules:
  0.0 186.6 jit_solution(722450851289965977)
XLA Ops:
  0.6 2.1 %shard_map.106 = bf16[256,2048]{1,0:T(8,128)(2,1)} custom-call(bf16[256,8192]{1,0:T(8,128)(2,1)} %bitcast.82), custom_call_target="tpu_custom_call" | custom-call | bytes 2097152 | tf_op jit(solution)/shard_map/pallas_call | solution.py:86
  2.8 3.2 %collective-permute-start.3 = (bf16[256,2048]{1,0:T(8,128)(2,1)}, bf16[256,2048]{1,0:T(8,128)(2,1)}, u32[]{:S(2)}, u32[]{:S(2)}) collective-permute-start(bf16[256,2048]{1,0:T(8,128)(2,1)} %shard_map.106), channel_id=1, source_target_pairs={{0,2},{1,3},{2,0},{3,1},{4,6},{5,7},{6,4},{7,5},{8,10},{9,11},{10,... | collective-permute-start | bytes 3145736 | tf_op jit(solution)/shard_map/ppermute | solution.py:30
  5.9 2.1 %shard_map.103 = bf16[256,2048]{1,0:T(8,128)(2,1)} custom-call(bf16[256,8192]{1,0:T(8,128)(2,1)} %bitcast.83), custom_call_target="tpu_custom_call" | custom-call | bytes 2097152 | tf_op jit(solution)/shard_map/pallas_call | solution.py:86
  9.2 3.9 %collective-permute-start = (bf16[1024,512]{1,0:T(8,128)(2,1)}, bf16[1024,512]{1,0:T(8,128)(2,1)}, u32[]{:S(2)}, u32[]{:S(2)}) collective-permute-start(bf16[1024,512]{1,0:T(8,128)(2,1)} %convert_element_type.105), channel_id=1, source_target_pairs={{0,4},{1,5},{2,6},{3,7},{4,0},{5,1},{6,2},{7,3},{8,12},{9,13},{10,... | collective-permute-start | bytes 3145736 | tf_op jit(solution)/shard_map/ppermute | solution.py:30
  13.0 2.1 %shard_map.105 = bf16[256,2048]{1,0:T(8,128)(2,1)} custom-call(bf16[256,8192]{1,0:T(8,128)(2,1)} %bitcast.84), custom_call_target="tpu_custom_call" | custom-call | bytes 2097152 | tf_op jit(solution)/shard_map/pallas_call | solution.py:86
  15.8 2.6 %collective-permute-start.2 = (bf16[256,2048]{1,0:T(8,128)(2,1)}, bf16[256,2048]{1,0:T(8,128)(2,1)}, u32[]{:S(2)}, u32[]{:S(2)}) collective-permute-start(bf16[256,2048]{1,0:T(8,128)(2,1)} %shard_map.103), channel_id=1, source_target_pairs={{0,3},{1,0},{2,1},{3,2},{4,7},{5,4},{6,5},{7,6},{8,11},{9,8},{10,9... | collective-permute-start | bytes 3145736 | tf_op jit(solution)/shard_map/ppermute | solution.py:30
  18.4 4.5 %all-to-all-start = ((bf16[8,128,512]{2,1,0:T(8,128)(2,1)}), bf16[8,128,512]{2,1,0:T(8,128)(2,1)}, u32[]{:S(2)}, u32[]{:S(2)}) async-start(bf16[8,128,512]{2,1,0:T(8,128)(2,1)} %bitcast.4), calls=%async_computation | async-start | bytes 2097152 | tf_op jit(solution)/shard_map/all_to_all | solution.py:137
  22.9 2.2 %shard_map.104 = bf16[256,2048]{1,0:T(8,128)(2,1)} custom-call(bf16[256,8192]{1,0:T(8,128)(2,1)} %bitcast.85), custom_call_target="tpu_custom_call" | custom-call | bytes 2097152 | tf_op jit(solution)/shard_map/pallas_call | solution.py:86
  25.3 5.5 %collective-permute-done.3 = bf16[256,2048]{1,0:T(8,128)(2,1)} collective-permute-done((bf16[256,2048]{1,0:T(8,128)(2,1)}, bf16[256,2048]{1,0:T(8,128)(2,1)}, u32[]{:S(2)}, u32[]{:S(2)}) %collective-permute-start.3) | collective-permute-done | bytes 1048608 | tf_op jit(solution)/shard_map/ppermute | solution.py:30
  30.8 5.5 %collective-permute-done = bf16[1024,512]{1,0:T(8,128)(2,1)} collective-permute-done((bf16[1024,512]{1,0:T(8,128)(2,1)}, bf16[1024,512]{1,0:T(8,128)(2,1)}, u32[]{:S(2)}, u32[]{:S(2)}) %collective-permute-start) | collective-permute-done | bytes 1048608 | tf_op jit(solution)/shard_map/ppermute | solution.py:30
  36.2 2.6 %fusion.28 = bf16[256,512]{0,1:T(8,128)(2,1)S(1)} fusion(bf16[256,2048]{1,0:T(8,128)(2,1)} %collective-permute-done.3, bf16[1024,512]{1,0:T(8,128)(2,1)} %collective-permute-done, bf16[1024,512]{1,0:T(8,128)(2,1)} %convert_element_type.105), kind=kOutput, calls=%fused_computation.33 | convolution fusion | flops 541196288 | bytes 3407872 | tf_op jit(solution)/shard_map/dot_general | solution.py:42
  39.6 13.6 %collective-permute-done.1 = bf16[256,2048]{1,0:T(8,128)(2,1)} collective-permute-done((bf16[256,2048]{1,0:T(8,128)(2,1)}, bf16[256,2048]{1,0:T(8,128)(2,1)}, u32[]{:S(2)}, u32[]{:S(2)}) %collective-permute-start.1) | collective-permute-done | bytes 1048608 | tf_op jit(solution)/shard_map/ppermute | solution.py:30
  53.4 2.8 %convolution_convert_fusion.3 = bf16[256,512]{0,1:T(8,128)(2,1)S(1)} fusion(bf16[256,2048]{1,0:T(8,128)(2,1)} %collective-permute-done.2, bf16[1024,512]{1,0:T(8,128)(2,1)} %collective-permute-done, bf16[1024,512]{1,0:T(8,128)(2,1)} %convert_element_type.105), kind=kOutput, calls=%fused_computation.31 | convolution fusion | flops 541196288 | bytes 3407872 | tf_op jit(solution)/shard_map/dot_general | solution.py:42
  57.7 2.8 %convolution_convert_fusion.4 = bf16[256,512]{0,1:T(8,128)(2,1)S(1)} fusion(bf16[256,2048]{1,0:T(8,128)(2,1)} %collective-permute-done.1, bf16[1024,512]{1,0:T(8,128)(2,1)} %collective-permute-done, bf16[1024,512]{1,0:T(8,128)(2,1)} %convert_element_type.105), kind=kOutput, calls=%fused_computation.32 | convolution fusion | flops 541196288 | bytes 3407872 | tf_op jit(solution)/shard_map/dot_general | solution.py:42
  60.5 1.9 %collective-permute-start.4 = (bf16[256,512]{0,1:T(8,128)(2,1)S(1)}, bf16[256,512]{0,1:T(8,128)(2,1)S(1)}, u32[]{:S(2)}, u32[]{:S(2)}) collective-permute-start(bf16[256,512]{0,1:T(8,128)(2,1)S(1)} %convolution_convert_fusion.4), channel_id=1, source_target_pairs={{0,3},{1,0},{2,1},{3,2},{4,7},{5,4},{6,5},{7,6},{8,11},{9,8},{10,9... | collective-permute-start | bytes 786440 | tf_op jit(solution)/shard_map/ppermute | solution.py:30
  62.3 2.3 %convolution_bitcast_fusion = f32[256,512]{0,1:T(8,128)S(1)} fusion(bf16[256,2048]{1,0:T(8,128)(2,1)S(1)} %copy-done.5, bf16[1024,512]{1,0:T(8,128)(2,1)} %collective-permute-done, bf16[1024,512]{1,0:T(8,128)(2,1)} %convert_element_type.105), kind=kOutput, calls=%fused_computation.29 | convolution fusion | flops 541065216 | bytes 3670016 | tf_op jit(solution)/shard_map/dot_general | solution.py:42
  66.0 2.0 %collective-permute-start.15 = (f32[128,512]{1,0:T(8,128)S(1)}, f32[128,512]{1,0:T(8,128)S(1)}, u32[]{:S(2)}, u32[]{:S(2)}) collective-permute-start(f32[128,512]{1,0:T(8,128)S(1)} %convert_reduce_fusion), channel_id=1, source_target_pairs={{0,64},{8,72},{16,80},{24,88},{32,96},{40,104},{48,112},{56,120},{... | collective-permute-start | bytes 786440 | tf_op jit(solution)/shard_map/ppermute | solution.py:142
  68.5 3.1 %collective-permute-start.9 = (bf16[256,256]{0,1:T(8,128)(2,1)S(1)}, bf16[256,256]{0,1:T(8,128)(2,1)S(1)}, u32[]{:S(2)}, u32[]{:S(2)}) collective-permute-start(bf16[256,256]{0,1:T(8,128)(2,1)S(1)} %get-tuple-element.62), channel_id=1, source_target_pairs={{0,3},{1,0},{2,1},{3,2},{4,7},{5,4},{6,5},{7,6},{8,11},{9,8},{10,9... | collective-permute-start | bytes 393224 | tf_op jit(solution)/shard_map/ppermute | solution.py:30
  72.7 2.1 %pad_maximum_fusion = bf16[1024,2048]{1,0:T(8,128)(2,1)S(1)} fusion(bf16[256,2048]{1,0:T(8,128)(2,1)} %collective-permute-done.2, bf16[256,2048]{1,0:T(8,128)(2,1)} %collective-permute-done.3, bf16[256,2048]{1,0:T(8,128)(2,1)} %collective-permute-done.1, bf16[256,2048]{1,0:T(8,128)(2,1)S(1)} %copy-done.5), kind=kLoop, calls=%fused_computation | loop fusion | flops 16777216 | bytes 8388608 | tf_op jit(solution)/shard_map/concatenate | solution.py:152
  74.9 2.7 %collective-permute-start.12 = (bf16[256,256]{0,1:T(8,128)(2,1)S(1)}, bf16[256,256]{0,1:T(8,128)(2,1)S(1)}, u32[]{:S(2)}, u32[]{:S(2)}) collective-permute-start(bf16[256,256]{0,1:T(8,128)(2,1)S(1)} %get-tuple-element.61), channel_id=1, source_target_pairs={{0,3},{1,0},{2,1},{3,2},{4,7},{5,4},{6,5},{7,6},{8,11},{9,8},{10,9... | collective-permute-start | bytes 393224 | tf_op jit(solution)/shard_map/ppermute | solution.py:30
  77.6 1.8 collective-permute-start.11
  81.4 4.0 %collective-permute-start.13 = (bf16[1024,256]{1,0:T(8,128)(2,1)S(1)}, bf16[1024,256]{1,0:T(8,128)(2,1)S(1)}, u32[]{:S(2)}, u32[]{:S(2)}) collective-permute-start(bf16[1024,256]{1,0:T(8,128)(2,1)S(1)} %fusion.16), channel_id=1, source_target_pairs={{0,4},{1,5},{2,6},{3,7},{4,0},{5,1},{6,2},{7,3},{8,12},{9,13},{10,... | collective-permute-start | bytes 1572872 | tf_op jit(solution)/shard_map/ppermute | solution.py:30
  86.4 4.1 %collective-permute-start.14 = (bf16[1024,256]{1,0:T(8,128)(2,1)S(1)}, bf16[1024,256]{1,0:T(8,128)(2,1)S(1)}, u32[]{:S(2)}, u32[]{:S(2)}) collective-permute-start(bf16[1024,256]{1,0:T(8,128)(2,1)S(1)} %fusion.19), channel_id=1, source_target_pairs={{0,4},{1,5},{2,6},{3,7},{4,0},{5,1},{6,2},{7,3},{8,12},{9,13},{10,... | collective-permute-start | bytes 1572872 | tf_op jit(solution)/shard_map/ppermute | solution.py:30
  91.4 6.8 %collective-permute-done.13 = bf16[1024,256]{1,0:T(8,128)(2,1)S(1)} collective-permute-done((bf16[1024,256]{1,0:T(8,128)(2,1)S(1)}, bf16[1024,256]{1,0:T(8,128)(2,1)S(1)}, u32[]{:S(2)}, u32[]{:S(2)}) %collective-permute-start.13) | collective-permute-done | bytes 524320 | tf_op jit(solution)/shard_map/ppermute | solution.py:30
  98.2 2.4 %fusion.37 = (bf16[1024,256]{1,0:T(8,128)(2,1)S(1)}, f32[1024,256]{1,0:T(8,128)}) fusion(f32[1,1024,512]{2,1,0:T(8,128)S(1)} %copy-done, bf16[1024,256]{1,0:T(8,128)(2,1)S(1)} %collective-permute-done.13, f32[1,1024,512]{2,1,0:T(8,128)S(1)} %copy-done.8, f32[1,1024,512]{2,1,0:T(8,128)S(1)} %copy-done.11, bf16[1024,256]{0,1:T(8,128)(2,1)S(1)} %pad_maximum_fusion.2, ...), kind=kOutput, calls=%fused_computation.54 | convolution fusion | flops 541327360 | bytes 7864320 | tf_op jit(solution)/shard_map/dot_general | solution.py:50
  100.6 3.5 %collective-permute-start.16 = (bf16[1024,256]{1,0:T(8,128)(2,1)S(1)}, bf16[1024,256]{1,0:T(8,128)(2,1)S(1)}, u32[]{:S(2)}, u32[]{:S(2)}) collective-permute-start(bf16[1024,256]{1,0:T(8,128)(2,1)S(1)} %get-tuple-element.45), channel_id=1, source_target_pairs={{0,4},{1,5},{2,6},{3,7},{4,0},{5,1},{6,2},{7,3},{8,12},{9,13},{10,... | collective-permute-start | bytes 1572872 | tf_op jit(solution)/shard_map/ppermute | solution.py:30
  104.2 5.3 %collective-permute-done.14 = bf16[1024,256]{1,0:T(8,128)(2,1)S(1)} collective-permute-done((bf16[1024,256]{1,0:T(8,128)(2,1)S(1)}, bf16[1024,256]{1,0:T(8,128)(2,1)S(1)}, u32[]{:S(2)}, u32[]{:S(2)}) %collective-permute-start.14) | collective-permute-done | bytes 524320 | tf_op jit(solution)/shard_map/ppermute | solution.py:30
  110.4 3.6 %collective-permute-start.23 = (bf16[1024,256]{1,0:T(8,128)(2,1)S(1)}, bf16[1024,256]{1,0:T(8,128)(2,1)S(1)}, u32[]{:S(2)}, u32[]{:S(2)}) collective-permute-start(bf16[1024,256]{1,0:T(8,128)(2,1)S(1)} %fusion.38), channel_id=1, source_target_pairs={{0,4},{1,5},{2,6},{3,7},{4,0},{5,1},{6,2},{7,3},{8,12},{9,13},{10,... | collective-permute-start | bytes 1572872 | tf_op jit(solution)/shard_map/ppermute | solution.py:30
  114.0 6.7 %collective-permute-done.16 = bf16[1024,256]{1,0:T(8,128)(2,1)S(1)} collective-permute-done((bf16[1024,256]{1,0:T(8,128)(2,1)S(1)}, bf16[1024,256]{1,0:T(8,128)(2,1)S(1)}, u32[]{:S(2)}, u32[]{:S(2)}) %collective-permute-start.16) | collective-permute-done | bytes 524320 | tf_op jit(solution)/shard_map/ppermute | solution.py:30
  122.0 2.0 %collective-permute-start.17 = (bf16[256,256]{0,1:T(8,128)(2,1)S(1)}, bf16[256,256]{0,1:T(8,128)(2,1)S(1)}, u32[]{:S(2)}, u32[]{:S(2)}) collective-permute-start(bf16[256,256]{0,1:T(8,128)(2,1)S(1)} %get-tuple-element.67), channel_id=1, source_target_pairs={{0,3},{1,0},{2,1},{3,2},{4,7},{5,4},{6,5},{7,6},{8,11},{9,8},{10,9... | collective-permute-start | bytes 393224 | tf_op jit(solution)/shard_map/ppermute | solution.py:30
  125.0 2.7 %collective-permute-done.23 = bf16[1024,256]{1,0:T(8,128)(2,1)S(1)} collective-permute-done((bf16[1024,256]{1,0:T(8,128)(2,1)S(1)}, bf16[1024,256]{1,0:T(8,128)(2,1)S(1)}, u32[]{:S(2)}, u32[]{:S(2)}) %collective-permute-start.23) | collective-permute-done | bytes 524320 | tf_op jit(solution)/shard_map/ppermute | solution.py:30
  129.0 1.6 collective-permute-done.19
  130.6 2.8 %collective-permute-done.18 = bf16[256,256]{0,1:T(8,128)(2,1)S(1)} collective-permute-done((bf16[256,256]{0,1:T(8,128)(2,1)S(1)}, bf16[256,256]{0,1:T(8,128)(2,1)S(1)}, u32[]{:S(2)}, u32[]{:S(2)}) %collective-permute-start.18) | collective-permute-done | bytes 131104 | tf_op jit(solution)/shard_map/ppermute | solution.py:30
  137.9 2.6 %collective-permute-start.25 = (bf16[256,256]{0,1:T(8,128)(2,1)}, bf16[256,256]{0,1:T(8,128)(2,1)S(1)}, u32[]{:S(2)}, u32[]{:S(2)}) collective-permute-start(bf16[256,256]{0,1:T(8,128)(2,1)} %get-tuple-element.65), channel_id=1, source_target_pairs={{0,2},{1,3},{2,0},{3,1},{4,6},{5,7},{6,4},{7,5},{8,10},{9,11},{10,... | collective-permute-start | bytes 393224 | tf_op jit(solution)/shard_map/ppermute | solution.py:30
  140.4 2.6 %collective-permute-start.24 = (bf16[256,256]{0,1:T(8,128)(2,1)S(1)}, bf16[256,256]{0,1:T(8,128)(2,1)S(1)}, u32[]{:S(2)}, u32[]{:S(2)}) collective-permute-start(bf16[256,256]{0,1:T(8,128)(2,1)S(1)} %get-tuple-element.66), channel_id=1, source_target_pairs={{0,3},{1,0},{2,1},{3,2},{4,7},{5,4},{6,5},{7,6},{8,11},{9,8},{10,9... | collective-permute-start | bytes 393224 | tf_op jit(solution)/shard_map/ppermute | solution.py:30
  143.1 1.6 broadcast_in_dim.4
  144.7 4.4 %all-to-all-start.1 = ((f32[8,128,512]{2,1,0:T(8,128)}), f32[8,128,512]{2,1,0:T(8,128)}, u32[]{:S(2)}, u32[]{:S(2)}) async-start(f32[8,128,512]{2,1,0:T(8,128)} %broadcast_in_dim.4), calls=%async_computation.1 | async-start | bytes 4194304 | tf_op jit(solution)/shard_map/all_to_all | solution.py:188
  150.1 2.5 %fusion.22 = bf16[1024,256]{1,0:T(8,128)(2,1)S(1)} fusion(bf16[1024,256]{0,1:T(8,128)(2,1)S(1)} %pad_maximum_fusion.4, bf16[1024,2048]{1,0:T(8,128)(2,1)} %copy-done.3), kind=kOutput, calls=%fused_computation.25 | convolution fusion | flops 537133056 | bytes 3145728 | tf_op jit(solution)/shard_map/dot_general | solution.py:50
  154.8 4.1 %collective-permute-start.30 = (bf16[1024,256]{1,0:T(8,128)(2,1)S(1)}, bf16[1024,256]{1,0:T(8,128)(2,1)S(1)}, u32[]{:S(2)}, u32[]{:S(2)}) collective-permute-start(bf16[1024,256]{1,0:T(8,128)(2,1)S(1)} %fusion.22), channel_id=1, source_target_pairs={{0,4},{1,5},{2,6},{3,7},{4,0},{5,1},{6,2},{7,3},{8,12},{9,13},{10,... | collective-permute-start | bytes 1572872 | tf_op jit(solution)/shard_map/ppermute | solution.py:30
  159.1 1.6 collective-permute-done.28
  160.7 2.2 %collective-permute-done.27 = bf16[256,256]{0,1:T(8,128)(2,1)S(1)} collective-permute-done((bf16[256,256]{0,1:T(8,128)(2,1)S(1)}, bf16[256,256]{0,1:T(8,128)(2,1)S(1)}, u32[]{:S(2)}, u32[]{:S(2)}) %collective-permute-start.27) | collective-permute-done | bytes 131104 | tf_op jit(solution)/shard_map/ppermute | solution.py:30
  163.0 1.6 fusion.25
  164.6 4.3 %collective-permute-start.31 = (bf16[1024,256]{1,0:T(8,128)(2,1)}, bf16[1024,256]{1,0:T(8,128)(2,1)}, u32[]{:S(2)}, u32[]{:S(2)}) collective-permute-start(bf16[1024,256]{1,0:T(8,128)(2,1)} %fusion.25), channel_id=1, source_target_pairs={{0,4},{1,5},{2,6},{3,7},{4,0},{5,1},{6,2},{7,3},{8,12},{9,13},{10,... | collective-permute-start | bytes 1572872 | tf_op jit(solution)/shard_map/ppermute | solution.py:30
  169.0 1.7 fusion.8
  171.9 3.2 %add_add_fusion.1 = f32[1024,256]{1,0:T(8,128)} fusion(bf16[1024,256]{1,0:T(8,128)(2,1)S(1)} %collective-permute-done.30, f32[1,1024,512]{2,1,0:T(8,128)S(1)} %copy-done, f32[1024,256]{1,0:T(8,128)S(1)} %copy-done.19, bf16[1024,256]{1,0:T(8,128)(2,1)S(1)} %copy-done.18, f32[1,1024,512]{2,1,0:T(8,128)S(1)} %copy-done.9, f32[1,1024,512]{2,1,0:T(8,128)S(1)} %copy-done.12, ...), kind=kOutput, calls=%fused_computation.51 | convolution fusion | flops 544997376 | bytes 8912896 | tf_op jit(solution)/shard_map/dot_general | solution.py:50
  176.2 5.8 %multiply_add_fusion = (f32[1024,512]{1,0:T(8,128)}, f32[1024,512]{1,0:T(8,128)}) fusion(f32[1024,512]{1,0:T(8,128)} %param.15, f32[1024,512]{1,0:T(8,128)} %param.13, f32[8,128,512]{2,1,0:T(8,128)} %all-to-all-done.1), kind=kLoop, calls=%fused_computation.5 | loop fusion | flops 3670016 | bytes 10485760 | tf_op jit(solution)/shard_map/add | solution.py:22
  182.4 2.6 %add_add_fusion = f32[1024,256]{1,0:T(8,128)S(1)} fusion(f32[1024,256]{1,0:T(8,128)S(1)} %copy-done.14, bf16[1024,256]{1,0:T(8,128)(2,1)} %collective-permute-done.31, f32[1,1024,512]{2,1,0:T(8,128)S(1)} %copy-done, f32[1024,256]{1,0:T(8,128)S(1)} %copy-done.2, bf16[1024,256]{1,0:T(8,128)(2,1)S(1)} %copy-done.7, f32[1,1024,512]{2,1,0:T(8,128)S(1)} %copy-done.10, ...), kind=kLoop, calls=%fused_computation.50 | loop fusion | flops 8126464 | bytes 7340032 | tf_op jit(solution)/shard_map/add | solution.py:222
  185.0 1.6 maximum_bitcast_fusion
  (99 shorter events, 26.5 us)
Async XLA Ops:
  2.7 5.3 %copy-start = (f32[1,1024,512]{2,1,0:T(8,128)S(1)}, f32[1,1024,512]{2,1,0:T(8,128)}, u32[]{:S(2)}) copy-start(f32[1,1024,512]{2,1,0:T(8,128)} %param.10) | copy-start | bytes 6291460
  2.8 28.0 %collective-permute-start.3 = (bf16[256,2048]{1,0:T(8,128)(2,1)}, bf16[256,2048]{1,0:T(8,128)(2,1)}, u32[]{:S(2)}, u32[]{:S(2)}) collective-permute-start(bf16[256,2048]{1,0:T(8,128)(2,1)} %shard_map.106), channel_id=1, source_target_pairs={{0,2},{1,3},{2,0},{3,1},{4,6},{5,7},{6,4},{7,5},{8,10},{9,11},{10,... | collective-permute-start | bytes 3145736 | tf_op jit(solution)/shard_map/ppermute | solution.py:30
  9.2 27.1 %collective-permute-start = (bf16[1024,512]{1,0:T(8,128)(2,1)}, bf16[1024,512]{1,0:T(8,128)(2,1)}, u32[]{:S(2)}, u32[]{:S(2)}) collective-permute-start(bf16[1024,512]{1,0:T(8,128)(2,1)} %convert_element_type.105), channel_id=1, source_target_pairs={{0,4},{1,5},{2,6},{3,7},{4,0},{5,1},{6,2},{7,3},{8,12},{9,13},{10,... | collective-permute-start | bytes 3145736 | tf_op jit(solution)/shard_map/ppermute | solution.py:30
  15.1 38.0 %collective-permute-start.1 = (bf16[256,2048]{1,0:T(8,128)(2,1)}, bf16[256,2048]{1,0:T(8,128)(2,1)}, u32[]{:S(2)}, u32[]{:S(2)}) collective-permute-start(bf16[256,2048]{1,0:T(8,128)(2,1)} %shard_map.105), channel_id=1, source_target_pairs={{0,1},{1,2},{2,3},{3,0},{4,5},{5,6},{6,7},{7,4},{8,9},{9,10},{10,1... | collective-permute-start | bytes 3145736 | tf_op jit(solution)/shard_map/ppermute | solution.py:30
  15.8 37.6 %collective-permute-start.2 = (bf16[256,2048]{1,0:T(8,128)(2,1)}, bf16[256,2048]{1,0:T(8,128)(2,1)}, u32[]{:S(2)}, u32[]{:S(2)}) collective-permute-start(bf16[256,2048]{1,0:T(8,128)(2,1)} %shard_map.103), channel_id=1, source_target_pairs={{0,3},{1,0},{2,1},{3,2},{4,7},{5,4},{6,5},{7,6},{8,11},{9,8},{10,9... | collective-permute-start | bytes 3145736 | tf_op jit(solution)/shard_map/ppermute | solution.py:30
  18.4 21.1 %all-to-all-start = ((bf16[8,128,512]{2,1,0:T(8,128)(2,1)}), bf16[8,128,512]{2,1,0:T(8,128)(2,1)}, u32[]{:S(2)}, u32[]{:S(2)}) async-start(bf16[8,128,512]{2,1,0:T(8,128)(2,1)} %bitcast.4), calls=%async_computation | async-start | bytes 2097152 | tf_op jit(solution)/shard_map/all_to_all | solution.py:137
  38.8 29.2 %collective-permute-start.6 = (bf16[256,512]{0,1:T(8,128)(2,1)S(1)}, bf16[256,512]{0,1:T(8,128)(2,1)S(1)}, u32[]{:S(2)}, u32[]{:S(2)}) collective-permute-start(bf16[256,512]{0,1:T(8,128)(2,1)S(1)} %fusion.28), channel_id=1, source_target_pairs={{0,2},{1,3},{2,0},{3,1},{4,6},{5,7},{6,4},{7,5},{8,10},{9,11},{10,... | collective-permute-start | bytes 786440 | tf_op jit(solution)/shard_map/ppermute | solution.py:30
  56.2 6.2 %copy-start.5 = (bf16[256,2048]{1,0:T(8,128)(2,1)S(1)}, bf16[256,2048]{1,0:T(8,128)(2,1)}, u32[]{:S(2)}) copy-start(bf16[256,2048]{1,0:T(8,128)(2,1)} %shard_map.104) | copy-start | bytes 3145732
  56.2 11.9 %collective-permute-start.5 = (bf16[256,512]{0,1:T(8,128)(2,1)S(1)}, bf16[256,512]{0,1:T(8,128)(2,1)S(1)}, u32[]{:S(2)}, u32[]{:S(2)}) collective-permute-start(bf16[256,512]{0,1:T(8,128)(2,1)S(1)} %convolution_convert_fusion.3), channel_id=1, source_target_pairs={{0,1},{1,2},{2,3},{3,0},{4,5},{5,6},{6,7},{7,4},{8,9},{9,10},{10,1... | collective-permute-start | bytes 786440 | tf_op jit(solution)/shard_map/ppermute | solution.py:30
  60.5 7.8 %collective-permute-start.4 = (bf16[256,512]{0,1:T(8,128)(2,1)S(1)}, bf16[256,512]{0,1:T(8,128)(2,1)S(1)}, u32[]{:S(2)}, u32[]{:S(2)}) collective-permute-start(bf16[256,512]{0,1:T(8,128)(2,1)S(1)} %convolution_convert_fusion.4), channel_id=1, source_target_pairs={{0,3},{1,0},{2,1},{3,2},{4,7},{5,4},{6,5},{7,6},{8,11},{9,8},{10,9... | collective-permute-start | bytes 786440 | tf_op jit(solution)/shard_map/ppermute | solution.py:30
  66.0 38.1 %collective-permute-start.15 = (f32[128,512]{1,0:T(8,128)S(1)}, f32[128,512]{1,0:T(8,128)S(1)}, u32[]{:S(2)}, u32[]{:S(2)}) collective-permute-start(f32[128,512]{1,0:T(8,128)S(1)} %convert_reduce_fusion), channel_id=1, source_target_pairs={{0,64},{8,72},{16,80},{24,88},{32,96},{40,104},{48,112},{56,120},{... | collective-permute-start | bytes 786440 | tf_op jit(solution)/shard_map/ppermute | solution.py:142
  68.5 9.1 %collective-permute-start.9 = (bf16[256,256]{0,1:T(8,128)(2,1)S(1)}, bf16[256,256]{0,1:T(8,128)(2,1)S(1)}, u32[]{:S(2)}, u32[]{:S(2)}) collective-permute-start(bf16[256,256]{0,1:T(8,128)(2,1)S(1)} %get-tuple-element.62), channel_id=1, source_target_pairs={{0,3},{1,0},{2,1},{3,2},{4,7},{5,4},{6,5},{7,6},{8,11},{9,8},{10,9... | collective-permute-start | bytes 393224 | tf_op jit(solution)/shard_map/ppermute | solution.py:30
  71.6 7.8 %collective-permute-start.8 = (bf16[256,256]{0,1:T(8,128)(2,1)S(1)}, bf16[256,256]{0,1:T(8,128)(2,1)S(1)}, u32[]{:S(2)}, u32[]{:S(2)}) collective-permute-start(bf16[256,256]{0,1:T(8,128)(2,1)S(1)} %get-tuple-element.62), channel_id=1, source_target_pairs={{0,2},{1,3},{2,0},{3,1},{4,6},{5,7},{6,4},{7,5},{8,10},{9,11},{10,... | collective-permute-start | bytes 393224 | tf_op jit(solution)/shard_map/ppermute | solution.py:30
  72.1 8.5 %collective-permute-start.7 = (bf16[256,256]{0,1:T(8,128)(2,1)S(1)}, bf16[256,256]{0,1:T(8,128)(2,1)S(1)}, u32[]{:S(2)}, u32[]{:S(2)}) collective-permute-start(bf16[256,256]{0,1:T(8,128)(2,1)S(1)} %get-tuple-element.62), channel_id=1, source_target_pairs={{0,1},{1,2},{2,3},{3,0},{4,5},{5,6},{6,7},{7,4},{8,9},{9,10},{10,1... | collective-permute-start | bytes 393224 | tf_op jit(solution)/shard_map/ppermute | solution.py:30
  74.8 52.8 %copy-start.3 = (bf16[1024,2048]{1,0:T(8,128)(2,1)}, bf16[1024,2048]{1,0:T(8,128)(2,1)S(1)}, u32[]{:S(2)}) copy-start(bf16[1024,2048]{1,0:T(8,128)(2,1)S(1)} %pad_maximum_fusion) | copy-start | bytes 12582916
  74.9 10.5 %collective-permute-start.12 = (bf16[256,256]{0,1:T(8,128)(2,1)S(1)}, bf16[256,256]{0,1:T(8,128)(2,1)S(1)}, u32[]{:S(2)}, u32[]{:S(2)}) collective-permute-start(bf16[256,256]{0,1:T(8,128)(2,1)S(1)} %get-tuple-element.61), channel_id=1, source_target_pairs={{0,3},{1,0},{2,1},{3,2},{4,7},{5,4},{6,5},{7,6},{8,11},{9,8},{10,9... | collective-permute-start | bytes 393224 | tf_op jit(solution)/shard_map/ppermute | solution.py:30
  77.6 7.8 %collective-permute-start.11 = (bf16[256,256]{0,1:T(8,128)(2,1)S(1)}, bf16[256,256]{0,1:T(8,128)(2,1)S(1)}, u32[]{:S(2)}, u32[]{:S(2)}) collective-permute-start(bf16[256,256]{0,1:T(8,128)(2,1)S(1)} %get-tuple-element.61), channel_id=1, source_target_pairs={{0,2},{1,3},{2,0},{3,1},{4,6},{5,7},{6,4},{7,5},{8,10},{9,11},{10,... | collective-permute-start | bytes 393224 | tf_op jit(solution)/shard_map/ppermute | solution.py:30
  79.3 6.2 %collective-permute-start.10 = (bf16[256,256]{0,1:T(8,128)(2,1)S(1)}, bf16[256,256]{0,1:T(8,128)(2,1)S(1)}, u32[]{:S(2)}, u32[]{:S(2)}) collective-permute-start(bf16[256,256]{0,1:T(8,128)(2,1)S(1)} %get-tuple-element.61), channel_id=1, source_target_pairs={{0,1},{1,2},{2,3},{3,0},{4,5},{5,6},{6,7},{7,4},{8,9},{9,10},{10,1... | collective-permute-start | bytes 393224 | tf_op jit(solution)/shard_map/ppermute | solution.py:30
  81.4 16.8 %collective-permute-start.13 = (bf16[1024,256]{1,0:T(8,128)(2,1)S(1)}, bf16[1024,256]{1,0:T(8,128)(2,1)S(1)}, u32[]{:S(2)}, u32[]{:S(2)}) collective-permute-start(bf16[1024,256]{1,0:T(8,128)(2,1)S(1)} %fusion.16), channel_id=1, source_target_pairs={{0,4},{1,5},{2,6},{3,7},{4,0},{5,1},{6,2},{7,3},{8,12},{9,13},{10,... | collective-permute-start | bytes 1572872 | tf_op jit(solution)/shard_map/ppermute | solution.py:30
  86.4 23.1 %collective-permute-start.14 = (bf16[1024,256]{1,0:T(8,128)(2,1)S(1)}, bf16[1024,256]{1,0:T(8,128)(2,1)S(1)}, u32[]{:S(2)}, u32[]{:S(2)}) collective-permute-start(bf16[1024,256]{1,0:T(8,128)(2,1)S(1)} %fusion.19), channel_id=1, source_target_pairs={{0,4},{1,5},{2,6},{3,7},{4,0},{5,1},{6,2},{7,3},{8,12},{9,13},{10,... | collective-permute-start | bytes 1572872 | tf_op jit(solution)/shard_map/ppermute | solution.py:30
  90.6 7.7 %copy-start.8 = (f32[1,1024,512]{2,1,0:T(8,128)S(1)}, f32[1,1024,512]{2,1,0:T(8,128)}, u32[]{:S(2)}) copy-start(f32[1,1024,512]{2,1,0:T(8,128)} %param.11) | copy-start | bytes 6291460
  90.6 7.7 %copy-start.11 = (f32[1,1024,512]{2,1,0:T(8,128)S(1)}, f32[1,1024,512]{2,1,0:T(8,128)}, u32[]{:S(2)}) copy-start(f32[1,1024,512]{2,1,0:T(8,128)} %param.12) | copy-start | bytes 6291460
  91.4 18.1 %copy-start.1 = (f32[1024,256]{1,0:T(8,128)}, f32[1024,256]{1,0:T(8,128)S(1)}, u32[]{:S(2)}) copy-start(f32[1024,256]{1,0:T(8,128)S(1)} %fusion.12) | copy-start | bytes 3145732
  100.6 20.1 %collective-permute-start.16 = (bf16[1024,256]{1,0:T(8,128)(2,1)S(1)}, bf16[1024,256]{1,0:T(8,128)(2,1)S(1)}, u32[]{:S(2)}, u32[]{:S(2)}) collective-permute-start(bf16[1024,256]{1,0:T(8,128)(2,1)S(1)} %get-tuple-element.45), channel_id=1, source_target_pairs={{0,4},{1,5},{2,6},{3,7},{4,0},{5,1},{6,2},{7,3},{8,12},{9,13},{10,... | collective-permute-start | bytes 1572872 | tf_op jit(solution)/shard_map/ppermute | solution.py:30
  110.4 17.3 %collective-permute-start.23 = (bf16[1024,256]{1,0:T(8,128)(2,1)S(1)}, bf16[1024,256]{1,0:T(8,128)(2,1)S(1)}, u32[]{:S(2)}, u32[]{:S(2)}) collective-permute-start(bf16[1024,256]{1,0:T(8,128)(2,1)S(1)} %fusion.38), channel_id=1, source_target_pairs={{0,4},{1,5},{2,6},{3,7},{4,0},{5,1},{6,2},{7,3},{8,12},{9,13},{10,... | collective-permute-start | bytes 1572872 | tf_op jit(solution)/shard_map/ppermute | solution.py:30
  122.0 6.9 %collective-permute-start.17 = (bf16[256,256]{0,1:T(8,128)(2,1)S(1)}, bf16[256,256]{0,1:T(8,128)(2,1)S(1)}, u32[]{:S(2)}, u32[]{:S(2)}) collective-permute-start(bf16[256,256]{0,1:T(8,128)(2,1)S(1)} %get-tuple-element.67), channel_id=1, source_target_pairs={{0,3},{1,0},{2,1},{3,2},{4,7},{5,4},{6,5},{7,6},{8,11},{9,8},{10,9... | collective-permute-start | bytes 393224 | tf_op jit(solution)/shard_map/ppermute | solution.py:30
  124.0 6.6 %collective-permute-start.19 = (bf16[256,256]{0,1:T(8,128)(2,1)S(1)}, bf16[256,256]{0,1:T(8,128)(2,1)S(1)}, u32[]{:S(2)}, u32[]{:S(2)}) collective-permute-start(bf16[256,256]{0,1:T(8,128)(2,1)S(1)} %get-tuple-element.68), channel_id=1, source_target_pairs={{0,2},{1,3},{2,0},{3,1},{4,6},{5,7},{6,4},{7,5},{8,10},{9,11},{10,... | collective-permute-start | bytes 393224 | tf_op jit(solution)/shard_map/ppermute | solution.py:30
  124.6 8.8 %collective-permute-start.18 = (bf16[256,256]{0,1:T(8,128)(2,1)S(1)}, bf16[256,256]{0,1:T(8,128)(2,1)S(1)}, u32[]{:S(2)}, u32[]{:S(2)}) collective-permute-start(bf16[256,256]{0,1:T(8,128)(2,1)S(1)} %get-tuple-element.69), channel_id=1, source_target_pairs={{0,1},{1,2},{2,3},{3,0},{4,5},{5,6},{6,7},{7,4},{8,9},{9,10},{10,1... | collective-permute-start | bytes 393224 | tf_op jit(solution)/shard_map/ppermute | solution.py:30
  133.5 7.0 %collective-permute-start.22 = (bf16[256,256]{0,1:T(8,128)(2,1)S(1)}, bf16[256,256]{0,1:T(8,128)(2,1)S(1)}, u32[]{:S(2)}, u32[]{:S(2)}) collective-permute-start(bf16[256,256]{0,1:T(8,128)(2,1)S(1)} %subtract_convert_fusion.1), channel_id=1, source_target_pairs={{0,3},{1,0},{2,1},{3,2},{4,7},{5,4},{6,5},{7,6},{8,11},{9,8},{10,9... | collective-permute-start | bytes 393224 | tf_op jit(solution)/shard_map/ppermute | solution.py:30
  133.5 15.5 %collective-permute-start.21 = (bf16[256,256]{0,1:T(8,128)(2,1)S(1)}, bf16[256,256]{0,1:T(8,128)(2,1)}, u32[]{:S(2)}, u32[]{:S(2)}) collective-permute-start(bf16[256,256]{0,1:T(8,128)(2,1)S(1)} %subtract_convert_fusion.1), channel_id=1, source_target_pairs={{0,2},{1,3},{2,0},{3,1},{4,6},{5,7},{6,4},{7,5},{8,10},{9,11},{10,... | collective-permute-start | bytes 393224 | tf_op jit(solution)/shard_map/ppermute | solution.py:30
  134.0 15.0 %collective-permute-start.20 = (bf16[256,256]{0,1:T(8,128)(2,1)S(1)}, bf16[256,256]{0,1:T(8,128)(2,1)}, u32[]{:S(2)}, u32[]{:S(2)}) collective-permute-start(bf16[256,256]{0,1:T(8,128)(2,1)S(1)} %subtract_convert_fusion.1), channel_id=1, source_target_pairs={{0,1},{1,2},{2,3},{3,0},{4,5},{5,6},{6,7},{7,4},{8,9},{9,10},{10,1... | collective-permute-start | bytes 393224 | tf_op jit(solution)/shard_map/ppermute | solution.py:30
  136.3 13.8 %collective-permute-start.26 = (bf16[256,256]{0,1:T(8,128)(2,1)}, bf16[256,256]{0,1:T(8,128)(2,1)S(1)}, u32[]{:S(2)}, u32[]{:S(2)}) collective-permute-start(bf16[256,256]{0,1:T(8,128)(2,1)} %get-tuple-element.64), channel_id=1, source_target_pairs={{0,1},{1,2},{2,3},{3,0},{4,5},{5,6},{6,7},{7,4},{8,9},{9,10},{10,1... | collective-permute-start | bytes 393224 | tf_op jit(solution)/shard_map/ppermute | solution.py:30
  137.9 12.2 %collective-permute-start.25 = (bf16[256,256]{0,1:T(8,128)(2,1)}, bf16[256,256]{0,1:T(8,128)(2,1)S(1)}, u32[]{:S(2)}, u32[]{:S(2)}) collective-permute-start(bf16[256,256]{0,1:T(8,128)(2,1)} %get-tuple-element.65), channel_id=1, source_target_pairs={{0,2},{1,3},{2,0},{3,1},{4,6},{5,7},{6,4},{7,5},{8,10},{9,11},{10,... | collective-permute-start | bytes 393224 | tf_op jit(solution)/shard_map/ppermute | solution.py:30
  140.4 9.7 %collective-permute-start.24 = (bf16[256,256]{0,1:T(8,128)(2,1)S(1)}, bf16[256,256]{0,1:T(8,128)(2,1)S(1)}, u32[]{:S(2)}, u32[]{:S(2)}) collective-permute-start(bf16[256,256]{0,1:T(8,128)(2,1)S(1)} %get-tuple-element.66), channel_id=1, source_target_pairs={{0,3},{1,0},{2,1},{3,2},{4,7},{5,4},{6,5},{7,6},{8,11},{9,8},{10,9... | collective-permute-start | bytes 393224 | tf_op jit(solution)/shard_map/ppermute | solution.py:30
  144.7 31.6 %all-to-all-start.1 = ((f32[8,128,512]{2,1,0:T(8,128)}), f32[8,128,512]{2,1,0:T(8,128)}, u32[]{:S(2)}, u32[]{:S(2)}) async-start(f32[8,128,512]{2,1,0:T(8,128)} %broadcast_in_dim.4), calls=%async_computation.1 | async-start | bytes 4194304 | tf_op jit(solution)/shard_map/all_to_all | solution.py:188
  150.1 12.9 %copy-start.4 = (bf16[1024,2048]{1,0:T(8,128)(2,1)S(1)}, bf16[1024,2048]{1,0:T(8,128)(2,1)}, u32[]{:S(2)}) copy-start(bf16[1024,2048]{1,0:T(8,128)(2,1)} %copy-done.3) | copy-start | bytes 12582916
  152.7 6.4 %collective-permute-start.29 = (bf16[256,256]{0,1:T(8,128)(2,1)S(1)}, bf16[256,256]{0,1:T(8,128)(2,1)S(1)}, u32[]{:S(2)}, u32[]{:S(2)}) collective-permute-start(bf16[256,256]{0,1:T(8,128)(2,1)S(1)} %subtract_convert_fusion), channel_id=1, source_target_pairs={{0,3},{1,0},{2,1},{3,2},{4,7},{5,4},{6,5},{7,6},{8,11},{9,8},{10,9... | collective-permute-start | bytes 393224 | tf_op jit(solution)/shard_map/ppermute | solution.py:30
  152.8 7.9 %collective-permute-start.28 = (bf16[256,256]{0,1:T(8,128)(2,1)S(1)}, bf16[256,256]{0,1:T(8,128)(2,1)S(1)}, u32[]{:S(2)}, u32[]{:S(2)}) collective-permute-start(bf16[256,256]{0,1:T(8,128)(2,1)S(1)} %subtract_convert_fusion), channel_id=1, source_target_pairs={{0,2},{1,3},{2,0},{3,1},{4,6},{5,7},{6,4},{7,5},{8,10},{9,11},{10,... | collective-permute-start | bytes 393224 | tf_op jit(solution)/shard_map/ppermute | solution.py:30
  154.3 8.7 %collective-permute-start.27 = (bf16[256,256]{0,1:T(8,128)(2,1)S(1)}, bf16[256,256]{0,1:T(8,128)(2,1)S(1)}, u32[]{:S(2)}, u32[]{:S(2)}) collective-permute-start(bf16[256,256]{0,1:T(8,128)(2,1)S(1)} %subtract_convert_fusion), channel_id=1, source_target_pairs={{0,1},{1,2},{2,3},{3,0},{4,5},{5,6},{6,7},{7,4},{8,9},{9,10},{10,1... | collective-permute-start | bytes 393224 | tf_op jit(solution)/shard_map/ppermute | solution.py:30
  154.8 16.9 %collective-permute-start.30 = (bf16[1024,256]{1,0:T(8,128)(2,1)S(1)}, bf16[1024,256]{1,0:T(8,128)(2,1)S(1)}, u32[]{:S(2)}, u32[]{:S(2)}) collective-permute-start(bf16[1024,256]{1,0:T(8,128)(2,1)S(1)} %fusion.22), channel_id=1, source_target_pairs={{0,4},{1,5},{2,6},{3,7},{4,0},{5,1},{6,2},{7,3},{8,12},{9,13},{10,... | collective-permute-start | bytes 1572872 | tf_op jit(solution)/shard_map/ppermute | solution.py:30
  164.6 17.8 %collective-permute-start.31 = (bf16[1024,256]{1,0:T(8,128)(2,1)}, bf16[1024,256]{1,0:T(8,128)(2,1)}, u32[]{:S(2)}, u32[]{:S(2)}) collective-permute-start(bf16[1024,256]{1,0:T(8,128)(2,1)} %fusion.25), channel_id=1, source_target_pairs={{0,4},{1,5},{2,6},{3,7},{4,0},{5,1},{6,2},{7,3},{8,12},{9,13},{10,... | collective-permute-start | bytes 1572872 | tf_op jit(solution)/shard_map/ppermute | solution.py:30
  168.9 3.0 %copy-start.19 = (f32[1024,256]{1,0:T(8,128)S(1)}, f32[1024,256]{1,0:T(8,128)}, u32[]{:S(2)}) copy-start(f32[1024,256]{1,0:T(8,128)} %get-tuple-element.71) | copy-start | bytes 3145732
  175.1 7.3 %copy-start.2 = (f32[1024,256]{1,0:T(8,128)S(1)}, f32[1024,256]{1,0:T(8,128)}, u32[]{:S(2)}) copy-start(f32[1024,256]{1,0:T(8,128)} %copy-done.1) | copy-start | bytes 3145732
  176.2 6.1 %copy-start.7 = (bf16[1024,256]{1,0:T(8,128)(2,1)S(1)}, bf16[1024,256]{1,0:T(8,128)(2,1)}, u32[]{:S(2)}) copy-start(bf16[1024,256]{1,0:T(8,128)(2,1)} %copy-done.6) | copy-start | bytes 1572868
  176.2 6.1 %copy-start.10 = (f32[1,1024,512]{2,1,0:T(8,128)S(1)}, f32[1,1024,512]{2,1,0:T(8,128)}, u32[]{:S(2)}) copy-start(f32[1,1024,512]{2,1,0:T(8,128)} %param.11) | copy-start | bytes 6291460
  176.2 6.2 %copy-start.13 = (f32[1,1024,512]{2,1,0:T(8,128)S(1)}, f32[1,1024,512]{2,1,0:T(8,128)}, u32[]{:S(2)}) copy-start(f32[1,1024,512]{2,1,0:T(8,128)} %param.12) | copy-start | bytes 6291460
  176.2 6.2 %copy-start.14 = (f32[1024,256]{1,0:T(8,128)S(1)}, f32[1024,256]{1,0:T(8,128)}, u32[]{:S(2)}) copy-start(f32[1024,256]{1,0:T(8,128)} %fusion.8) | copy-start | bytes 3145732
  182.0 3.0 %copy-start.15 = (f32[1024,256]{1,0:T(8,128)S(1)}, f32[1024,256]{1,0:T(8,128)}, u32[]{:S(2)}) copy-start(f32[1024,256]{1,0:T(8,128)} %add_add_fusion.1) | copy-start | bytes 3145732
  (6 other events, 13.9 us)
